TPU v7x, 32 devices: a whole 2x2x4 slice. The times are simulated.
32 devices in a mesh: section: 2 (over y), batch: 16 (over z, x, core).
Axes of the slice: x: 2, y: 2, z: 4, core: 2. Of those that a mesh axis runs over, the one named last changes fastest.
Arguments:
- streams: bfloat16 [2, 13056, 768], P('section', 'batch'), may hold values from -6 to 6
- cotangent: bfloat16 [13056, 768], P('batch'), may hold values from -6 to 6
- counts: int32 [96], P('batch'), may hold values from 22 to 136, as said below
- positions: int32 [96, 136], P('batch'), may hold values from 0 to 224, as said below
- radar_counts: int32 [96], P('batch'), may hold values from 22 to 136, as said below
- radar_positions: int32 [96, 136], P('batch'), may hold values from 0 to 224, as said below
- qkv_weight: bfloat16 [2, 768, 2304], P('section'), may hold values from -0.21875 to 0.21875
- out_weight: bfloat16 [2, 768, 768], P('section'), may hold values from -0.875 to 0.875
- fc1_weight: bfloat16 [2, 768, 3072], P('section'), may hold values from -0.21875 to 0.21875
- fc2_weight: bfloat16 [2, 3072, 768], P('section'), may hold values from -0.15625 to 0.15625
- attn_bias: float32 [2, 2304], P('section'), may hold values from -3 to 3
- mlp_bias: float32 [2, 3840], P('section'), may hold values from -3 to 3
- norm_gains: float32 [2, 1536], P('section'), may hold values from 0.5 to 1.5
- norm_shifts: float32 [2, 1536], P('section'), may hold values from -2 to 2
- cross_qkv_weight: bfloat16 [768, 2304], replicated, may hold values from -0.21875 to 0.21875
- cross_out_weight: bfloat16 [768, 768], replicated, may hold values from -0.875 to 0.875
- cross_gain: float32 [768], replicated, may hold values from 0.5 to 1.5
- cross_bias: float32 [3072], replicated, may hold values from -2 to 2
Outputs:
- layer_out: float32 [2, 13056, 768], P('section', 'batch')
- input_grads: float32 [2, 13056, 768], P('section', 'batch')
- grad_qkv: float32 [2, 768, 2304], P('section', 'batch')
- grad_out: float32 [2, 768, 768], P('section', 'batch')
- grad_fc1: float32 [2, 768, 3072], P('section', 'batch')
- grad_fc2: float32 [2, 3072, 768], P('section', 'batch')
- grad_attn_bias: float32 [2, 2304], P('section', 'batch')
- grad_mlp_bias: float32 [2, 3840], P('section', 'batch')
- grad_norm_gains: float32 [2, 1536], P('section', 'batch')
- grad_norm_shifts: float32 [2, 1536], P('section', 'batch')
- grad_cross_qkv: float32 [768, 2304], P('batch')
- grad_cross_out: float32 [768, 768], P('batch')
- grad_cross_gain: float32 [768], P('batch')
- grad_cross_bias: float32 [3072], P('batch')
Inputs may be any that keep to these rules, and one draw needn't show every extreme that they name: The first counts[i] optical slots of image i are live. `positions`: row * 15 + column of the patch in each optical slot; all different within an image. The first radar_counts[i] radar slots of image i are live. `radar_positions`: row * 15 + column of the patch in each radar slot; all different within an image.
All inputs are finite; a program needn't handle non-finite values.
Results may differ from a plain program's by a relative error of at most 0.019.
Values may be sent and summed in bfloat16 or wider, within the bound.
No kernel may reach another device: no remote copies, remote signals or barrier semaphores. Data moves between devices by JAX's collectives and lax.ppermute only.
A program may use at most 256 MiB of HBM per device.

v0:
```python
from functools import partial

import jax
import jax.numpy as jnp
from jax import lax
from jax.sharding import PartitionSpec as P

H = 12
HD = 64
GRID = 15


SCORE_SCALE = 0.125
NORM_EPS = 1e-06
MASKED_SCORE = -1e30


def from_behind(block, axis, distance):
    devices = range(lax.axis_size(axis))
    route = [(i - distance, i) for i in devices if i - distance in devices]
    return lax.ppermute(block, axis, route)


def matmul(left_mat, right_mat):
    return jnp.dot(left_mat, right_mat, preferred_element_type=jnp.float32)


def matmul_tn(left_mat, right_mat):
    return lax.dot_general(
        left_mat, right_mat, (((0,), (0,)), ((), ())), preferred_element_type=jnp.float32
    )


def matmul_nt(left_mat, right_mat):
    return lax.dot_general(
        left_mat, right_mat, (((1,), (1,)), ((), ())), preferred_element_type=jnp.float32
    )


def layer_norm(values_in, gain_vec, shift_vec):
    average = jnp.mean(values_in, axis=-1, keepdims=True)
    centred = values_in - average
    spread = jnp.mean(centred * centred, axis=-1, keepdims=True)
    return centred * lax.rsqrt(spread + NORM_EPS) * gain_vec + shift_vec


def norm_back(values_in, gain_vec, shift_vec, upstream):
    return jax.vjp(layer_norm, values_in, gain_vec, shift_vec)[1](upstream)


def exact_gelu(values_in):
    return jax.nn.gelu(values_in, approximate=False)


def gelu_back(values_in, upstream):
    return jax.vjp(exact_gelu, values_in)[1](upstream)[0]


def alibi_bias(query_pos, key_pos):
    gap_row = (query_pos[:, None] // GRID - key_pos[None, :] // GRID).astype(jnp.float32)
    gap_col = (query_pos[:, None] % GRID - key_pos[None, :] % GRID).astype(jnp.float32)
    distance = jnp.sqrt(gap_row * gap_row + gap_col * gap_col)
    slopes = 2.0 ** (-8.0 * (jnp.arange(H, dtype=jnp.float32) + 1.0) / H)
    return -slopes[:, None, None] * distance[None, :, :]


def to_heads(matrix):
    return matrix.reshape(matrix.shape[0], H, HD).transpose(1, 0, 2)


def from_heads(stacked):
    return stacked.transpose(1, 0, 2).reshape(stacked.shape[1], H * HD)


def attend(queries, key_rows, value_rows, score_bias, is_live):
    head_q, head_k, head_v = (to_heads(queries), to_heads(key_rows), to_heads(value_rows))
    raw_scores = (
        jnp.einsum("hqd,hkd->hqk", head_q, head_k, preferred_element_type=jnp.float32) * SCORE_SCALE
    )
    scores = jnp.where(is_live[None, None, :], raw_scores + score_bias, MASKED_SCORE)
    highest = jnp.max(scores, axis=-1, keepdims=True)
    weights = jnp.exp(scores - highest)
    totals = jnp.sum(weights, axis=-1, keepdims=True)
    weights_low = (weights / totals).astype(jnp.bfloat16)
    mixed_heads = jnp.einsum(
        "hqk,hkd->hqd", weights_low, head_v, preferred_element_type=jnp.float32
    )
    return (from_heads(mixed_heads).astype(jnp.bfloat16), highest + jnp.log(totals))


def attend_back(queries, key_rows, value_rows, score_bias, is_live, logsum, grad_heard):
    head_q, head_k, head_v = (to_heads(queries), to_heads(key_rows), to_heads(value_rows))
    head_g = to_heads(grad_heard)
    raw_scores = (
        jnp.einsum("hqd,hkd->hqk", head_q, head_k, preferred_element_type=jnp.float32) * SCORE_SCALE
    )
    scores = jnp.where(is_live[None, None, :], raw_scores + score_bias, MASKED_SCORE)
    weights = jnp.exp(scores - logsum)
    grad_v = jnp.einsum(
        "hqk,hqd->hkd", weights.astype(jnp.bfloat16), head_g, preferred_element_type=jnp.float32
    )
    grad_w = jnp.einsum("hqd,hkd->hqk", head_g, head_v, preferred_element_type=jnp.float32)
    inner = jnp.sum(grad_w * weights, axis=-1, keepdims=True)
    grad_s = (weights * (grad_w - inner)).astype(jnp.bfloat16)
    grad_q = (
        jnp.einsum("hqk,hkd->hqd", grad_s, head_k, preferred_element_type=jnp.float32) * SCORE_SCALE
    )
    grad_k = (
        jnp.einsum("hqk,hqd->hkd", grad_s, head_q, preferred_element_type=jnp.float32) * SCORE_SCALE
    )
    return (from_heads(grad_q), from_heads(grad_k), from_heads(grad_v))


def cross_forward(
    middle,
    radar_rows,
    radar_live,
    radar_pos,
    image_pos,
    cross_qkv,
    cross_out,
    cross_gains,
    cross_vec,
):
    model_width = middle.shape[1]
    normed = layer_norm(middle, cross_gains, cross_vec[3 * model_width :]).astype(jnp.bfloat16)
    queries = (matmul(normed, cross_qkv[:, :model_width]) + cross_vec[:model_width]).astype(
        jnp.bfloat16
    )
    radar_proj = matmul(radar_rows, cross_qkv[:, model_width:])
    key_rows = radar_proj[:, :model_width].astype(jnp.bfloat16)
    value_rows = (radar_proj[:, model_width:] + cross_vec[model_width : 2 * model_width]).astype(
        jnp.bfloat16
    )
    attended, logsum = attend(
        queries, key_rows, value_rows, alibi_bias(image_pos, radar_pos), radar_live
    )
    after_cross = (
        middle + matmul(attended, cross_out) + cross_vec[2 * model_width : 3 * model_width]
    )
    return (after_cross, (normed, queries, key_rows, value_rows, attended, logsum))


def cross_skip(
    middle,
    radar_rows,
    radar_live,
    radar_pos,
    image_pos,
    cross_qkv,
    cross_out,
    cross_gains,
    cross_vec,
):
    blanks = jnp.zeros(middle.shape, jnp.bfloat16)
    return (
        middle,
        (blanks, blanks, blanks, blanks, blanks, jnp.zeros((H, middle.shape[0], 1), jnp.float32)),
    )


def cross_back(
    grad_after,
    middle,
    cross_stored,
    radar_rows,
    radar_live,
    radar_pos,
    image_pos,
    cross_qkv,
    cross_out,
    cross_gains,
    cross_vec,
):
    normed, queries, key_rows, value_rows, attended, logsum = cross_stored
    model_width = middle.shape[1]
    grad_proj = grad_after.astype(jnp.bfloat16)
    grad_outw = matmul_tn(attended, grad_proj)
    grad_heard = matmul_nt(grad_proj, cross_out).astype(jnp.bfloat16)
    grad_q, grad_k, grad_v = attend_back(
        queries,
        key_rows,
        value_rows,
        alibi_bias(image_pos, radar_pos),
        radar_live,
        logsum,
        grad_heard,
    )
    grad_q = grad_q.astype(jnp.bfloat16)
    grad_k = grad_k.astype(jnp.bfloat16)
    grad_v = grad_v.astype(jnp.bfloat16)
    grad_weight = jnp.concatenate(
        [matmul_tn(normed, grad_q), matmul_tn(radar_rows, grad_k), matmul_tn(radar_rows, grad_v)],
        axis=1,
    )
    grad_radar = matmul_nt(grad_k, cross_qkv[:, model_width : 2 * model_width]) + matmul_nt(
        grad_v, cross_qkv[:, 2 * model_width :]
    )
    grad_middle, grad_gain, grad_shift = norm_back(
        middle,
        cross_gains,
        cross_vec[3 * model_width :],
        matmul_nt(grad_q, cross_qkv[:, :model_width]),
    )
    grad_vec = jnp.concatenate(
        [
            jnp.sum(grad_q.astype(jnp.float32), axis=0),
            jnp.sum(grad_v.astype(jnp.float32), axis=0),
            jnp.sum(grad_proj.astype(jnp.float32), axis=0),
            grad_shift,
        ]
    )
    return (grad_middle + grad_after, grad_radar, (grad_weight, grad_outw, grad_gain, grad_vec))


def cross_skip_back(
    grad_after,
    middle,
    cross_stored,
    radar_rows,
    radar_live,
    radar_pos,
    image_pos,
    cross_qkv,
    cross_out,
    cross_gains,
    cross_vec,
):
    return (
        grad_after,
        jnp.zeros(middle.shape, jnp.float32),
        (
            jnp.zeros(cross_qkv.shape, jnp.float32),
            jnp.zeros(cross_out.shape, jnp.float32),
            jnp.zeros(cross_gains.shape, jnp.float32),
            jnp.zeros(cross_vec.shape, jnp.float32),
        ),
    )


def layer_forward(current, rows_now, params, is_merged):
    image_live, image_pos, radar_rows, radar_live, radar_pos = rows_now
    (
        qkv_mat,
        out_mat,
        fc1_mat,
        fc2_mat,
        attn_vec,
        mlp_vec,
        gain_vec,
        shift_vec,
        cross_qkv,
        cross_out,
        cross_gains,
        cross_vec,
    ) = params
    model_width = current.shape[1]
    hidden = fc1_mat.shape[1]
    normed = layer_norm(current, gain_vec[:model_width], shift_vec[:model_width]).astype(
        jnp.bfloat16
    )
    joined = matmul(normed, qkv_mat)
    queries = (joined[:, :model_width] + attn_vec[:model_width]).astype(jnp.bfloat16)
    key_rows = joined[:, model_width : 2 * model_width].astype(jnp.bfloat16)
    value_rows = (joined[:, 2 * model_width :] + attn_vec[model_width : 2 * model_width]).astype(
        jnp.bfloat16
    )
    attended, logsum = attend(
        queries, key_rows, value_rows, alibi_bias(image_pos, image_pos), image_live
    )
    middle = current + matmul(attended, out_mat) + attn_vec[2 * model_width :]
    after_cross, cross_stored = lax.cond(
        is_merged,
        cross_forward,
        cross_skip,
        middle,
        radar_rows,
        radar_live,
        radar_pos,
        image_pos,
        cross_qkv,
        cross_out,
        cross_gains,
        cross_vec,
    )
    normed_two = layer_norm(after_cross, gain_vec[model_width:], shift_vec[model_width:]).astype(
        jnp.bfloat16
    )
    up_proj = matmul(normed_two, fc1_mat) + mlp_vec[:hidden]
    active = exact_gelu(up_proj).astype(jnp.bfloat16)
    result = after_cross + matmul(active, fc2_mat) + mlp_vec[hidden:]
    row_mask = image_live.astype(jnp.float32)[:, None]
    stored = (
        current,
        normed,
        queries,
        key_rows,
        value_rows,
        attended,
        logsum,
        middle,
        cross_stored,
        after_cross,
        normed_two,
        up_proj,
        active,
    )
    return (result * row_mask, stored)


def layer_backward(seed_now, stored, rows_now, params, is_merged):
    image_live, image_pos, radar_rows, radar_live, radar_pos = rows_now
    (
        qkv_mat,
        out_mat,
        fc1_mat,
        fc2_mat,
        attn_vec,
        mlp_vec,
        gain_vec,
        shift_vec,
        cross_qkv,
        cross_out,
        cross_gains,
        cross_vec,
    ) = params
    (
        current,
        normed,
        queries,
        key_rows,
        value_rows,
        attended,
        logsum,
        middle,
        cross_stored,
        after_cross,
        normed_two,
        up_proj,
        active,
    ) = stored
    model_width = current.shape[1]
    upstream = seed_now * image_live.astype(jnp.float32)[:, None]
    grad_branch = upstream.astype(jnp.bfloat16)
    grad_fc2 = matmul_tn(active, grad_branch)
    grad_b2 = jnp.sum(grad_branch.astype(jnp.float32), axis=0)
    grad_up = gelu_back(up_proj, matmul_nt(grad_branch, fc2_mat)).astype(jnp.bfloat16)
    grad_fc1 = matmul_tn(normed_two, grad_up)
    grad_b1 = jnp.sum(grad_up.astype(jnp.float32), axis=0)
    grad_after, grad_gain_two, grad_shift_two = norm_back(
        after_cross, gain_vec[model_width:], shift_vec[model_width:], matmul_nt(grad_up, fc1_mat)
    )
    grad_after = grad_after + upstream
    grad_middle, grad_radar, cross_grads = lax.cond(
        is_merged,
        cross_back,
        cross_skip_back,
        grad_after,
        middle,
        cross_stored,
        radar_rows,
        radar_live,
        radar_pos,
        image_pos,
        cross_qkv,
        cross_out,
        cross_gains,
        cross_vec,
    )
    grad_proj = grad_middle.astype(jnp.bfloat16)
    grad_outw = matmul_tn(attended, grad_proj)
    grad_bo = jnp.sum(grad_proj.astype(jnp.float32), axis=0)
    grad_heard = matmul_nt(grad_proj, out_mat).astype(jnp.bfloat16)
    grad_q, grad_k, grad_v = attend_back(
        queries,
        key_rows,
        value_rows,
        alibi_bias(image_pos, image_pos),
        image_live,
        logsum,
        grad_heard,
    )
    grad_joined = jnp.concatenate([grad_q, grad_k, grad_v], axis=1).astype(jnp.bfloat16)
    grad_qkv = matmul_tn(normed, grad_joined)
    column_sums = jnp.sum(grad_joined.astype(jnp.float32), axis=0)
    grad_attn = jnp.concatenate(
        [column_sums[:model_width], column_sums[2 * model_width :], grad_bo]
    )
    grad_state, grad_gain_one, grad_shift_one = norm_back(
        current, gain_vec[:model_width], shift_vec[:model_width], matmul_nt(grad_joined, qkv_mat)
    )
    grad_state = grad_state + grad_middle
    layer_grads = (
        grad_qkv,
        grad_outw,
        grad_fc1,
        grad_fc2,
        grad_attn,
        jnp.concatenate([grad_b1, grad_b2]),
        jnp.concatenate([grad_gain_one, grad_gain_two]),
        jnp.concatenate([grad_shift_one, grad_shift_two]),
    )
    return (grad_state, grad_radar, layer_grads, cross_grads)


def pick_tick(tick_at, stacked):
    return lax.dynamic_index_in_dim(stacked, tick_at, 0, False)


def body(
    streams,
    cotangent,
    counts,
    positions,
    radar_counts,
    radar_positions,
    qkv_weight,
    out_weight,
    fc1_weight,
    fc2_weight,
    attn_bias,
    mlp_bias,
    norm_gains,
    norm_shifts,
    cross_qkv_weight,
    cross_out_weight,
    cross_gain,
    cross_bias,
):
    batches = counts.shape[0]
    slot_count = positions.shape[1]
    model_width = cotangent.shape[1]
    section_id = lax.axis_index("section")
    is_first = section_id == 0
    is_merged = section_id > 0
    params = (
        qkv_weight[0],
        out_weight[0],
        fc1_weight[0],
        fc2_weight[0],
        attn_bias[0],
        mlp_bias[0],
        norm_gains[0],
        norm_shifts[0],
        cross_qkv_weight,
        cross_out_weight,
        cross_gain,
        cross_bias,
    )
    own_rows = streams[0].reshape(batches, slot_count, model_width)
    seed_rows = cotangent.reshape(batches, slot_count, model_width)
    slot_ids = jnp.arange(slot_count, dtype=jnp.int32)
    tick_ids = jnp.arange(batches + 1, dtype=jnp.int32)

    def context(batch_index):
        image_live = slot_ids < lax.dynamic_index_in_dim(counts, batch_index, 0, False)
        image_pos = lax.dynamic_index_in_dim(positions, batch_index, 0, False)
        own_now = lax.dynamic_index_in_dim(own_rows, batch_index, 0, False)
        radar_live = slot_ids < lax.dynamic_index_in_dim(radar_counts, batch_index, 0, False)
        radar_pos = lax.dynamic_index_in_dim(radar_positions, batch_index, 0, False)
        return (image_live, image_pos, own_now, radar_live, radar_pos)

    def forward_tick(loop_state, tick_id):
        received, outputs = loop_state
        batch_index = tick_id - section_id
        is_valid = (batch_index >= 0) & (batch_index < batches)
        batch_index = jnp.clip(batch_index, 0, batches - 1)
        rows_now = context(batch_index)
        current = jnp.where(is_first, rows_now[2], received).astype(jnp.float32)
        result, stored = layer_forward(current, rows_now, params, is_merged)
        previous = lax.dynamic_index_in_dim(outputs, batch_index, 0, False)
        outputs = lax.dynamic_update_index_in_dim(
            outputs, jnp.where(is_valid, result, previous), batch_index, 0
        )
        sent_rows = from_behind(result.astype(jnp.bfloat16), "section", 1)
        return ((sent_rows, outputs), stored)

    start_rows = jnp.zeros((slot_count, model_width), jnp.bfloat16)
    start_outputs = jnp.zeros((batches, slot_count, model_width), jnp.float32)
    (unused_rows, outputs), kept_rows = lax.scan(
        forward_tick, (start_rows, start_outputs), tick_ids
    )
    layer_shapes = [weight_now.shape for weight_now in params[:8]]
    cross_shapes = [weight_now.shape for weight_now in params[8:]]
    layer_init = tuple((jnp.zeros(dims_now, jnp.float32) for dims_now in layer_shapes))
    cross_init = tuple((jnp.zeros(dims_now, jnp.float32) for dims_now in cross_shapes))

    def backward_tick(loop_state, tick_id):
        received, grads_in, layer_acc, cross_acc = loop_state
        batch_index = batches - section_id - tick_id
        is_valid = (batch_index >= 0) & (batch_index < batches)
        batch_index = jnp.clip(batch_index, 0, batches - 1)
        forward_at = batch_index + section_id
        rows_now = context(batch_index)
        stored = jax.tree.map(partial(pick_tick, forward_at), kept_rows)
        target = lax.dynamic_index_in_dim(seed_rows, batch_index, 0, False)
        seed_now = jnp.where(is_first, received, target).astype(jnp.float32) * is_valid.astype(
            jnp.float32
        )
        grad_state, grad_radar, layer_grads, cross_grads = layer_backward(
            seed_now, stored, rows_now, params, is_merged
        )
        previous = lax.dynamic_index_in_dim(grads_in, batch_index, 0, False)
        fresh = jnp.where(is_first, grad_state, grad_radar)
        grads_in = lax.dynamic_update_index_in_dim(
            grads_in, jnp.where(is_valid, fresh, previous), batch_index, 0
        )
        sent_rows = from_behind(grad_state.astype(jnp.bfloat16), "section", -1)
        layer_parts = tuple(layer_grads)
        cross_parts = tuple(cross_grads)
        layer_acc = jax.tree.map(jnp.add, layer_acc, layer_parts)
        cross_acc = jax.tree.map(jnp.add, cross_acc, cross_parts)
        return ((sent_rows, grads_in, layer_acc, cross_acc), None)

    start_grads = jnp.zeros((batches, slot_count, model_width), jnp.float32)
    (unused_back, grads_in, layer_acc, cross_acc), unused_ys = lax.scan(
        backward_tick, (start_rows, start_grads, layer_init, cross_init), tick_ids
    )
    layer_total = (
        lax.psum_scatter(layer_acc[0][None], "batch", scatter_dimension=1, tiled=True),
        lax.psum_scatter(layer_acc[1][None], "batch", scatter_dimension=1, tiled=True),
        lax.psum_scatter(layer_acc[2][None], "batch", scatter_dimension=1, tiled=True),
        lax.psum_scatter(layer_acc[3][None], "batch", scatter_dimension=1, tiled=True),
        lax.psum_scatter(layer_acc[4][None], "batch", scatter_dimension=1, tiled=True),
        lax.psum_scatter(layer_acc[5][None], "batch", scatter_dimension=1, tiled=True),
        lax.psum_scatter(layer_acc[6][None], "batch", scatter_dimension=1, tiled=True),
        lax.psum_scatter(layer_acc[7][None], "batch", scatter_dimension=1, tiled=True),
    )
    cross_share = (
        lax.psum_scatter(cross_acc[0], "batch", scatter_dimension=0, tiled=True),
        lax.psum_scatter(cross_acc[1], "batch", scatter_dimension=0, tiled=True),
        lax.psum_scatter(cross_acc[2], "batch", scatter_dimension=0, tiled=True),
        lax.psum_scatter(cross_acc[3], "batch", scatter_dimension=0, tiled=True),
    )
    cross_total = (
        lax.psum(cross_share[0].astype(jnp.bfloat16), "section").astype(jnp.float32),
        lax.psum(cross_share[1].astype(jnp.bfloat16), "section").astype(jnp.float32),
        lax.psum(cross_share[2].astype(jnp.bfloat16), "section").astype(jnp.float32),
        lax.psum(cross_share[3].astype(jnp.bfloat16), "section").astype(jnp.float32),
    )
    layer_out = outputs.reshape(batches * slot_count, model_width)[None]
    input_grads = grads_in.reshape(batches * slot_count, model_width)[None]
    return (
        layer_out,
        input_grads,
        layer_total[0],
        layer_total[1],
        layer_total[2],
        layer_total[3],
        layer_total[4],
        layer_total[5],
        layer_total[6],
        layer_total[7],
        cross_total[0],
        cross_total[1],
        cross_total[2],
        cross_total[3],
    )


def solution(mesh):
    in_specs = (
        P("section", "batch", None),
        P("batch", None),
        P("batch"),
        P("batch", None),
        P("batch"),
        P("batch", None),
        P("section", None, None),
        P("section", None, None),
        P("section", None, None),
        P("section", None, None),
        P("section", None),
        P("section", None),
        P("section", None),
        P("section", None),
        P(),
        P(),
        P(),
        P(),
    )
    out_specs = (
        P("section", "batch", None),
        P("section", "batch", None),
        P("section", "batch", None),
        P("section", "batch", None),
        P("section", "batch", None),
        P("section", "batch", None),
        P("section", "batch"),
        P("section", "batch"),
        P("section", "batch"),
        P("section", "batch"),
        P("batch", None),
        P("batch", None),
        P("batch"),
        P("batch"),
    )
    return jax.shard_map(body, mesh=mesh, in_specs=in_specs, out_specs=out_specs, check_vma=False)
```

profile of v0, /device:TPU:6, one launch (start us, length us, event | category | flops | bytes accessed | tf_op | source)
XLA Modules:
  0.0 2036.3 jit_solution(9939261794532593443)
XLA Ops:
  13.4 385.2 %while.94 = (s32[]{:T(128)}, bf16[136,768]{1,0:T(8,128)(2,1)}, f32[6,136,768]{2,1,0:T(8,128)}, f32[7,136,768]{2,1,0:T(8,128)}, bf16[7,136,768]{2,1,0:T(8,128)(2,...) while((s32[]{:T(128)}, bf16[136,768]{1,0:T(8,128)(2,1)}, ...), condition=%wide.region_13.14_spmd.clone.clone, body=%wide.region_0.13_spmd.clone.clone.sunk | while | flops 2720141056 | bytes 68754920 | solution.py:480
  29.5 14.0 conditional.8
  194.7 14.0 conditional.8
  304.7 14.0 conditional.8
  359.7 14.0 conditional.8
  410.6 798.5 %while.95 = (s32[]{:T(128)}, bf16[136,768]{1,0:T(8,128)(2,1)S(1)}, f32[6,136,768]{2,1,0:T(8,128)}, f32[768,2304]{1,0:T(8,128)}, f32[768,768]{1,0:T(8,128)}, /*in...) while((s32[]{:T(128)}, bf16[136,768]{1,0:T(8,128)(2,1)S(1)}, ...), condition=%wide.region_44.45_spmd.clone.clone, body=%wide.region_14.44_spmd.clone.clone.sunk | while | flops 5493462528 | bytes 418685344 | solution.py:516
  457.4 32.0 %conditional.9 = (f32[136,768]{1,0:T(8,128)S(1)}, f32[136,768]{1,0:T(8,128)S(1)}, f32[768,2304]{0,1:T(8,128)}, f32[768,768]{1,0:T(8,128)}, f32[768]{0:T(1024)}, /*index=5*/f32[3072]{0:T(1024)S(1)}) conditional(s32[]{:T(128)} %convert_element_type.691, f32[136,768]{1,0:T(8,128)S(1)} %add_add_fusion.10, (s32[6]{0:T(128)}, s32[]{:T(128)}, ...), branch_computations={%region_19.19_spmd, %region_20.30_spmd} | conditional | flops 1435488896 | bytes 66449304 | solution.py:354
  565.0 32.0 %conditional.9 = (f32[136,768]{1,0:T(8,128)S(1)}, f32[136,768]{1,0:T(8,128)S(1)}, f32[768,2304]{0,1:T(8,128)}, f32[768,768]{1,0:T(8,128)}, f32[768]{0:T(1024)}, /*index=5*/f32[3072]{0:T(1024)S(1)}) conditional(s32[]{:T(128)} %convert_element_type.691, f32[136,768]{1,0:T(8,128)S(1)} %add_add_fusion.10, (s32[6]{0:T(128)}, s32[]{:T(128)}, ...), branch_computations={%region_19.19_spmd, %region_20.30_spmd} | conditional | flops 1435488896 | bytes 66449304 | solution.py:354
  676.8 32.0 %conditional.9 = (f32[136,768]{1,0:T(8,128)S(1)}, f32[136,768]{1,0:T(8,128)S(1)}, f32[768,2304]{0,1:T(8,128)}, f32[768,768]{1,0:T(8,128)}, f32[768]{0:T(1024)}, /*index=5*/f32[3072]{0:T(1024)S(1)}) conditional(s32[]{:T(128)} %convert_element_type.691, f32[136,768]{1,0:T(8,128)S(1)} %add_add_fusion.10, (s32[6]{0:T(128)}, s32[]{:T(128)}, ...), branch_computations={%region_19.19_spmd, %region_20.30_spmd} | conditional | flops 1435488896 | bytes 66449304 | solution.py:354
  788.6 32.0 %conditional.9 = (f32[136,768]{1,0:T(8,128)S(1)}, f32[136,768]{1,0:T(8,128)S(1)}, f32[768,2304]{0,1:T(8,128)}, f32[768,768]{1,0:T(8,128)}, f32[768]{0:T(1024)}, /*index=5*/f32[3072]{0:T(1024)S(1)}) conditional(s32[]{:T(128)} %convert_element_type.691, f32[136,768]{1,0:T(8,128)S(1)} %add_add_fusion.10, (s32[6]{0:T(128)}, s32[]{:T(128)}, ...), branch_computations={%region_19.19_spmd, %region_20.30_spmd} | conditional | flops 1435488896 | bytes 66449304 | solution.py:354
  900.5 32.0 %conditional.9 = (f32[136,768]{1,0:T(8,128)S(1)}, f32[136,768]{1,0:T(8,128)S(1)}, f32[768,2304]{0,1:T(8,128)}, f32[768,768]{1,0:T(8,128)}, f32[768]{0:T(1024)}, /*index=5*/f32[3072]{0:T(1024)S(1)}) conditional(s32[]{:T(128)} %convert_element_type.691, f32[136,768]{1,0:T(8,128)S(1)} %add_add_fusion.10, (s32[6]{0:T(128)}, s32[]{:T(128)}, ...), branch_computations={%region_19.19_spmd, %region_20.30_spmd} | conditional | flops 1435488896 | bytes 66449304 | solution.py:354
  1012.3 32.0 %conditional.9 = (f32[136,768]{1,0:T(8,128)S(1)}, f32[136,768]{1,0:T(8,128)S(1)}, f32[768,2304]{0,1:T(8,128)}, f32[768,768]{1,0:T(8,128)}, f32[768]{0:T(1024)}, /*index=5*/f32[3072]{0:T(1024)S(1)}) conditional(s32[]{:T(128)} %convert_element_type.691, f32[136,768]{1,0:T(8,128)S(1)} %add_add_fusion.10, (s32[6]{0:T(128)}, s32[]{:T(128)}, ...), branch_computations={%region_19.19_spmd, %region_20.30_spmd} | conditional | flops 1435488896 | bytes 66449304 | solution.py:354
  1124.1 32.0 %conditional.9 = (f32[136,768]{1,0:T(8,128)S(1)}, f32[136,768]{1,0:T(8,128)S(1)}, f32[768,2304]{0,1:T(8,128)}, f32[768,768]{1,0:T(8,128)}, f32[768]{0:T(1024)}, /*index=5*/f32[3072]{0:T(1024)S(1)}) conditional(s32[]{:T(128)} %convert_element_type.691, f32[136,768]{1,0:T(8,128)S(1)} %add_add_fusion.10, (s32[6]{0:T(128)}, s32[]{:T(128)}, ...), branch_computations={%region_19.19_spmd, %region_20.30_spmd} | conditional | flops 1435488896 | bytes 66449304 | solution.py:354
  1223.9 49.3 %reduce-scatter.29.cloned.1.call-done = f32[48,768]{1,0:T(8,128)} async-done(((f32[768,768]{1,0:T(8,128)}), f32[48,768]{1,0:T(8,128)}) %reduce-scatter.29.cloned.1.call-update) | async-done | bytes 147472 | tf_op jit(solution)/shard_map/reduce_scatter | solution.py:531
  1274.8 92.1 %reduce-scatter.27.cloned.1.call-done = f32[48,2304]{1,0:T(8,128)} async-done(((f32[768,2304]{1,0:T(8,128)}), f32[48,2304]{1,0:T(8,128)}) %reduce-scatter.27.cloned.1.call-update) | async-done | bytes 442384 | tf_op jit(solution)/shard_map/reduce_scatter | solution.py:530
  1373.4 55.3 %all-reduce.2 = (bf16[768]{0:T(1024)(128)(2,1)S(1)}, bf16[3072]{0:T(1024)(128)(2,1)S(1)}) all-reduce(f32[768]{0:T(1024)S(1)} %copy-done.68, f32[3072]{0:T(1024)S(1)} %get-tuple-element.1777), channel_id=12, replica_groups=mesh['section'=2,'batch'=16] {'batch'}, use_global_device_ids=true, to_apply=%region_57.58.clone | all-reduce | flops 3840 | bytes 23040
  1436.2 49.7 %reduce-scatter.37.cloned.1.call-done = f32[96,1]{1,0:T(8,128)} async-done(((f32[1536,1]{1,0:T(8,128)}), f32[96,1]{1,0:T(8,128)}) %reduce-scatter.37.cloned.1.call-update) | async-done | bytes 400
  1487.3 59.2 %reduce-scatter.31.cloned.1.call-done = f32[144,1]{1,0:T(8,128)} async-done(((f32[2304,1]{1,0:T(8,128)}), f32[144,1]{1,0:T(8,128)}) %reduce-scatter.31.cloned.1.call-update) | async-done | bytes 592
  1548.0 62.0 %reduce-scatter.33.cloned.1.call-done = f32[240,1]{1,0:T(8,128)} async-done(((f32[3840,1]{1,0:T(8,128)}), f32[240,1]{1,0:T(8,128)}) %reduce-scatter.33.cloned.1.call-update) | async-done | bytes 976
  1611.5 23.7 %all-reduce.7.cloned.1.call-done = (bf16[48,2304]{1,0:T(8,128)(2,1)}, bf16[48,768]{1,0:T(8,128)(2,1)}) async-done(((bf16[48,2304]{1,0:T(8,128)(2,1)}, bf16[48,768]{1,0:T(8,128)(2,1)}), (bf16[48,2304]{1,0:T(8,128)(2,1)}, bf16[48,768]{1,0:T(8,128)(2,1)})) %all-reduce.7.cloned.1.call-update) | async-done | bytes 294928 | tf_op jit(solution)/shard_map/psum | solution.py:536
  1638.5 64.7 %reduce-scatter.21.cloned.1.call-done = f32[1,48,768]{2,1,0:T(8,128)} async-done(((f32[1,768,768]{2,1,0:T(8,128)}), f32[1,48,768]{2,1,0:T(8,128)}) %reduce-scatter.21.cloned.1.call-update) | async-done | bytes 147472 | tf_op jit(solution)/shard_map/reduce_scatter | solution.py:521
  1703.1 94.4 %reduce-scatter.19.cloned.1.call-done = f32[1,48,2304]{2,1,0:T(8,128)} async-done(((f32[1,768,2304]{2,1,0:T(8,128)}), f32[1,48,2304]{2,1,0:T(8,128)}) %reduce-scatter.19.cloned.1.call-update) | async-done | bytes 442384 | tf_op jit(solution)/shard_map/reduce_scatter | solution.py:520
  1797.5 115.5 %reduce-scatter.23.cloned.1.call-done = f32[1,48,3072]{2,1,0:T(8,128)} async-done(((f32[1,768,3072]{2,1,0:T(8,128)}), f32[1,48,3072]{2,1,0:T(8,128)}) %reduce-scatter.23.cloned.1.call-update) | async-done | bytes 589840 | tf_op jit(solution)/shard_map/reduce_scatter | solution.py:522
  1913.0 116.4 %reduce-scatter.25.cloned.1.call-done = f32[1,192,768]{2,1,0:T(8,128)} async-done(((f32[1,3072,768]{2,1,0:T(8,128)}), f32[1,192,768]{2,1,0:T(8,128)}) %reduce-scatter.25.cloned.1.call-update) | async-done | bytes 589840 | tf_op jit(solution)/shard_map/reduce_scatter | solution.py:523
  (2448 shorter events, 1240.5 us)
Async XLA Ops:
  7.2 1266.0 %reduce-scatter.29.cloned.1.call-start = ((), (), s32[]{:S(2)}) async-start(), calls=%async_computation.15 | async-start | bytes 2506752 | tf_op jit(solution)/shard_map/reduce_scatter | solution.py:531
  55.8 12.6 collective-permute-start
  110.8 12.6 collective-permute-start
  165.9 12.6 collective-permute-start
  221.0 12.6 collective-permute-start
  330.9 12.6 collective-permute-start
  386.0 12.6 collective-permute-start
  501.8 35.6 %collective-permute-start.1 = (bf16[136,768]{1,0:T(8,128)(2,1)S(1)}, bf16[136,768]{1,0:T(8,128)(2,1)S(1)}, u32[]{:S(2)}, u32[]{:S(2)}) collective-permute-start(bf16[136,768]{1,0:T(8,128)(2,1)S(1)} %get-tuple-element.3615), channel_id=1, source_target_pairs={{16,0},{17,1},{18,2},{19,3},{20,4},{21,5},{22,6},{23,7},{24,8},{25... | collective-permute-start | bytes 626696 | tf_op jit(solution)/shard_map/while/body/eval_jaxpr/ppermute | solution.py:21
  609.5 39.8 %collective-permute-start.1 = (bf16[136,768]{1,0:T(8,128)(2,1)S(1)}, bf16[136,768]{1,0:T(8,128)(2,1)S(1)}, u32[]{:S(2)}, u32[]{:S(2)}) collective-permute-start(bf16[136,768]{1,0:T(8,128)(2,1)S(1)} %get-tuple-element.3615), channel_id=1, source_target_pairs={{16,0},{17,1},{18,2},{19,3},{20,4},{21,5},{22,6},{23,7},{24,8},{25... | collective-permute-start | bytes 626696 | tf_op jit(solution)/shard_map/while/body/eval_jaxpr/ppermute | solution.py:21
  721.3 39.8 %collective-permute-start.1 = (bf16[136,768]{1,0:T(8,128)(2,1)S(1)}, bf16[136,768]{1,0:T(8,128)(2,1)S(1)}, u32[]{:S(2)}, u32[]{:S(2)}) collective-permute-start(bf16[136,768]{1,0:T(8,128)(2,1)S(1)} %get-tuple-element.3615), channel_id=1, source_target_pairs={{16,0},{17,1},{18,2},{19,3},{20,4},{21,5},{22,6},{23,7},{24,8},{25... | collective-permute-start | bytes 626696 | tf_op jit(solution)/shard_map/while/body/eval_jaxpr/ppermute | solution.py:21
  833.1 39.8 %collective-permute-start.1 = (bf16[136,768]{1,0:T(8,128)(2,1)S(1)}, bf16[136,768]{1,0:T(8,128)(2,1)S(1)}, u32[]{:S(2)}, u32[]{:S(2)}) collective-permute-start(bf16[136,768]{1,0:T(8,128)(2,1)S(1)} %get-tuple-element.3615), channel_id=1, source_target_pairs={{16,0},{17,1},{18,2},{19,3},{20,4},{21,5},{22,6},{23,7},{24,8},{25... | collective-permute-start | bytes 626696 | tf_op jit(solution)/shard_map/while/body/eval_jaxpr/ppermute | solution.py:21
  944.9 39.8 %collective-permute-start.1 = (bf16[136,768]{1,0:T(8,128)(2,1)S(1)}, bf16[136,768]{1,0:T(8,128)(2,1)S(1)}, u32[]{:S(2)}, u32[]{:S(2)}) collective-permute-start(bf16[136,768]{1,0:T(8,128)(2,1)S(1)} %get-tuple-element.3615), channel_id=1, source_target_pairs={{16,0},{17,1},{18,2},{19,3},{20,4},{21,5},{22,6},{23,7},{24,8},{25... | collective-permute-start | bytes 626696 | tf_op jit(solution)/shard_map/while/body/eval_jaxpr/ppermute | solution.py:21
  1056.8 39.8 %collective-permute-start.1 = (bf16[136,768]{1,0:T(8,128)(2,1)S(1)}, bf16[136,768]{1,0:T(8,128)(2,1)S(1)}, u32[]{:S(2)}, u32[]{:S(2)}) collective-permute-start(bf16[136,768]{1,0:T(8,128)(2,1)S(1)} %get-tuple-element.3615), channel_id=1, source_target_pairs={{16,0},{17,1},{18,2},{19,3},{20,4},{21,5},{22,6},{23,7},{24,8},{25... | collective-permute-start | bytes 626696 | tf_op jit(solution)/shard_map/while/body/eval_jaxpr/ppermute | solution.py:21
  1168.6 39.8 %collective-permute-start.1 = (bf16[136,768]{1,0:T(8,128)(2,1)S(1)}, bf16[136,768]{1,0:T(8,128)(2,1)S(1)}, u32[]{:S(2)}, u32[]{:S(2)}) collective-permute-start(bf16[136,768]{1,0:T(8,128)(2,1)S(1)} %get-tuple-element.3615), channel_id=1, source_target_pairs={{16,0},{17,1},{18,2},{19,3},{20,4},{21,5},{22,6},{23,7},{24,8},{25... | collective-permute-start | bytes 626696 | tf_op jit(solution)/shard_map/while/body/eval_jaxpr/ppermute | solution.py:21
  1209.1 157.8 %reduce-scatter.27.cloned.1.call-start = ((), (), s32[]{:S(2)}) async-start(), calls=%async_computation.14 | async-start | bytes 7520256 | tf_op jit(solution)/shard_map/reduce_scatter | solution.py:530
  1217.3 217.5 %reduce-scatter.35.cloned.1.call-start = ((), (), s32[]{:S(2)}) async-start(), calls=%async_computation.18 | async-start | bytes 835584
  1219.2 266.7 %reduce-scatter.37.cloned.1.call-start = ((), (), s32[]{:S(2)}) async-start(), calls=%async_computation.19 | async-start | bytes 835584
  1220.4 326.1 %reduce-scatter.31.cloned.1.call-start = ((), (), s32[]{:S(2)}) async-start(), calls=%async_computation.16 | async-start | bytes 1253376
  1221.8 388.1 %reduce-scatter.33.cloned.1.call-start = ((), (), s32[]{:S(2)}) async-start(), calls=%async_computation.17 | async-start | bytes 2088960
  1223.8 411.4 %all-reduce.7.cloned.1.call-start = ((), (), s32[]{:S(2)}) async-start(), calls=%async_computation.20 | async-start | bytes 589824 | tf_op jit(solution)/shard_map/psum | solution.py:536
  1368.7 334.5 %reduce-scatter.21.cloned.1.call-start = ((), (), s32[]{:S(2)}) async-start(), calls=%async_computation.11 | async-start | bytes 2506752 | tf_op jit(solution)/shard_map/reduce_scatter | solution.py:521
  1369.4 428.1 %reduce-scatter.19.cloned.1.call-start = ((), (), s32[]{:S(2)}) async-start(), calls=%async_computation.10 | async-start | bytes 7520256 | tf_op jit(solution)/shard_map/reduce_scatter | solution.py:520
  1370.1 542.9 %reduce-scatter.23.cloned.1.call-start = ((), (), s32[]{:S(2)}) async-start(), calls=%async_computation.12 | async-start | bytes 10027008 | tf_op jit(solution)/shard_map/reduce_scatter | solution.py:522
  1370.7 658.7 %reduce-scatter.25.cloned.1.call-start = ((), (), s32[]{:S(2)}) async-start(), calls=%async_computation.13 | async-start | bytes 10027008 | tf_op jit(solution)/shard_map/reduce_scatter | solution.py:523
  (558 other events, 2884.9 us)
Sparse Core Ops, SparseCore 0:
  1209.3 63.8 reduce-scatter.28
  1277.7 89.1 reduce-scatter.26
  1370.5 56.0 reduce-scatter.34
  1430.3 55.4 reduce-scatter.36
  1489.3 57.0 reduce-scatter.30
  1550.0 59.8 reduce-scatter.32
  1612.9 22.2 all-reduce.6
  1639.5 63.5 reduce-scatter.20
  1708.3 89.2 reduce-scatter.18
  1802.1 110.9 reduce-scatter.22
  1918.3 111.1 reduce-scatter.24
where the time goes:
time: 2060 us; the launch traced here: 2040 us
  waiting for transfers between devices  730 us (35%)
  matrix products  534 us (26%)
  other arithmetic  382 us (19%)
  local copies, waits for them, and re-layouts  256 us (12%)
  blocking collectives  60.2 us (3%)
  loops' own time  39.6 us (2%)
    dot_general x56, matrix products, matmul_tn(): lax.dot_general(left_mat, right_mat, (((0,), (0,)), ((), ())), preferred_...  190 us
    unnamed x15, waiting for transfers between devices  174 us
    dot_general x49, matrix products, matmul(): return jnp.dot(left_mat, right_mat, preferred_element_type=jnp.float32)  157 us
    dot_general x56, matrix products, matmul_nt(): lax.dot_general(left_mat, right_mat, (((1,), (1,)), ((), ())), preferred_...  128 us
    reduce_scatter x1, waiting for transfers between devices, body(): lax.psum_scatter(layer_acc[3][None], 'batch', scatter_dimension=1, tiled=...  116 us
    reduce_scatter x1, waiting for transfers between devices, body(): lax.psum_scatter(layer_acc[2][None], 'batch', scatter_dimension=1, tiled=...  116 us
    add x28, other arithmetic, backward_tick(): cross_acc = jax.tree.map(jnp.add, cross_acc, cross_parts)  105 us
    reduce_scatter x1, waiting for transfers between devices, body(): lax.psum_scatter(layer_acc[0][None], 'batch', scatter_dimension=1, tiled=...  94.4 us
  transfers between devices with their start and end apart: 25, of which 10 were waited for; matrix products, arithmetic and copies ran while one was open for 18% of the time, Pallas kernels for 0%

commit v1 on v0

v1 whole, which is shorter than its diff:
```python
import jax
import jax.numpy as jnp
from jax import lax
from jax.experimental import pallas as pl
from jax.experimental.pallas import tpu as pltpu
from jax.sharding import PartitionSpec as P

H = 12
HD = 64
PAIRS = H // 2
LANES = 2 * HD
GRID = 15
SCORE_SCALE = 0.125
NORM_EPS = 1e-06
FAR = 1e33
CHUNK = 16
BF = jnp.bfloat16
F32 = jnp.float32
VMEM_LIMIT = 60 << 20
CHEAP = pl.CostEstimate(flops=1, bytes_accessed=1, transcendentals=0)
ANY = pl.BlockSpec(memory_space=pl.ANY)
VM = pl.BlockSpec(memory_space=pltpu.VMEM)
SM = pl.BlockSpec(memory_space=pltpu.SMEM)


def dot_nn(left, right):
    return jnp.dot(left, right, preferred_element_type=F32)


def dot_tn(left, right):
    return lax.dot_general(left, right, (((0,), (0,)), ((), ())), preferred_element_type=F32)


def dot_nt(left, right):
    return lax.dot_general(left, right, (((1,), (1,)), ((), ())), preferred_element_type=F32)


class Copies:
    def __init__(self, sems):
        self.sems = sems
        self.used = 0

    def start(self, source, target):
        copy = pltpu.make_async_copy(source, target, self.sems.at[self.used])
        self.used += 1
        copy.start()
        return copy

    def reserve(self, count):
        first = self.used
        self.used += count
        return lambda at: self.sems.at[first + at]


def spans(rows):
    return [slice(at, at + CHUNK) for at in range(0, rows, CHUNK)]


def norm_parts(values):
    average = jnp.mean(values, axis=-1, keepdims=True)
    centred = values - average
    spread = jnp.mean(centred * centred, axis=-1, keepdims=True)
    scale = lax.rsqrt(spread + NORM_EPS)
    return centred * scale, scale


def norm_forward(source, gain, shift, target):
    for span in spans(source.shape[0]):
        unit, _ = norm_parts(source[span, :])
        target[span, :] = (unit * gain + shift).astype(BF)


def norm_backward(source, gain, upstream, residual, target):
    gain_sum = jnp.zeros((8, source.shape[1]), F32)
    shift_sum = jnp.zeros((8, source.shape[1]), F32)
    for span in spans(source.shape[0]):
        unit, scale = norm_parts(source[span, :])
        grad = upstream[span, :]
        product = grad * unit
        gain_sum = gain_sum + product[:8] + product[8:]
        shift_sum = shift_sum + grad[:8] + grad[8:]
        inner = grad * gain
        mean_one = jnp.mean(inner, axis=-1, keepdims=True)
        mean_two = jnp.mean(inner * unit, axis=-1, keepdims=True)
        target[span, :] = residual[span, :] + scale * (inner - mean_one - unit * mean_two)
    return (
        jnp.sum(gain_sum, axis=0, keepdims=True),
        jnp.sum(shift_sum, axis=0, keepdims=True),
    )


def gelu_both(values):
    cdf = 0.5 + 0.5 * lax.erf(values * 0.7071067811865476)
    density = 0.3989422804014327 * jnp.exp(-0.5 * values * values)
    return values * cdf, cdf + values * density


def place(positions):
    values = positions
    row = jnp.floor((values + 0.5) * (1.0 / GRID))
    return row, values - GRID * row


def distances(key_col, query_row, live_keys):
    row_q, col_q = place(query_row)
    row_k, col_k = place(key_col)
    gap_row = row_q - row_k
    gap_col = col_q - col_k
    distance = jnp.sqrt(gap_row * gap_row + gap_col * gap_col)
    slot = lax.broadcasted_iota(jnp.int32, distance.shape, 0)
    return jnp.where(slot < live_keys, distance, FAR)


def both_heads(pair):
    first = lax.broadcasted_iota(jnp.int32, pair.shape, 1) < HD
    zero = jnp.zeros_like(pair)
    return jnp.concatenate([jnp.where(first, pair, zero), jnp.where(first, zero, pair)], axis=0)


def one_pair(stacked):
    half = stacked.shape[0] // 2
    first = lax.broadcasted_iota(jnp.int32, (half, LANES), 1) < HD
    return jnp.where(first, stacked[:half], stacked[half:])


def by_size(plan, most_live, work):
    def step(image, carry):
        if plan.slots <= LANES:
            work(image, plan.slots)
        else:
            live = most_live(image)

            @pl.when(live <= LANES)
            def _():
                work(image, LANES)

            @pl.when(live > LANES)
            def _():
                work(image, plan.slots)

        return carry

    lax.fori_loop(0, plan.per, step, 0)


def rows_of(plan, image, first, size):
    return pl.ds(pl.multiple_of(image * plan.slots + first, 8), size)


def pair_lanes(base, pair):
    if isinstance(pair, int):
        return pl.ds(base + pair * LANES, LANES)
    return pl.ds(pl.multiple_of(base + pair * LANES, LANES), LANES)


def over_pairs(plan, work, size):
    unroll = PAIRS if size <= LANES else plan.unroll

    def step(at, carry):
        for part in range(unroll):
            work(at * unroll + part)
        return carry

    if unroll == PAIRS:
        step(0, 0)
    else:
        lax.fori_loop(0, PAIRS // unroll, step, 0)


def attend(plan, most_live, query, keys, values, spread, slopes, heard, weights):
    def work(image, size):
        rows = rows_of(plan, image, 0, size)
        if size < plan.slots:
            rest = rows_of(plan, image, size, plan.slots - size)
            heard[rest, :] = jnp.zeros((plan.slots - size, plan.width), F32)
        spread(image, size)
        gap_ref = spread.target

        def one(pair):
            q = both_heads(query[0][rows, pair_lanes(query[1], pair)]).astype(BF)
            k = keys[0][rows, pair_lanes(keys[1], pair)].astype(BF)
            v = values[0][rows, pair_lanes(values[1], pair)].astype(BF)
            first = lax.broadcasted_iota(jnp.int32, (1, 2 * size), 1) < size
            slope = jnp.where(first, slopes[2 * pair], slopes[2 * pair + 1])
            scores = dot_nt(k, q) - slope * gap_ref[image, :size, : 2 * size]
            scores = jnp.exp(scores - jnp.max(scores, axis=0, keepdims=True))
            totals = jnp.sum(scores, axis=0, keepdims=True)
            p = (scores * (1.0 / totals)).astype(BF)
            weights[image * PAIRS + pair, :size, : 2 * size] = p
            heard[rows, pair_lanes(0, pair)] = one_pair(dot_tn(p, v))

        over_pairs(plan, one, size)

    by_size(plan, most_live, work)


def attend_back(plan, most_live, query, keys, values, grad_heard, weights, grads):
    grad_q, grad_k, grad_v = grads

    def work(image, size):
        rows = rows_of(plan, image, 0, size)
        if size < plan.slots:
            rest = rows_of(plan, image, size, plan.slots - size)
            for ref, offset in grads:
                ref[rest, offset : offset + plan.width] = jnp.zeros((plan.slots - size, plan.width), F32)

        def one(pair):
            q = both_heads(query[0][rows, pair_lanes(query[1], pair)]).astype(BF)
            k = keys[0][rows, pair_lanes(keys[1], pair)].astype(BF)
            v = values[0][rows, pair_lanes(values[1], pair)].astype(BF)
            g = both_heads(grad_heard[rows, pair_lanes(0, pair)]).astype(BF)
            p = weights[image * PAIRS + pair, :size, : 2 * size]
            wide = p.astype(F32)
            product = dot_nt(v, g) * wide
            grad_s = (product - wide * jnp.sum(product, axis=0, keepdims=True)).astype(BF)
            grad_v[0][rows, pair_lanes(grad_v[1], pair)] = dot_nn(p, g)
            grad_k[0][rows, pair_lanes(grad_k[1], pair)] = dot_nn(grad_s, q)
            grad_q[0][rows, pair_lanes(grad_q[1], pair)] = one_pair(dot_tn(grad_s, k)) * SCORE_SCALE

        over_pairs(plan, one, size)

    by_size(plan, most_live, work)


def columns_of(positions):
    images = positions.shape[0]
    low = positions.astype(F32).astype(BF)
    row = lax.broadcasted_iota(jnp.int32, (images, LANES), 0)
    lane = lax.broadcasted_iota(jnp.int32, (images, LANES), 1)
    return dot_tn(low, (row == lane).astype(F32).astype(BF))


def twice(positions, size):
    slots = positions.shape[1]
    low = positions.astype(F32).astype(BF)
    row = lax.broadcasted_iota(jnp.int32, (slots, 2 * size), 0)
    lane = lax.broadcasted_iota(jnp.int32, (slots, 2 * size), 1)
    from_slot = jnp.where(lane < size, lane, lane - size)
    return dot_nn(low, (row == from_slot).astype(F32).astype(BF))


class Spread:
    def __init__(self, plan, r, target, k, key_positions, key_count):
        self.plan, self.r, self.target, self.k = plan, r, target, k
        self.key_positions, self.key_count = key_positions, key_count

    def __call__(self, image, size):
        at = self.k * self.plan.per + image
        query = twice(self.r["positions"][pl.ds(at, 1), :], size)
        keys = columns_of(self.r[self.key_positions][pl.ds(at, 1), :])
        self.target[image, :size, : 2 * size] = distances(
            keys[:size, :1], query, self.r[self.key_count][at]
        )


def most_live(plan, r, k, names):
    def live(image):
        found = r[names[0]][k * plan.per + image]
        for name in names[1:]:
            found = jnp.maximum(found, r[name][k * plan.per + image])
        return found

    return live


def fill_rows(target, images, slots, counts, first_image, source):
    for image in range(images):
        live = counts[first_image + image]
        for at in range(0, slots, 8):
            span = slice(image * slots + at, image * slots + at + 8)
            row = at + lax.broadcasted_iota(jnp.int32, (8, source.shape[1]), 0)
            target[span, :] = jnp.where(row < live, source[span, :], 0.0)


class Plan:
    def __init__(self, batches, slots, width, hidden, halving, unroll=1):
        self.batches, self.slots, self.width, self.hidden = batches, slots, width, hidden
        self.halving = halving
        self.unroll = unroll
        self.per = 2 if batches % 2 == 0 else 1
        self.steps = batches // self.per
        self.rows = self.per * slots
        self.total = batches * slots

    def unrolled(self, unroll):
        return Plan(self.batches, self.slots, self.width, self.hidden, self.halving, unroll)


def small_shape(plan):
    rows = 13 + plan.hidden // plan.width
    return (-(-rows // 8) * 8, plan.width)


WEIGHT_NAMES = ("wqkv", "wout", "wfc1", "wfc2", "wcqkv", "wcout")


def scratch_shapes(plan):
    r, d, f = plan.rows, plan.width, plan.hidden
    w = {
        "wqkv": ((d, 3 * d), BF),
        "wout": ((d, d), BF),
        "wfc1": ((d, f), BF),
        "wfc2": ((f, d), BF),
        "wcqkv": ((d, 3 * d), BF),
        "wcout": ((d, d), BF),
        "xb": ((r, d), BF),
        "x": ((r, d), F32),
        "n": ((r, d), BF),
        "qkv": ((r, 3 * d), F32),
        "p": ((plan.per * PAIRS, plan.slots, 2 * plan.slots), BF),
        "dist": ((plan.per, plan.slots, 2 * plan.slots), F32),
        "heard": ((r, d), F32),
        "o": ((r, d), BF),
        "h": ((r, d), F32),
        "n2": ((r, d), BF),
        "u": ((r, f), F32),
        "a": ((r, f), BF),
        "gp": ((r, f), BF),
        "y": ((r, d), F32),
        "yout": ((r, d), F32),
        "ysend": ((r, d), BF),
        "gin": ((r, d), BF),
        "g": ((r, d), F32),
        "gbr": ((r, d), BF),
        "du": ((r, f), BF),
        "dn": ((r, d), F32),
        "dh": ((r, d), F32),
        "gm": ((r, d), BF),
        "go": ((r, d), F32),
        "dqkv": ((r, 3 * d), F32),
        "dqkvb": ((r, 3 * d), BF),
        "dx": ((r, d), F32),
        "dxb": ((r, d), BF),
        "ln": ((8, d), F32),
        "cdist": ((plan.per, plan.slots, 2 * plan.slots), F32),
        "m": ((r, d), BF),
        "cq": ((r, d), F32),
        "ckvb": ((r, 2 * d), BF),
        "ckv": ((r, 2 * d), F32),
        "cp": ((plan.per * PAIRS, plan.slots, 2 * plan.slots), BF),
        "cheard": ((r, d), F32),
        "co": ((r, d), BF),
        "h2": ((r, d), F32),
        "gaf": ((r, d), BF),
        "cgo": ((r, d), F32),
        "dcqkv": ((r, 3 * d), F32),
        "dcq": ((r, d), BF),
        "dckv": ((r, 2 * d), BF),
        "dm": ((r, d), F32),
        "dmid": ((r, d), F32),
        "gl": ((plan.total, f), BF),
        "gr": ((plan.total, f), BF),
        "gsums": ((8, f), F32),
        "small": (small_shape(plan), F32),
        "gnat": ((2, 16, d // 16, d) if plan.halving else (2, d, d), BF),
        "gnat_tall": ((2, 4, d // 4, d), BF),
        "gout": ((2, 2, 8, d // 16, d), BF),
        "gout_tall": ((2, 2, 2, d // 4, d), BF),
        "rdr": ((plan.total, d), F32),
        "rb": ((plan.total, d), BF),
        "rkv": ((plan.total, 2 * d), BF),
    }
    return w


def chunk_shape(plan, height, breadth):
    if not plan.halving:
        return (height, breadth), BF
    if height == plan.width:
        return (8, height // 16, breadth), BF
    return (2, 2, 2, height // 16, breadth), BF


def chunk_state(name, height, breadth):
    def size(plan, amount):
        return plan.hidden if amount is None else amount * plan.width

    def main(plan):
        return chunk_shape(plan, size(plan, height), size(plan, breadth))

    def sums(plan):
        return (8, size(plan, breadth)), F32

    return {name: main, name + "_send": main, name + "_sums": sums}


STATE = {
    "n": lambda p: ((p.total, p.width), BF),
    "o": lambda p: ((p.total, p.width), BF),
    "n2": lambda p: ((p.total, p.width), BF),
    "a": lambda p: ((p.total, p.hidden), BF),
    "layer_out": lambda p: ((p.total, p.width), F32),
    "qkv": lambda p: ((p.total, 3 * p.width), F32),
    "p": lambda p: ((p.batches * PAIRS, p.slots, 2 * p.slots), BF),
    "h": lambda p: ((p.total, p.width), F32),
    "gp": lambda p: ((p.total, p.hidden), BF),
    "ckv": lambda p: ((p.total, 2 * p.width), BF),
    "gbr": lambda p: ((p.total, p.width), BF),
    "du": lambda p: ((p.total, p.hidden), BF),
    "gm": lambda p: ((p.total, p.width), BF),
    "dqkv": lambda p: ((p.total, 3 * p.width), BF),
    "input_grads": lambda p: ((p.total, p.width), F32),
    "m": lambda p: ((p.total, p.width), BF),
    "co": lambda p: ((p.total, p.width), BF),
    "gaf": lambda p: ((p.total, p.width), BF),
    "dcq": lambda p: ((p.total, p.width), BF),
    "dckv": lambda p: ((p.total, 2 * p.width), BF),
    "between": lambda p: ((p.rows, p.width), F32),
    "send": lambda p: ((p.rows, p.width), BF),
    "ln": lambda p: ((8, p.width), F32),
    "small": lambda p: (small_shape(p), F32),
    **chunk_state("cross", 1, 4),
    **chunk_state("fc2", None, 1),
    **chunk_state("fc1", 1, None),
    **chunk_state("attn", 1, 4),
}

FORWARD_0 = dict(
    reads=("streams",),
    writes=("n", "o", "n2", "a", "layer_out", "qkv", "p", "h", "gp", "send"),
    weights=("wqkv", "wout", "wfc1", "wfc2"),
    scratch=("xb", "x", "n", "qkv", "p", "dist", "heard", "o", "h", "n2", "u", "a", "gp", "y", "yout", "ysend"),
)
RADAR = dict(reads=("streams",), writes=("ckv",), weights=("wcqkv",), scratch=["rb", "rkv"])
MERGED = dict(
    reads=("received", "cotangent", "ckv"),
    writes=("n", "o", "n2", "a", "layer_out", "gbr", "du", "gm", "dqkv", "m", "co", "gaf", "dcq", "dckv", "send", "ln"),
    weights=WEIGHT_NAMES,
    scratch=("xb", "x", "n", "qkv", "p", "dist", "heard", "o", "h", "n2", "u", "a", "gp", "y", "yout", "gin", "g", "gbr", "du", "dn", "dh", "gm", "go", "dqkv", "dqkvb", "dxb", "ln", "cdist", "m", "cq", "ckvb", "ckv", "cp", "cheard", "co", "h2", "gaf", "cgo", "dcqkv", "dcq", "dckv", "dm", "dmid",),
)
BACKWARD_0 = dict(
    reads=("streams", "returned", "qkv", "p", "h", "gp"),
    writes=("gbr", "du", "gm", "dqkv", "input_grads", "ln"),
    weights=("wfc2", "wfc1", "wout", "wqkv"),
    scratch=("xb", "x", "qkv", "p", "h", "gp", "gin", "g", "gbr", "du", "dn", "dh", "gm", "go", "dqkv", "dqkvb", "dx", "ln"),
)
BACKWARD_MLP = dict(
    reads=("returned", "gp", "h"),
    writes=("du", "between", "ln"),
    weights=("wfc2", "wfc1"),
    scratch=("h", "gp", "gin", "g", "gbr", "du", "dn", "dh", "ln"),
)
BACKWARD_SELF = dict(
    reads=("between", "streams", "qkv", "p"),
    writes=("gm", "dqkv", "input_grads", "ln"),
    weights=("wout", "wqkv"),
    scratch=("xb", "x", "qkv", "p", "dn", "dh", "gm", "go", "dqkv", "dqkvb", "dx", "ln"),
)
RADAR_BACK = dict(
    reads=("dckv",), writes=("input_grads",), weights=("wcqkv",), scratch=("rkv", "rdr")
)
GRAD_SCRATCH = ("gl", "gr", "gnat", "gout", "gsums")
GRADS_CROSS = dict(
    reads=("m", "streams", "co", "dcq", "dckv", "gaf"),
    writes=("cross", "cross_send", "cross_sums"),
    weights=(),
    scratch=GRAD_SCRATCH,
)
GRADS_FC2 = dict(
    reads=("a", "gbr", "returned"),
    writes=("fc2", "fc2_send", "fc2_sums"),
    weights=(),
    scratch=("gl", "gr", "gnat", "gnat_tall", "gout_tall", "gsums", "gin", "dn", "g"),
)
GRADS_FC1 = dict(
    reads=("n2", "du"), writes=("fc1", "fc1_send", "fc1_sums"), weights=(), scratch=GRAD_SCRATCH
)
GRADS_ATTN = dict(
    reads=("n", "o", "dqkv", "gm", "fc1_sums", "fc2_sums", "cross_sums"),
    writes=("attn", "attn_send", "attn_sums", "small"),
    weights=(),
    scratch=GRAD_SCRATCH + ("small",),
)
GRADS_MORE = {
    name: tuple(dict.fromkeys(GRADS_FC2[name] + GRADS_FC1[name]))
    for name in GRADS_FC2
}
JOBS = {
    "forward": FORWARD_0,
    "radar": RADAR,
    "merged": MERGED,
    "backward": BACKWARD_0,
    "backward_mlp": BACKWARD_MLP,
    "backward_self": BACKWARD_SELF,
    "radar_back": RADAR_BACK,
    "grads_cross": GRADS_CROSS,
    "grads_fc2": GRADS_FC2,
    "grads_fc1": GRADS_FC1,
    "grads_attn": GRADS_ATTN,
    "grads_more": GRADS_MORE,
}
TILE = 768


def tiles(extent, tile=TILE):
    return [slice(at, min(at + tile, extent)) for at in range(0, extent, tile)]


def self_forward(plan, r, s, c, k, waits, save):
    d = plan.width
    rows = pl.ds(k * plan.rows, plan.rows)
    out = []
    gain, shift, bias = r["gains"], r["shifts"], r["attn_bias"]
    norm_forward(s["x"], gain[:, :d], shift[:, :d], s["n"])
    out.append(c.start(s["n"], r["n"].at[rows]))
    waits["wqkv"].wait()
    normed = s["n"][...]
    s["qkv"][:, :d] = (dot_nn(normed, s["wqkv"][:, :d]) + bias[:, :d]).astype(BF).astype(F32) * SCORE_SCALE
    s["qkv"][:, d : 2 * d] = dot_nn(normed, s["wqkv"][:, d : 2 * d])
    s["qkv"][:, 2 * d :] = dot_nn(normed, s["wqkv"][:, 2 * d :]) + bias[:, d : 2 * d]
    if save:
        out.append(c.start(s["qkv"], r["qkv"].at[rows]))
    attend(
        plan,
        most_live(plan, r, k, ("counts",)),
        (s["qkv"], 0),
        (s["qkv"], d),
        (s["qkv"], 2 * d),
        Spread(plan, r, s["dist"], k, "positions", "counts"),
        r["slopes"],
        s["heard"],
        s["p"],
    )
    if save:
        out.append(c.start(s["p"], r["p"].at[pl.ds(k * plan.per * PAIRS, plan.per * PAIRS)]))
    s["o"][...] = s["heard"][...].astype(BF)
    out.append(c.start(s["o"], r["o"].at[rows]))
    waits["wout"].wait()
    s["h"][...] = s["x"][...] + dot_nn(s["o"][...], s["wout"][...]) + bias[:, 2 * d :]
    if save:
        out.append(c.start(s["h"], r["h"].at[rows]))
    return out


def mlp_forward(plan, r, s, c, k, waits, after, save):
    d, f = plan.width, plan.hidden
    rows = pl.ds(k * plan.rows, plan.rows)
    out = []
    norm_forward(after, r["gains"][:, d:], r["shifts"][:, d:], s["n2"])
    out.append(c.start(s["n2"], r["n2"].at[rows]))
    waits["wfc1"].wait()
    bias = r["mlp_bias"]
    for tile in tiles(f):
        s["u"][:, tile] = dot_nn(s["n2"][...], s["wfc1"][:, tile]) + bias[:, tile]
        for span in spans(plan.rows):
            active, slope = gelu_both(s["u"][span, tile])
            s["a"][span, tile] = active.astype(BF)
            s["gp"][span, tile] = slope.astype(BF)
    out.append(c.start(s["a"], r["a"].at[rows]))
    if save:
        out.append(c.start(s["gp"], r["gp"].at[rows]))
    waits["wfc2"].wait()
    s["y"][...] = after[...] + dot_nn(s["a"][...], s["wfc2"][...]) + bias[:, f:]
    fill_rows(s["yout"], plan.per, plan.slots, r["counts"], k * plan.per, s["y"])
    out.append(c.start(s["yout"], r["layer_out"].at[rows]))
    return out


def mlp_backward(plan, r, s, c, k, waits, after, target):
    d, f = plan.width, plan.hidden
    rows = pl.ds(k * plan.rows, plan.rows)
    out = []
    s["dn"][...] = s["gin"][...].astype(F32)
    fill_rows(s["g"], plan.per, plan.slots, r["counts"], k * plan.per, s["dn"])
    s["gbr"][...] = s["g"][...].astype(BF)
    if "gbr" in r:
        out.append(c.start(s["gbr"], r["gbr"].at[rows]))
    if "wfc2" in waits:
        waits["wfc2"].wait()
    for tile in tiles(f):
        grad = dot_nt(s["gbr"][...], s["wfc2"][tile, :])
        s["du"][:, tile] = (grad * s["gp"][:, tile].astype(F32)).astype(BF)
    out.append(c.start(s["du"], r["du"].at[rows]))
    if "wfc1" in waits:
        waits["wfc1"].wait()
    s["dn"][...] = dot_nt(s["du"][...], s["wfc1"][...])
    sums = norm_backward(after, r["gains"][:, d:], s["dn"], s["g"], target)
    return out, sums


def self_backward(plan, r, s, c, k, waits, grad, target):
    d = plan.width
    rows = pl.ds(k * plan.rows, plan.rows)
    out = []
    s["gm"][...] = grad[...].astype(BF)
    out.append(c.start(s["gm"], r["gm"].at[rows]))
    if "wout" in waits:
        waits["wout"].wait()
    s["go"][...] = dot_nt(s["gm"][...], s["wout"][...])
    attend_back(
        plan,
        most_live(plan, r, k, ("counts",)),
        (s["qkv"], 0),
        (s["qkv"], d),
        (s["qkv"], 2 * d),
        s["go"],
        s["p"],
        [(s["dqkv"], part * d) for part in range(3)],
    )
    s["dqkvb"][...] = s["dqkv"][...].astype(BF)
    out.append(c.start(s["dqkvb"], r["dqkv"].at[rows]))
    if "wqkv" in waits:
        waits["wqkv"].wait()
    s["dn"][...] = dot_nt(s["dqkvb"][...], s["wqkv"][...])
    sums = norm_backward(s["x"], r["gains"][:, :d], s["dn"], grad, target)
    return out, sums


def write_sums(s, c, r, parts):
    s["ln"][...] = jnp.zeros_like(s["ln"])
    for at, part in enumerate(parts):
        s["ln"][at : at + 1, :] = part
    return c.start(s["ln"], r["ln"])


def start_weights(r, s, c, names):
    return {name: c.start(r[name], s[name]) for name in names}


def run_forward(plan, r, s, c, k):
    rows = pl.ds(k * plan.rows, plan.rows)
    arrive = c.start(r["streams"].at[rows], s["xb"])
    waits = start_weights(r, s, c, FORWARD_0["weights"])
    arrive.wait()
    s["x"][...] = s["xb"][...].astype(F32)
    out = self_forward(plan, r, s, c, k, waits, True)
    out += mlp_forward(plan, r, s, c, k, waits, s["h"], True)
    s["ysend"][...] = s["yout"][...].astype(BF)
    out.append(c.start(s["ysend"], r["send"]))
    for copy in out:
        copy.wait()


def run_radar(plan, r, s, c, k):
    d = plan.width
    arrive = c.start(r["streams"], s["rb"])
    weight = c.start(r["wcqkv"], s["wcqkv"])
    arrive.wait()
    weight.wait()
    s["rkv"][:, :d] = dot_nn(s["rb"][...], s["wcqkv"][:, d : 2 * d]).astype(BF)
    s["rkv"][:, d:] = (
        dot_nn(s["rb"][...], s["wcqkv"][:, 2 * d :]) + r["cross_bias"][:, d : 2 * d]
    ).astype(BF)
    c.start(s["rkv"], r["ckv"]).wait()


def run_merged(plan, r, s, c, k):
    plan = plan.unrolled(3)
    d = plan.width
    rows = pl.ds(k * plan.rows, plan.rows)
    arrive = c.start(r["received"], s["xb"])
    waits = start_weights(r, s, c, ("wqkv", "wout", "wcqkv", "wcout", "wfc1", "wfc2"))
    arrive_kv = c.start(r["ckv"].at[rows], s["ckvb"])
    arrive_grad = c.start(r["cotangent"].at[rows], s["gin"])
    arrive.wait()
    s["x"][...] = s["xb"][...].astype(F32)
    out = self_forward(plan, r, s, c, k, waits, False)
    bias = r["cross_bias"]
    norm_forward(s["h"], r["cross_gain"][...], bias[:, 3 * d :], s["m"])
    out.append(c.start(s["m"], r["m"].at[rows]))
    waits["wcqkv"].wait()
    s["cq"][...] = (dot_nn(s["m"][...], s["wcqkv"][:, :d]) + bias[:, :d]).astype(BF).astype(F32) * SCORE_SCALE
    arrive_kv.wait()
    s["ckv"][...] = s["ckvb"][...].astype(F32)
    live = most_live(plan, r, k, ("counts", "radar_counts"))
    attend(
        plan,
        live,
        (s["cq"], 0),
        (s["ckv"], 0),
        (s["ckv"], d),
        Spread(plan, r, s["cdist"], k, "radar_positions", "radar_counts"),
        r["slopes"],
        s["cheard"],
        s["cp"],
    )
    s["co"][...] = s["cheard"][...].astype(BF)
    out.append(c.start(s["co"], r["co"].at[rows]))
    waits["wcout"].wait()
    s["h2"][...] = s["h"][...] + dot_nn(s["co"][...], s["wcout"][...]) + bias[:, 2 * d : 3 * d]
    out += mlp_forward(plan, r, s, c, k, waits, s["h2"], False)
    arrive_grad.wait()
    more, sums_two = mlp_backward(plan, r, s, c, k, {}, s["h2"], s["dh"])
    out += more
    s["gaf"][...] = s["dh"][...].astype(BF)
    out.append(c.start(s["gaf"], r["gaf"].at[rows]))
    s["cgo"][...] = dot_nt(s["gaf"][...], s["wcout"][...])
    attend_back(
        plan,
        live,
        (s["cq"], 0),
        (s["ckv"], 0),
        (s["ckv"], d),
        s["cgo"],
        s["cp"],
        [(s["dcqkv"], part * d) for part in range(3)],
    )
    s["dcq"][...] = s["dcqkv"][:, :d].astype(BF)
    s["dckv"][...] = s["dcqkv"][:, d:].astype(BF)
    out.append(c.start(s["dcq"], r["dcq"].at[rows]))
    out.append(c.start(s["dckv"], r["dckv"].at[rows]))
    s["dm"][...] = dot_nt(s["dcq"][...], s["wcqkv"][:, :d])
    sums_cross = norm_backward(s["h"], r["cross_gain"][...], s["dm"], s["dh"], s["dmid"])
    more, sums_one = self_backward(plan, r, s, c, k, {}, s["dmid"], s["dh"])
    out += more
    s["dxb"][...] = s["dh"][...].astype(BF)
    out.append(c.start(s["dxb"], r["send"]))
    out.append(write_sums(s, c, r, sums_one + sums_two + sums_cross))
    for copy in out:
        copy.wait()


def load_mlp_back(plan, r, s, c, k):
    rows = pl.ds(k * plan.rows, plan.rows)
    arrive = [c.start(r["returned"], s["gin"])]
    waits = start_weights(r, s, c, ("wfc2",))
    arrive.append(c.start(r["gp"].at[rows], s["gp"]))
    waits.update(start_weights(r, s, c, ("wfc1",)))
    arrive.append(c.start(r["h"].at[rows], s["h"]))
    return arrive, waits


def load_self_back(plan, r, s, c, k):
    rows = pl.ds(k * plan.rows, plan.rows)
    waits = start_weights(r, s, c, ("wout",))
    arrive = [
        c.start(r["qkv"].at[rows], s["qkv"]),
        c.start(r["p"].at[pl.ds(k * plan.per * PAIRS, plan.per * PAIRS)], s["p"]),
    ]
    waits.update(start_weights(r, s, c, ("wqkv",)))
    arrive.append(c.start(r["streams"].at[rows], s["xb"]))
    return arrive, waits


def wait_all(copies):
    for copy in copies:
        copy.wait()


def run_backward(plan, r, s, c, k):
    rows = pl.ds(k * plan.rows, plan.rows)
    arrive, waits = load_mlp_back(plan, r, s, c, k)
    arrive_self, waits_self = load_self_back(plan, r, s, c, k)
    waits.update(waits_self)
    wait_all(arrive)
    out, sums_two = mlp_backward(plan, r, s, c, k, waits, s["h"], s["dh"])
    wait_all(arrive_self)
    s["x"][...] = s["xb"][...].astype(F32)
    more, sums_one = self_backward(plan, r, s, c, k, waits, s["dh"], s["dx"])
    out += more
    out.append(c.start(s["dx"], r["input_grads"].at[rows]))
    out.append(write_sums(s, c, r, sums_one + sums_two))
    wait_all(out)


def run_backward_mlp(plan, r, s, c, k):
    arrive, waits = load_mlp_back(plan, r, s, c, k)
    wait_all(arrive)
    out, sums_two = mlp_backward(plan, r, s, c, k, waits, s["h"], s["dh"])
    out.append(c.start(s["dh"], r["between"]))
    nothing = jnp.zeros_like(sums_two[0])
    out.append(write_sums(s, c, r, (nothing, nothing) + sums_two))
    wait_all(out)


def run_backward_self(plan, r, s, c, k):
    rows = pl.ds(k * plan.rows, plan.rows)
    arrive = [c.start(r["between"], s["dh"])]
    more, waits = load_self_back(plan, r, s, c, k)
    wait_all(arrive + more)
    s["x"][...] = s["xb"][...].astype(F32)
    out, sums_one = self_backward(plan, r, s, c, k, waits, s["dh"], s["dx"])
    out.append(c.start(s["dx"], r["input_grads"].at[rows]))
    out.append(write_sums(s, c, r, sums_one))
    wait_all(out)


def run_radar_back(plan, r, s, c, k):
    d = plan.width
    arrive = c.start(r["dckv"], s["rkv"])
    weight = c.start(r["wcqkv"], s["wcqkv"])
    arrive.wait()
    weight.wait()
    s["rdr"][...] = dot_nt(s["rkv"][...], s["wcqkv"][:, d:])
    c.start(s["rdr"], r["input_grads"]).wait()


def slot_of(relative):
    return ((relative >> 1) & 1) * 4 + ((relative >> 2) & 1) * 2 + ((relative >> 3) & 1)


def weight_grads(plan, r, s, c, lefts, rights, left_of, tall, name, fix=None):
    d, total = plan.width, plan.total

    def blocks(buffer, names):
        found = []
        for array in names:
            for tile in tiles(r[array].shape[1], d):
                at = len(found) * d
                found.append((r[array].at[:, tile], buffer.at[:, at : at + d]))
        return found

    left_blocks, right_blocks = blocks(s["gl"], lefts), blocks(s["gr"], rights)
    count = max(len(left_blocks), len(right_blocks))
    loads, seen = [], set()
    for t in range(count):
        wanted = [(0, 0 if tall else t), (1, left_of(t))]
        fresh = [key for key in wanted if key not in seen]
        seen.update(fresh)
        loads.append([c.start(*(right_blocks, left_blocks)[side][at]) for side, at in fresh])
    if fix is not None:
        wait_all(loads[0])
        loads[0] = []
        fix()
    mine = r["device"][0]
    block = d // 4 if tall else d // 16
    natural = s["gnat_tall" if tall and plan.halving else "gnat"]
    gout = s["gout_tall" if tall else "gout"] if plan.halving else None
    sems = c.reserve(4)

    def columns(at):
        return pl.ds(pl.multiple_of(at * d, LANES), d)

    def copies_out(t):
        slot = lax.rem(t, 2)
        found = []
        for sent in range(2 if plan.halving else 1):
            ref = r[name + ("_send" if sent else "")]
            if not plan.halving:
                target = ref.at[columns(t), :] if tall else ref.at[:, columns(t)]
                source = natural.at[slot]
            elif tall:
                away = t ^ (mine >> 2)
                target, source = ref.at[:, away & 1, away >> 1], gout.at[slot, sent]
            else:
                target, source = ref.at[:, :, columns(t)], gout.at[slot, sent]
            found.append(pltpu.make_async_copy(source, target, sems(slot * 2 + sent)))
        return found

    def wait_out(t):
        wait_all(copies_out(t))

    def hand_on(t):
        for one in copies_out(t):
            one.start()

    def arrange(slot):
        if tall:
            for relative in range(4):
                gout[slot, relative & 1, relative >> 1] = natural[slot, (mine & 3) ^ relative]
        else:
            for relative in range(16):
                gout[slot, relative & 1, slot_of(relative)] = natural[slot, mine ^ relative]

    behind = 1 if plan.halving else 0

    def step(t, carry):
        for at, found in enumerate(loads):
            if found:
                pl.when(t == at)(lambda found=found: wait_all(found))
        pl.when(t >= 2 + behind)(lambda: wait_out(t - 2 - behind))
        slot = lax.rem(t, 2)
        grad = s["gr"][:, columns(0 if tall else t)]
        low = dot_tn(s["gl"][:, columns(left_of(t))], grad).astype(BF)
        if plan.halving:
            for part in range(d // block):
                natural[slot, part] = low[part * block : (part + 1) * block]
            arrange(1 - slot)
        else:
            natural[slot] = low
        sums = jnp.sum(grad.astype(F32).reshape(total // 8, 8, d), axis=0)
        s["gsums"][:, columns(0 if tall else t)] = sums
        pl.when(t >= behind)(lambda: hand_on(t - behind))
        return carry

    lax.fori_loop(0, count, step, 0)
    if plan.halving:
        wait_out(count - 3)
        arrange((count - 1) % 2)
        hand_on(count - 1)
    breadth = len(right_blocks) * d
    last = c.start(s["gsums"].at[:, :breadth], r[name + "_sums"])
    wait_out(count - 2)
    wait_out(count - 1)
    last.wait()


def run_grads_cross(plan, r, s, c, k):
    weight_grads(
        plan, r, s, c, ("m", "streams", "co"), ("dcq", "dckv", "gaf"),
        lambda t: (t + 1) // 2, False, "cross",
    )


def run_grads_fc2(plan, r, s, c, k):
    last = plan.steps - 1
    arrive = c.start(r["returned"], s["gin"])

    def fix():
        arrive.wait()

        @pl.when(r["section"][0] == 0)
        def _():
            s["dn"][...] = s["gin"][...].astype(F32)
            fill_rows(s["g"], plan.per, plan.slots, r["counts"], last * plan.per, s["dn"])
            s["gr"][last * plan.rows :, : plan.width] = s["g"][...].astype(BF)

    weight_grads(plan, r, s, c, ("a",), ("gbr",), lambda t: t, True, "fc2", fix)


def run_grads_fc1(plan, r, s, c, k):
    weight_grads(plan, r, s, c, ("n2",), ("du",), lambda t: 0 * t, False, "fc1")


def run_grads_more(plan, r, s, c, k):
    run_grads_fc2(plan, r, s, c, k)
    run_grads_fc1(plan, r, s, c, k)


def run_grads_attn(plan, r, s, c, k):
    weight_grads(plan, r, s, c, ("n", "o"), ("dqkv", "gm"), lambda t: t // 3, False, "attn")
    d = plan.width
    first = sum(r[name][...] for name in r if name.startswith("ln_first"))
    second = sum(r[name][...] for name in r if name.startswith("ln_second"))
    norms = jnp.where(r["section"][0] == 0, first, second)
    ratio = plan.hidden // d

    def column(ref, at):
        return jnp.sum(ref[:, at * d : (at + 1) * d], axis=0, keepdims=True)

    rows = [column(s["gsums"], 0), column(s["gsums"], 2), column(s["gsums"], 3)]
    rows += [column(r["fc1_sums"], at) for at in range(ratio)] + [column(r["fc2_sums"], 0)]
    rows += [norms[0:1], norms[2:3], norms[1:2], norms[3:4], norms[4:5]]
    rows += [column(r["cross_sums"], at) for at in (0, 2, 3)] + [norms[5:6]]
    s["small"][...] = jnp.zeros_like(s["small"])
    for at, row in enumerate(rows):
        s["small"][at : at + 1, :] = row
    c.start(s["small"], r["small"]).wait()


RUN = {
    "forward": run_forward,
    "radar": run_radar,
    "merged": run_merged,
    "backward": run_backward,
    "backward_mlp": run_backward_mlp,
    "backward_self": run_backward_self,
    "radar_back": run_radar_back,
    "grads_cross": run_grads_cross,
    "grads_fc2": run_grads_fc2,
    "grads_fc1": run_grads_fc1,
    "grads_attn": run_grads_attn,
    "grads_more": run_grads_more,
}


def phase(plan, fixed, state, weights, first, second, after=()):
    jobs = [job for job in (first, second) if job is not None]
    shared = len(jobs) == 2 and jobs[0][0] == jobs[1][0]
    kinds = [JOBS[job[0]] for job in jobs]
    taken = {}
    for job in jobs:
        taken.update(job[2])
    writes = []
    for kind in kinds:
        writes += [name for name in kind["writes"] if name not in writes]
    reads = []
    for kind in kinds:
        for name in kind["reads"]:
            if name in state and name not in reads and name not in writes:
                reads.append(name)
            elif name in ("streams", "cotangent"):
                taken[name] = fixed[name]
    used = [name for name in WEIGHT_NAMES if any(name in kind["weights"] for kind in kinds)]
    fresh = [name for name in writes if name not in state or name in ("send", "ln")]
    kept = [name for name in writes if name not in fresh]
    small = [name for name in fixed if name not in ("streams", "cotangent")]
    if all(job[0].startswith("grads") for job in jobs):
        small = ["section", "device", "counts"]
    elif not any(job[0] in ("radar", "merged") for job in jobs):
        small = [name for name in small if not name.startswith("cross")]
    every = scratch_shapes(plan)
    need = list(used)
    for kind in kinds:
        need += [name for name in kind["scratch"] if name not in need]

    operands, specs, names = [], [], []
    for name in small:
        operands.append(fixed[name])
        specs.append(SM if name in ("section", "device", "counts", "radar_counts", "slopes") else VM)
        names.append(name)
    for name in used:
        operands.append(weights[name])
        specs.append(ANY)
        names.append(name)
    for name, array in list(taken.items()) + [(name, state[name]) for name in reads]:
        operands.append(array)
        specs.append(VM if name.startswith("ln_") or name.endswith("_sums") else ANY)
        names.append(name)
    operands += after
    specs += [ANY] * len(after)
    names += [None] * len(after)
    alias = {}
    for at, name in enumerate(kept):
        alias[len(operands)] = at
        operands.append(state[name])
        specs.append(ANY)
        names.append(None)
    outs = kept + fresh
    shapes = [jax.ShapeDtypeStruct(*STATE[name](plan)) for name in outs]

    def kernel(*refs):
        r, s = {}, {}
        for name, ref in zip(names, refs):
            if name is not None:
                r[name] = ref
        refs = refs[len(names) :]
        for name, ref in zip(outs, refs):
            r[name] = ref
        refs = refs[len(outs) :]
        for name, ref in zip(need, refs):
            s[name] = ref
        sems = refs[len(need)]
        if shared:
            RUN[first[0]](plan, r, s, Copies(sems), first[1])
            return
        for which, job in ((0, first), (1, second)):
            if job is not None:

                @pl.when(r["section"][0] == which)
                def _():
                    RUN[job[0]](plan, r, s, Copies(sems), job[1])

    results = pl.pallas_call(
        kernel,
        out_shape=shapes,
        in_specs=specs,
        out_specs=[ANY] * len(outs),
        scratch_shapes=[pltpu.VMEM(*every[name]) for name in need] + [pltpu.SemaphoreType.DMA((32,))],
        input_output_aliases=alias,
        compiler_params=pltpu.CompilerParams(vmem_limit_bytes=VMEM_LIMIT),
        cost_estimate=CHEAP,
        name="_".join(job[0] + str(job[1]) for job in jobs),
    )(*operands)
    new = dict(zip(outs, results))
    for name in outs:
        if name not in ("send", "ln"):
            state[name] = new[name]
    return new.get("send"), new.get("ln")


def body(
    streams,
    cotangent,
    counts,
    positions,
    radar_counts,
    radar_positions,
    qkv_weight,
    out_weight,
    fc1_weight,
    fc2_weight,
    attn_bias,
    mlp_bias,
    norm_gains,
    norm_shifts,
    cross_qkv_weight,
    cross_out_weight,
    cross_gain,
    cross_bias,
):
    devices = lax.axis_size("batch")
    section_id = lax.axis_index("section")
    me = lax.axis_index("batch")
    width = cotangent.shape[1]
    hidden = fc1_weight.shape[2]
    halving = devices == 16
    plan = Plan(counts.shape[0], positions.shape[1], width, hidden, halving)
    device = me.astype(jnp.int32).reshape(1)
    section = section_id.astype(jnp.int32).reshape(1)
    head_slopes = [2.0 ** (-8.0 * (head + 1.0) / H) for head in range(H)]
    fixed = {
        "section": section,
        "device": device,
        "counts": counts,
        "radar_counts": radar_counts,
        "slopes": jnp.array(head_slopes, F32),
        "positions": positions,
        "radar_positions": radar_positions,
        "attn_bias": attn_bias,
        "mlp_bias": mlp_bias,
        "gains": norm_gains,
        "shifts": norm_shifts,
        "cross_gain": cross_gain.reshape(1, width),
        "cross_bias": cross_bias.reshape(1, 4 * width),
        "streams": streams[0],
        "cotangent": cotangent,
    }
    weights = dict(
        zip(
            WEIGHT_NAMES,
            (
                qkv_weight[0],
                out_weight[0],
                fc1_weight[0],
                fc2_weight[0],
                cross_qkv_weight,
                cross_out_weight,
            ),
        )
    )
    state = {}
    steps = plan.steps
    arrived = []
    for k in range(steps):
        second = ("radar", 0, {}) if k == min(1, steps - 1) else None
        send, _ = phase(plan, fixed, state, weights, ("forward", k, {}), second)
        arrived.append(lax.ppermute(send, "section", [(0, 1)]))
    returned, first_sums, second_sums = [], [], []
    for k in range(steps):
        send, sums = phase(
            plan, fixed, state, weights, None, ("merged", k, {"received": arrived[k]})
        )
        second_sums.append(sums)
        returned.append(lax.ppermute(send, "section", [(1, 0)]))
        if 0 < k < steps - 1:
            _, sums = phase(
                plan, fixed, state, weights, ("backward", k - 1, {"returned": returned[k - 1]}), None
            )
            first_sums.append(sums)

    route = {bit: [(at, at ^ bit) for at in range(devices)] for bit in (1, 2, 4, 8)} if halving else {}

    def trade(block, bit):
        return lax.ppermute(block, "batch", route[bit])

    def trade_second(block, bit):
        pairs = [(devices + left, devices + right) for left, right in route[bit]]
        return lax.ppermute(block, ("section", "batch"), pairs)

    def scatter(part):
        return lax.psum_scatter(part, "batch", scatter_dimension=0, tiled=True).astype(F32)

    def run(first, second, after=()):
        _, sums = phase(plan, fixed, state, weights, first, second, after=list(after))
        if first is not None and first[0].startswith("backward"):
            first_sums.append(sums)

    def both(job, taken, after=()):
        run((job, 0, taken), (job, 0, taken), after)

    def add_up(parts, low, high):
        return sum(part[low:high].astype(F32) for part in parts)

    def begin(name, exchange, pieces=1):
        kept, sent = state[name], state[name + "_send"]
        kept, sent = (x.reshape(8, -1, x.shape[-1]) for x in (kept, sent))
        come = [exchange(piece, 1) for piece in jnp.split(sent, pieces)]
        return [kept, jnp.concatenate(come) if pieces > 1 else come[0]]

    def step(parts, exchange, bit):
        half = parts[-1].shape[0] // 2
        return parts + [exchange(add_up(parts, half, 2 * half).astype(BF), bit)]

    def total(parts):
        return add_up(parts, 0, 1)[0]

    def taken_sums():
        found = {"ln_first" + str(at): array for at, array in enumerate(first_sums)}
        return found | {"ln_second" + str(at): array for at, array in enumerate(second_sums)}

    def once(*arrays):
        return lax.optimization_barrier(arrays)

    last = steps - 1
    queue = [("backward", k, {"returned": returned[k]}) for k in range(max(last - 1, 0), last)] or [None]
    for job in queue[:-1]:
        run(job, None)
    run(queue[-1], ("grads_cross", 0, {}))
    if halving:
        state["cross_send"], returned[last] = once(state["cross_send"], returned[last])
        cross = step(begin("cross", trade_second), trade_second, 2)
        taken = {"returned": returned[last]}
        run(("grads_fc2", 0, taken), ("grads_more", 0, taken), [cross[1]])
        state["fc2"], state["fc2_send"], cross[-1] = once(
            state["fc2"], state["fc2_send"], cross[-1]
        )
        fc2 = begin("fc2", trade)
        ahead = add_up(fc2, 4, 8).astype(BF)
        cross[-1], ahead = once(cross[-1], ahead)
        fc2.append(trade(ahead, 2))
        cross = step(cross, trade_second, 4)
        run(("backward_mlp", last, taken), None, [cross[-1]])
        run(("grads_fc1", 0, {}), None)
        cross = step(cross, trade_second, 8)
        state["fc1"], state["fc1_send"], fc2[-1] = once(
            state["fc1"], state["fc1_send"], fc2[-1]
        )
        fc1 = begin("fc1", trade)
        fc2 = step(fc2, trade, 4)
        run(("backward_self", last, {}), None, [fc1[-1]])
        fc1 = step(fc1, trade, 2)
        both("grads_attn", taken_sums())
        state["attn"], state["attn_send"], fc1[-1], fc2[-1], cross[-1] = once(
            state["attn"], state["attn_send"], fc1[-1], fc2[-1], cross[-1]
        )
        cross_share = total(cross)
        fc2 = step(fc2, trade, 8)
        attn = begin("attn", trade)
        attn[-1], fc2[-1] = once(attn[-1], fc2[-1])
        grad_fc2 = total(fc2)
        ahead = add_up(attn, 4, 8).astype(BF)
        ahead, fc1[-1] = once(ahead, fc1[-1])
        attn.append(trade(ahead, 2))
        fc1 = step(fc1, trade, 4)
        small, _ = once(state["small"], ahead)
        small = small + trade(small, 1)
        small = small + trade(small, 2)
        run(None, ("radar_back", 0, {}), [small])
        fc1 = step(fc1, trade, 8)
        attn[-1], fc1[-1], state["input_grads"] = once(attn[-1], fc1[-1], state["input_grads"])
        ahead = add_up(attn, 2, 4).astype(BF)
        ahead, fc1[-1], small, cross_share = once(ahead, fc1[-1], small, cross_share)
        attn.append(trade(ahead, 4))
        grad_fc1 = total(fc1)
        small = small + trade(small, 4)
        small = small + trade(small, 8)
        ahead = add_up(attn, 1, 2).astype(BF)
        ahead, small, cross_share = once(ahead, small, cross_share)
        attn.append(trade(ahead, 8))
        grad_attn = total(attn)
    else:
        both("grads_fc2", {"returned": returned[last]})
        run(("backward_mlp", last, {"returned": returned[last]}), None)
        both("grads_fc1", {})
        run(("backward_self", last, {}), None)
        both("grads_attn", taken_sums())
        small = lax.psum(state["small"], "batch")
        run(None, ("radar_back", 0, {}))
        cross_share, grad_fc2, grad_fc1, grad_attn = (
            scatter(state[name]) for name in ("cross", "fc2", "fc1", "attn")
        )
    split = qkv_weight.shape[2]

    is_first = section_id == 0

    def to_both(block):
        return jnp.where(is_first, lax.ppermute(block, "section", [(1, 0)]), block).astype(F32)

    cross_all = to_both(cross_share.astype(BF))
    ratio = hidden // width
    edges = [0, 3, 4 + ratio, 6 + ratio, 8 + ratio, 9 + ratio, 13 + ratio]
    cross_small = to_both(small[edges[4] : edges[6]])
    parts = []
    for low, high in zip(edges, edges[1:]):
        rows = small[low:high] if high <= edges[4] else cross_small[low - edges[4] : high - edges[4]]
        size = (high - low) * width // devices
        parts.append(lax.dynamic_slice(rows.reshape(-1), (me * size,), (size,)))
    return (
        state["layer_out"][None],
        state["input_grads"][None],
        grad_attn[None, :, :split],
        grad_attn[None, :, split:],
        grad_fc1[None],
        grad_fc2[None],
        parts[0][None],
        parts[1][None],
        parts[2][None],
        parts[3][None],
        cross_all[:, :split],
        cross_all[:, split:],
        parts[4],
        parts[5],
    )


def solution(mesh):
    in_specs = (
        P("section", "batch", None),
        P("batch", None),
        P("batch"),
        P("batch", None),
        P("batch"),
        P("batch", None),
        P("section", None, None),
        P("section", None, None),
        P("section", None, None),
        P("section", None, None),
        P("section", None),
        P("section", None),
        P("section", None),
        P("section", None),
        P(),
        P(),
        P(),
        P(),
    )
    out_specs = (
        P("section", "batch", None),
        P("section", "batch", None),
        P("section", "batch", None),
        P("section", "batch", None),
        P("section", "batch", None),
        P("section", "batch", None),
        P("section", "batch"),
        P("section", "batch"),
        P("section", "batch"),
        P("section", "batch"),
        P("batch", None),
        P("batch", None),
        P("batch"),
        P("batch"),
    )
    return jax.shard_map(body, mesh=mesh, in_specs=in_specs, out_specs=out_specs, check_vma=False)
```

time: 2060 us -> 363 us (0.18)
  waiting for transfers between devices: 730 us -> 122 us
  matrix products: 534 us -> 0 us
  other arithmetic: 382 us -> 33.1 us
  local copies, waits for them, and re-layouts: 256 us -> 12.6 us
  Pallas kernels: 0 us -> 158 us
  blocking collectives: 60.2 us -> 0 us
  loops' own time: 39.6 us -> 0 us
    dot_general x259 -> x0, matrix products: 534 us -> none  [the longest x56 190 us: matmul_tn(): lax.dot_general(left_mat, right_mat, (((0,), (0,)), ((), ())), preferred_...]
    reduce_scatter x6 -> x0, waiting for transfers between devices: 532 us -> none  [the longest x1 116 us: body(): lax.psum_scatter(layer_acc[3][None], 'batch', scatter_dimension=1, tiled=...]
    unnamed x15 -> x0, waiting for transfers between devices: 174 us -> none
    pallas_call x0 -> x14, Pallas kernels: none -> 158 us  [phase(): pl.pallas_call(kernel, out_shape=shapes, in_specs=specs, out_specs=[ANY]...]
    ppermute x14 -> x28, waiting for transfers between devices: 0.04 us -> 122 us  [the longest x16 78.6 us: trade(): return lax.ppermute(block, 'batch', route[bit])]
    add x70 -> x6, other arithmetic: 113 us -> 5.85 us  [the longest x2 4.26 us: add_up(): return sum((part[low:high].astype(F32) for part in parts))]
    dynamic_slice x105 -> x4, local copies, waits for them, and re-layouts: 101 us -> 2.5 us  [body(): parts.append(lax.dynamic_slice(rows.reshape(-1), (me * size,), (size,)))]
    reduce_sum x140 -> x0, other arithmetic: 97.4 us -> none  [the longest x21 27.8 us: layer_norm(): centred = values_in - average]
  transfers between devices with their start and end apart: 25 -> 28, of which waited for: 10 -> 19; matrix products, arithmetic and copies ran while one was open for 18% -> 6% of each run, Pallas kernels for 0% -> 44%
where the time goes in v1:
time: 363 us; the launch traced here: 358 us
  Pallas kernels  158 us (44%)
  waiting for transfers between devices  122 us (34%)
  other arithmetic  33.1 us (9%)
  starting transfers between devices  31.3 us (9%)
  local copies, waits for them, and re-layouts  12.6 us (3%)
    pallas_call x14, Pallas kernels, phase(): pl.pallas_call(kernel, out_shape=shapes, in_specs=specs, out_specs=[ANY]...  158 us
    ppermute x16, waiting for transfers between devices, trade(): return lax.ppermute(block, 'batch', route[bit])  78.6 us
    ppermute x4, waiting for transfers between devices, trade_second(): return lax.ppermute(block, ('section', 'batch'), pairs)  29.9 us
    convert_element_type x8, other arithmetic, step(): return parts + [exchange(add_up(parts, half, 2 * half).astype(BF), bit)]  17.4 us
    ppermute x3, waiting for transfers between devices, body(): arrived.append(lax.ppermute(send, 'section', [(0, 1)]))  11.3 us
    ppermute x3, starting transfers between devices, body(): returned.append(lax.ppermute(send, 'section', [(1, 0)]))  8.86 us
    ppermute x4, starting transfers between devices, trade_second(): return lax.ppermute(block, ('section', 'batch'), pairs)  8.61 us
    ppermute x16, starting transfers between devices, trade(): return lax.ppermute(block, 'batch', route[bit])  7.38 us
  transfers between devices with their start and end apart: 28, of which 19 were waited for; matrix products, arithmetic and copies ran while one was open for 6% of the time, Pallas kernels for 44%

profile of v1, /device:TPU:6, one launch (start us, length us, event | category | flops | bytes accessed | tf_op | source)
XLA Modules:
  0.0 358.4 jit_solution(13130821746676011750)
XLA Ops:
  3.7 7.6 %forward1_radar0.1 = (bf16[816,768]{1,0:T(8,128)(2,1)}, bf16[816,768]{1,0:T(8,128)(2,1)}, bf16[816,768]{1,0:T(8,128)(2,1)}, bf16[816,3072]{1,0:T(8,128)(2,1)}, f...) custom-call(s32[1]{0:T(128)} %bitcast.refs_0_, ...), custom_call_target="tpu_custom_call", output_to_operand_aliasing={{0}: (19, {}), {1}: (20, {}), {2}: (21, {}), {3}: (22, {}),... | custom-call | flops 1 | bytes 1 | tf_op jit(solution)/shard_map/forward1_radar0/pallas_call | solution.py:1034
  13.9 11.3 %collective-permute-done.2.refs_19_ = bf16[272,768]{1,0:T(8,128)(2,1)S(1)} collective-permute-done((bf16[272,768]{1,0:T(8,128)(2,1)}, bf16[272,768]{1,0:T(8,128)(2,1)S(1)}, u32[]{:S(2)}, u32[]{:S(2)}) %collective-permute-start.2) | collective-permute-done | bytes 417824 | tf_op jit(solution)/shard_map/ppermute | solution.py:1118
  25.9 29.6 %merged0.1 = (bf16[816,768]{1,0:T(8,128)(2,1)}, bf16[816,768]{1,0:T(8,128)(2,1)}, bf16[816,768]{1,0:T(8,128)(2,1)}, bf16[816,3072]{1,0:T(8,128)(2,1)}, f32[816,7...) custom-call(s32[1]{0:T(128)} %bitcast.refs_0_, ...), custom_call_target="tpu_custom_call", output_to_operand_aliasing={{0}: (22, {}), {1}: (23, {}), {2}: (24, {}), {3}: (25, {}),... | custom-call | flops 1 | bytes 1 | tf_op jit(solution)/shard_map/merged0/pallas_call | solution.py:1034
  55.6 6.2 %collective-permute-start.3 = (bf16[272,768]{1,0:T(8,128)(2,1)}, bf16[272,768]{1,0:T(8,128)(2,1)S(1)}, u32[]{:S(2)}, u32[]{:S(2)}) collective-permute-start(bf16[272,768]{1,0:T(8,128)(2,1)} %get-tuple-element.203), channel_id=1, source_target_pairs={{16,0},{17,1},{18,2},{19,3},{20,4},{21,5},{22,6},{23,7},{24,8},{25... | collective-permute-start | bytes 1253384 | tf_op jit(solution)/shard_map/ppermute | solution.py:1125
  63.9 31.6 %merged1.1 = (bf16[816,768]{1,0:T(8,128)(2,1)}, bf16[816,768]{1,0:T(8,128)(2,1)}, bf16[816,768]{1,0:T(8,128)(2,1)}, bf16[816,3072]{1,0:T(8,128)(2,1)}, f32[816,7...) custom-call(s32[1]{0:T(128)} %bitcast.refs_0_, ...), custom_call_target="tpu_custom_call", output_to_operand_aliasing={{0}: (22, {}), {1}: (23, {}), {2}: (24, {}), {3}: (25, {}),... | custom-call | flops 1 | bytes 1 | tf_op jit(solution)/shard_map/merged1/pallas_call | solution.py:1034
  99.5 31.6 %merged2.1 = (bf16[816,768]{1,0:T(8,128)(2,1)}, bf16[816,768]{1,0:T(8,128)(2,1)}, bf16[816,768]{1,0:T(8,128)(2,1)}, bf16[816,3072]{1,0:T(8,128)(2,1)}, f32[816,7...) custom-call(s32[1]{0:T(128)} %bitcast.refs_0_, ...), custom_call_target="tpu_custom_call", output_to_operand_aliasing={{0}: (22, {}), {1}: (23, {}), {2}: (24, {}), {3}: (25, {}),... | custom-call | flops 1 | bytes 1 | tf_op jit(solution)/shard_map/merged2/pallas_call | solution.py:1034
  133.3 10.5 %backward1_grads_cross0.1 = (bf16[816,768]{1,0:T(8,128)(2,1)}, bf16[816,3072]{1,0:T(8,128)(2,1)}, bf16[816,768]{1,0:T(8,128)(2,1)}, bf16[816,2304]{1,0:T(8,128)(...) custom-call(s32[1]{0:T(128)} %bitcast.refs_0_, ...), custom_call_target="tpu_custom_call", output_to_operand_aliasing={{0}: (26, {}), {1}: (27, {}), {2}: (28, {}), {3}: (29, {}),... | custom-call | flops 1 | bytes 1 | tf_op jit(solution)/shard_map/backward1_grads_cross0/pallas_call | solution.py:1034
  145.7 4.7 %collective-permute-done.6.refs_8_ = bf16[8,48,3072]{2,1,0:T(8,128)(2,1)S(1)} collective-permute-done((bf16[8,48,3072]{2,1,0:T(8,128)(2,1)}, bf16[8,48,3072]{2,1,0:T(8,128)(2,1)S(1)}, u32[]{:S(2)}, u32[]{:S(2)}) %collective-permute-start.6) | collective-permute-done | bytes 2359328 | tf_op jit(solution)/shard_map/ppermute | solution.py:1139
  150.4 3.6 %add_convert_fusion.2 = bf16[4,48,3072]{2,1,0:T(8,128)(2,1)} fusion(bf16[8,48,3072]{2,1,0:T(8,128)(2,1)S(1)} %collective-permute-done.6.refs_8_, bf16[8,48,3072]{2,1,0:T(8,128)(2,1)} %get-tuple-element.238), kind=kLoop, calls=%fused_computation.4 | loop fusion | flops 2359296 | bytes 3538944 | tf_op jit(solution)/shard_map/convert_element_type | solution.py:1163
  156.0 20.7 %grads_fc20_grads_more0.1 = (bf16[2,2,2,192,768]{4,3,2,1,0:T(8,128)(2,1)}, bf16[2,2,2,192,768]{4,3,2,1,0:T(8,128)(2,1)}, f32[8,768]{1,0:T(8,128)}, bf16[8,48,307...) custom-call(s32[1]{0:T(128)} %bitcast.refs_0_, s32[1]{0:T(128)} %bitcast.1.refs_1_, s32[6]{0:T(128)} %refs_2_.27, ...), custom_call_target="tpu_custom_call" | custom-call | flops 1 | bytes 1 | tf_op jit(solution)/shard_map/grads_fc20_grads_more0/pallas_call | solution.py:1034
  176.7 7.6 %collective-permute-done.7 = bf16[4,48,3072]{2,1,0:T(8,128)(2,1)} collective-permute-done((bf16[4,48,3072]{2,1,0:T(8,128)(2,1)}, bf16[4,48,3072]{2,1,0:T(8,128)(2,1)}, u32[]{:S(2)}, u32[]{:S(2)}) %collective-permute-start.7) | collective-permute-done | bytes 1179680 | tf_op jit(solution)/shard_map/ppermute | solution.py:1139
  185.6 3.4 collective-permute-done.8
  193.4 15.4 %collective-permute-done.9.refs_16_ = bf16[2,48,3072]{2,1,0:T(8,128)(2,1)S(1)} collective-permute-done((bf16[2,48,3072]{2,1,0:T(8,128)(2,1)S(1)}, bf16[2,48,3072]{2,1,0:T(8,128)(2,1)S(1)}, u32[]{:S(2)}, u32[]{:S(2)}) %collective-permute-start.9) | collective-permute-done | bytes 589856 | tf_op jit(solution)/shard_map/ppermute | solution.py:1139
  211.7 5.9 %collective-permute-done.10 = bf16[4,192,768]{2,1,0:T(8,128)(2,1)} collective-permute-done((bf16[4,192,768]{2,1,0:T(8,128)(2,1)S(1)}, bf16[4,192,768]{2,1,0:T(8,128)(2,1)}, u32[]{:S(2)}, u32[]{:S(2)}) %collective-permute-start.10) | collective-permute-done | bytes 1179680 | tf_op jit(solution)/shard_map/ppermute | solution.py:1135
  217.6 4.7 %collective-permute-done.11.refs_17_ = bf16[8,48,3072]{2,1,0:T(8,128)(2,1)S(1)} collective-permute-done((bf16[8,48,3072]{2,1,0:T(8,128)(2,1)}, bf16[8,48,3072]{2,1,0:T(8,128)(2,1)S(1)}, u32[]{:S(2)}, u32[]{:S(2)}) %collective-permute-start.11) | collective-permute-done | bytes 2359328 | tf_op jit(solution)/shard_map/ppermute | solution.py:1135
  233.0 11.7 %grads_attn0_grads_attn0.1 = (bf16[8,48,3072]{2,1,0:T(8,128)(2,1)}, bf16[8,48,3072]{2,1,0:T(8,128)(2,1)}, f32[8,3072]{1,0:T(8,128)}, f32[24,768]{1,0:T(8,128)}) custom-call(s32[1]{0:T(128)} %bitcast.refs_0_, s32[1]{0:T(128)} %bitcast.1.refs_1_, s32[6]{0:T(128)} %refs_2_.27, f32[8,768]{1,0:T(8,128)} %get-tuple-element.222.refs_3_, ...), custom_call_target="tpu_custom_call" | custom-call | flops 1 | bytes 1 | tf_op jit(solution)/shard_map/grads_attn0_grads_attn0/pallas_call | solution.py:1034
  249.1 3.9 %collective-permute-done.12 = bf16[4,48,3072]{2,1,0:T(8,128)(2,1)} collective-permute-done((bf16[4,48,3072]{2,1,0:T(8,128)(2,1)S(1)}, bf16[4,48,3072]{2,1,0:T(8,128)(2,1)}, u32[]{:S(2)}, u32[]{:S(2)}) %collective-permute-start.12) | collective-permute-done | bytes 1179680 | tf_op jit(solution)/shard_map/ppermute | solution.py:1135
  254.7 15.4 %collective-permute-done.16 = bf16[1,192,768]{2,1,0:T(8,128)(2,1)} collective-permute-done((bf16[1,192,768]{2,1,0:T(8,128)(2,1)S(1)}, bf16[1,192,768]{2,1,0:T(8,128)(2,1)}, u32[]{:S(2)}, u32[]{:S(2)}) %collective-permute-start.16) | collective-permute-done | bytes 294944 | tf_op jit(solution)/shard_map/ppermute | solution.py:1135
  270.1 3.6 add_convert_fusion
  279.1 12.4 %collective-permute-done.18 = bf16[2,48,3072]{2,1,0:T(8,128)(2,1)S(1)} collective-permute-done((bf16[2,48,3072]{2,1,0:T(8,128)(2,1)}, bf16[2,48,3072]{2,1,0:T(8,128)(2,1)S(1)}, u32[]{:S(2)}, u32[]{:S(2)}) %collective-permute-start.18) | collective-permute-done | bytes 589856 | tf_op jit(solution)/shard_map/ppermute | solution.py:1135
  295.0 11.1 %collective-permute-done.21 = f32[24,768]{1,0:T(8,128)S(1)} collective-permute-done((f32[24,768]{1,0:T(8,128)S(1)}, f32[24,768]{1,0:T(8,128)S(1)}, u32[]{:S(2)}, u32[]{:S(2)}) %collective-permute-start.21) | collective-permute-done | bytes 73760 | tf_op jit(solution)/shard_map/ppermute | solution.py:1135
  306.8 7.5 %radar_back0.1 = f32[816,768]{1,0:T(8,128)} custom-call(s32[1]{0:T(128)} %bitcast.refs_0_, s32[1]{0:T(128)} %bitcast.1.refs_1_, s32[6]{0:T(128)} %refs_2_.27, s32[6]{0:T(128)} %refs_3_.21, f32[12]{0:T(128)} %constant.34.clone.refs_4_, s32[6,136]{1,0:T(8,128)} %refs_5_.21, s32[6,136]{1,0:T(8,128)} %refs_6_.21, ...), custom_call_target="tpu_custom_call", output_to_operand_aliasing={{}: (14, {})} | custom-call | flops 1 | bytes 1 | tf_op jit(solution)/shard_map/radar_back0/pallas_call | solution.py:1034
  324.7 9.7 %collective-permute-done.24 = f32[24,768]{1,0:T(8,128)S(1)} collective-permute-done((f32[24,768]{1,0:T(8,128)S(1)}, f32[24,768]{1,0:T(8,128)S(1)}, u32[]{:S(2)}, u32[]{:S(2)}) %collective-permute-start.24) | collective-permute-done | bytes 73760 | tf_op jit(solution)/shard_map/ppermute | solution.py:1135
  349.0 6.4 %collective-permute-done.25 = bf16[1,48,3072]{2,1,0:T(8,128)(2,1)S(1)} collective-permute-done((bf16[1,48,3072]{2,1,0:T(8,128)(2,1)S(1)}, bf16[1,48,3072]{2,1,0:T(8,128)(2,1)S(1)}, u32[]{:S(2)}, u32[]{:S(2)}) %collective-permute-start.25) | collective-permute-done | bytes 294944 | tf_op jit(solution)/shard_map/ppermute | solution.py:1135
  (135 shorter events, 80.9 us)
Async XLA Ops:
  1.8 23.4 %collective-permute-start.2 = (bf16[272,768]{1,0:T(8,128)(2,1)}, bf16[272,768]{1,0:T(8,128)(2,1)S(1)}, u32[]{:S(2)}, u32[]{:S(2)}) collective-permute-start(bf16[272,768]{1,0:T(8,128)(2,1)} %get-tuple-element.178), channel_id=1, source_target_pairs={{0,16},{1,17},{2,18},{3,19},{4,20},{5,21},{6,22},{7,23},{8,24},{9,... | collective-permute-start | bytes 1253384 | tf_op jit(solution)/shard_map/ppermute | solution.py:1118
  11.3 51.9 %collective-permute-start.1 = (bf16[272,768]{1,0:T(8,128)(2,1)}, bf16[272,768]{1,0:T(8,128)(2,1)S(1)}, u32[]{:S(2)}, u32[]{:S(2)}) collective-permute-start(bf16[272,768]{1,0:T(8,128)(2,1)} %get-tuple-element.177), channel_id=1, source_target_pairs={{0,16},{1,17},{2,18},{3,19},{4,20},{5,21},{6,22},{7,23},{8,24},{9,... | collective-permute-start | bytes 1253384 | tf_op jit(solution)/shard_map/ppermute | solution.py:1118
  55.6 41.3 %collective-permute-start.3 = (bf16[272,768]{1,0:T(8,128)(2,1)}, bf16[272,768]{1,0:T(8,128)(2,1)S(1)}, u32[]{:S(2)}, u32[]{:S(2)}) collective-permute-start(bf16[272,768]{1,0:T(8,128)(2,1)} %get-tuple-element.203), channel_id=1, source_target_pairs={{16,0},{17,1},{18,2},{19,3},{20,4},{21,5},{22,6},{23,7},{24,8},{25... | collective-permute-start | bytes 1253384 | tf_op jit(solution)/shard_map/ppermute | solution.py:1125
  61.8 36.9 %collective-permute-start = (bf16[272,768]{1,0:T(8,128)(2,1)S(1)}, bf16[272,768]{1,0:T(8,128)(2,1)S(1)}, u32[]{:S(2)}, u32[]{:S(2)}) collective-permute-start(bf16[272,768]{1,0:T(8,128)(2,1)S(1)} %copy-done.22), channel_id=1, source_target_pairs={{0,16},{1,17},{2,18},{3,19},{4,20},{5,21},{6,22},{7,23},{8,24},{9,... | collective-permute-start | bytes 1253384 | tf_op jit(solution)/shard_map/ppermute | solution.py:1118
  95.5 37.0 %collective-permute-start.4 = (bf16[272,768]{1,0:T(8,128)(2,1)}, bf16[272,768]{1,0:T(8,128)(2,1)S(1)}, u32[]{:S(2)}, u32[]{:S(2)}) collective-permute-start(bf16[272,768]{1,0:T(8,128)(2,1)} %get-tuple-element.223), channel_id=1, source_target_pairs={{16,0},{17,1},{18,2},{19,3},{20,4},{21,5},{22,6},{23,7},{24,8},{25... | collective-permute-start | bytes 1253384 | tf_op jit(solution)/shard_map/ppermute | solution.py:1125
  131.2 12.6 %collective-permute-start.5 = (bf16[272,768]{1,0:T(8,128)(2,1)}, bf16[272,768]{1,0:T(8,128)(2,1)S(1)}, u32[]{:S(2)}, u32[]{:S(2)}) collective-permute-start(bf16[272,768]{1,0:T(8,128)(2,1)} %get-tuple-element.236), channel_id=1, source_target_pairs={{16,0},{17,1},{18,2},{19,3},{20,4},{21,5},{22,6},{23,7},{24,8},{25... | collective-permute-start | bytes 1253384 | tf_op jit(solution)/shard_map/ppermute | solution.py:1125
  143.8 6.6 %collective-permute-start.6 = (bf16[8,48,3072]{2,1,0:T(8,128)(2,1)}, bf16[8,48,3072]{2,1,0:T(8,128)(2,1)S(1)}, u32[]{:S(2)}, u32[]{:S(2)}) collective-permute-start(bf16[8,48,3072]{2,1,0:T(8,128)(2,1)} %get-tuple-element.239), channel_id=1, source_target_pairs={{16,17},{17,16},{18,19},{19,18},{20,21},{21,20},{22,23},{23,22},{2... | collective-permute-start | bytes 7077896 | tf_op jit(solution)/shard_map/ppermute | solution.py:1139
  154.1 30.2 %collective-permute-start.7 = (bf16[4,48,3072]{2,1,0:T(8,128)(2,1)}, bf16[4,48,3072]{2,1,0:T(8,128)(2,1)}, u32[]{:S(2)}, u32[]{:S(2)}) collective-permute-start(bf16[4,48,3072]{2,1,0:T(8,128)(2,1)} %add_convert_fusion.2), channel_id=1, source_target_pairs={{16,18},{17,19},{18,16},{19,17},{20,22},{21,23},{22,20},{23,21},{2... | collective-permute-start | bytes 3538952 | tf_op jit(solution)/shard_map/ppermute | solution.py:1139
  189.4 28.2 %collective-permute-start.10 = (bf16[4,192,768]{2,1,0:T(8,128)(2,1)S(1)}, bf16[4,192,768]{2,1,0:T(8,128)(2,1)}, u32[]{:S(2)}, u32[]{:S(2)}) collective-permute-start(bf16[4,192,768]{2,1,0:T(8,128)(2,1)S(1)} %fusion), channel_id=1, source_target_pairs={{0,2},{1,3},{2,0},{3,1},{4,6},{5,7},{6,4},{7,5},{8,10},{9,11},{10,... | collective-permute-start | bytes 3538952 | tf_op jit(solution)/shard_map/ppermute | solution.py:1135
  191.5 17.3 %collective-permute-start.9 = (bf16[2,48,3072]{2,1,0:T(8,128)(2,1)S(1)}, bf16[2,48,3072]{2,1,0:T(8,128)(2,1)S(1)}, u32[]{:S(2)}, u32[]{:S(2)}) collective-permute-start(bf16[2,48,3072]{2,1,0:T(8,128)(2,1)S(1)} %add_convert_fusion.6), channel_id=1, source_target_pairs={{16,20},{17,21},{18,22},{19,23},{20,16},{21,17},{22,18},{23,19},{2... | collective-permute-start | bytes 1769480 | tf_op jit(solution)/shard_map/ppermute | solution.py:1139
  224.8 28.2 %collective-permute-start.12 = (bf16[4,48,3072]{2,1,0:T(8,128)(2,1)S(1)}, bf16[4,48,3072]{2,1,0:T(8,128)(2,1)}, u32[]{:S(2)}, u32[]{:S(2)}) collective-permute-start(bf16[4,48,3072]{2,1,0:T(8,128)(2,1)S(1)} %add_convert_fusion.1), channel_id=1, source_target_pairs={{0,2},{1,3},{2,0},{3,1},{4,6},{5,7},{6,4},{7,5},{8,10},{9,11},{10,... | collective-permute-start | bytes 3538952 | tf_op jit(solution)/shard_map/ppermute | solution.py:1135
  227.5 21.6 %collective-permute-start.13 = (bf16[2,192,768]{2,1,0:T(8,128)(2,1)}, bf16[2,192,768]{2,1,0:T(8,128)(2,1)S(1)}, u32[]{:S(2)}, u32[]{:S(2)}) collective-permute-start(bf16[2,192,768]{2,1,0:T(8,128)(2,1)} %add_convert_fusion.5), channel_id=1, source_target_pairs={{0,4},{1,5},{2,6},{3,7},{4,0},{5,1},{6,2},{7,3},{8,12},{9,13},{10,... | collective-permute-start | bytes 1769480 | tf_op jit(solution)/shard_map/ppermute | solution.py:1135
  228.8 18.1 %collective-permute-start.14 = (bf16[1,48,3072]{2,1,0:T(8,128)(2,1)S(1)}, bf16[1,48,3072]{2,1,0:T(8,128)(2,1)S(1)}, u32[]{:S(2)}, u32[]{:S(2)}) collective-permute-start(bf16[1,48,3072]{2,1,0:T(8,128)(2,1)S(1)} %add_convert_fusion.10), channel_id=1, source_target_pairs={{16,24},{17,25},{18,26},{19,27},{20,28},{21,29},{22,30},{23,31},{2... | collective-permute-start | bytes 884744 | tf_op jit(solution)/shard_map/ppermute | solution.py:1139
  253.0 17.1 %collective-permute-start.15 = (bf16[8,48,3072]{2,1,0:T(8,128)(2,1)}, bf16[8,48,3072]{2,1,0:T(8,128)(2,1)S(1)}, u32[]{:S(2)}, u32[]{:S(2)}) collective-permute-start(bf16[8,48,3072]{2,1,0:T(8,128)(2,1)} %get-tuple-element.279), channel_id=1, source_target_pairs={{0,1},{1,0},{2,3},{3,2},{4,5},{5,4},{6,7},{7,6},{8,9},{9,8},{10,11... | collective-permute-start | bytes 7077896 | tf_op jit(solution)/shard_map/ppermute | solution.py:1135
  254.6 15.5 %collective-permute-start.16 = (bf16[1,192,768]{2,1,0:T(8,128)(2,1)S(1)}, bf16[1,192,768]{2,1,0:T(8,128)(2,1)}, u32[]{:S(2)}, u32[]{:S(2)}) collective-permute-start(bf16[1,192,768]{2,1,0:T(8,128)(2,1)S(1)} %add_convert_fusion.9), channel_id=1, source_target_pairs={{0,8},{1,9},{2,10},{3,11},{4,12},{5,13},{6,14},{7,15},{8,0},{9,1},... | collective-permute-start | bytes 884744 | tf_op jit(solution)/shard_map/ppermute | solution.py:1135
  276.0 15.5 %collective-permute-start.18 = (bf16[2,48,3072]{2,1,0:T(8,128)(2,1)}, bf16[2,48,3072]{2,1,0:T(8,128)(2,1)S(1)}, u32[]{:S(2)}, u32[]{:S(2)}) collective-permute-start(bf16[2,48,3072]{2,1,0:T(8,128)(2,1)} %add_convert_fusion.4), channel_id=1, source_target_pairs={{0,4},{1,5},{2,6},{3,7},{4,0},{5,1},{6,2},{7,3},{8,12},{9,13},{10,... | collective-permute-start | bytes 1769480 | tf_op jit(solution)/shard_map/ppermute | solution.py:1135
  276.0 38.3 %collective-permute-start.17 = (bf16[4,48,3072]{2,1,0:T(8,128)(2,1)}, bf16[4,48,3072]{2,1,0:T(8,128)(2,1)}, u32[]{:S(2)}, u32[]{:S(2)}) collective-permute-start(bf16[4,48,3072]{2,1,0:T(8,128)(2,1)} %add_convert_fusion), channel_id=1, source_target_pairs={{0,2},{1,3},{2,0},{3,1},{4,6},{5,7},{6,4},{7,5},{8,10},{9,11},{10,... | collective-permute-start | bytes 3538952 | tf_op jit(solution)/shard_map/ppermute | solution.py:1135
  278.5 27.6 %collective-permute-start.21 = (f32[24,768]{1,0:T(8,128)S(1)}, f32[24,768]{1,0:T(8,128)S(1)}, u32[]{:S(2)}, u32[]{:S(2)}) collective-permute-start(f32[24,768]{1,0:T(8,128)S(1)} %add.167), channel_id=1, source_target_pairs={{0,2},{1,3},{2,0},{3,1},{4,6},{5,7},{6,4},{7,5},{8,10},{9,11},{10,... | collective-permute-start | bytes 221192 | tf_op jit(solution)/shard_map/ppermute | solution.py:1135
  293.6 20.7 %collective-permute-start.19 = (bf16[1,48,3072]{2,1,0:T(8,128)(2,1)}, bf16[1,48,3072]{2,1,0:T(8,128)(2,1)S(1)}, u32[]{:S(2)}, u32[]{:S(2)}) collective-permute-start(bf16[1,48,3072]{2,1,0:T(8,128)(2,1)} %add_convert_fusion.8), channel_id=1, source_target_pairs={{0,8},{1,9},{2,10},{3,11},{4,12},{5,13},{6,14},{7,15},{8,0},{9,1},... | collective-permute-start | bytes 884744 | tf_op jit(solution)/shard_map/ppermute | solution.py:1135
  320.4 16.3 %collective-permute-start.22 = (bf16[2,48,3072]{2,1,0:T(8,128)(2,1)S(1)}, bf16[2,48,3072]{2,1,0:T(8,128)(2,1)S(1)}, u32[]{:S(2)}, u32[]{:S(2)}) collective-permute-start(bf16[2,48,3072]{2,1,0:T(8,128)(2,1)S(1)} %add_convert_fusion.3), channel_id=1, source_target_pairs={{0,4},{1,5},{2,6},{3,7},{4,0},{5,1},{6,2},{7,3},{8,12},{9,13},{10,... | collective-permute-start | bytes 1769480 | tf_op jit(solution)/shard_map/ppermute | solution.py:1135
  320.5 13.9 %collective-permute-start.24 = (f32[24,768]{1,0:T(8,128)S(1)}, f32[24,768]{1,0:T(8,128)S(1)}, u32[]{:S(2)}, u32[]{:S(2)}) collective-permute-start(f32[24,768]{1,0:T(8,128)S(1)} %add.181), channel_id=1, source_target_pairs={{0,8},{1,9},{2,10},{3,11},{4,12},{5,13},{6,14},{7,15},{8,0},{9,1},... | collective-permute-start | bytes 221192 | tf_op jit(solution)/shard_map/ppermute | solution.py:1135
  338.1 9.4 %collective-permute-start.26 = (bf16[48,3072]{1,0:T(8,128)(2,1)S(1)}, bf16[48,3072]{1,0:T(8,128)(2,1)S(1)}, u32[]{:S(2)}, u32[]{:S(2)}) collective-permute-start(bf16[48,3072]{1,0:T(8,128)(2,1)S(1)} %add_bitcast_fusion.1), channel_id=1, source_target_pairs={{16,0},{17,1},{18,2},{19,3},{20,4},{21,5},{22,6},{23,7},{24,8},{25... | collective-permute-start | bytes 884744 | tf_op jit(solution)/shard_map/ppermute | solution.py:1248
  339.5 6.1 %collective-permute-start.27 = (f32[5,768]{1,0:T(8,128)S(1)}, f32[5,768]{1,0:T(8,128)S(1)}, u32[]{:S(2)}, u32[]{:S(2)}) collective-permute-start(f32[5,768]{1,0:T(8,128)S(1)} %slice.250), channel_id=1, source_target_pairs={{16,0},{17,1},{18,2},{19,3},{20,4},{21,5},{22,6},{23,7},{24,8},{25... | collective-permute-start | bytes 46088 | tf_op jit(solution)/shard_map/ppermute | solution.py:1248
  340.8 14.6 %collective-permute-start.25 = (bf16[1,48,3072]{2,1,0:T(8,128)(2,1)S(1)}, bf16[1,48,3072]{2,1,0:T(8,128)(2,1)S(1)}, u32[]{:S(2)}, u32[]{:S(2)}) collective-permute-start(bf16[1,48,3072]{2,1,0:T(8,128)(2,1)S(1)} %add_convert_fusion.7), channel_id=1, source_target_pairs={{0,8},{1,9},{2,10},{3,11},{4,12},{5,13},{6,14},{7,15},{8,0},{9,1},... | collective-permute-start | bytes 884744 | tf_op jit(solution)/shard_map/ppermute | solution.py:1135
  (27 other events, 206.4 us)

commit v2 on v1

v2 whole, which is shorter than its diff:
```python
import enum
import typing

import jax
import jax.numpy as jnp
from jax import lax
from jax.experimental import pallas as pl
from jax.experimental.pallas import tpu as pltpu
from jax.sharding import PartitionSpec as P

SECTION, BATCH = "section", "batch"
H = 12
HD = 64
PAIRS = H // 2
LANES = 2 * HD
GRID = 15
SCORE_SCALE = 0.125
NORM_EPS = 1e-06
FAR = 1e33
CHUNK = 16
BF = jnp.bfloat16
F32 = jnp.float32
VMEM_LIMIT = 60 << 20
CHEAP = pl.CostEstimate(flops=1, bytes_accessed=1, transcendentals=0)
ANY = pl.BlockSpec(memory_space=pl.ANY)
VM = pl.BlockSpec(memory_space=pltpu.VMEM)
SM = pl.BlockSpec(memory_space=pltpu.SMEM)


class K(enum.Enum):
    a = enum.auto()
    attn = enum.auto()
    attn_bias = enum.auto()
    attn_send = enum.auto()
    attn_sums = enum.auto()
    backward = enum.auto()
    backward_mlp = enum.auto()
    backward_self = enum.auto()
    between = enum.auto()
    cdist = enum.auto()
    cgo = enum.auto()
    cheard = enum.auto()
    ckv = enum.auto()
    ckvb = enum.auto()
    co = enum.auto()
    cotangent = enum.auto()
    counts = enum.auto()
    cp = enum.auto()
    cq = enum.auto()
    cross = enum.auto()
    cross_bias = enum.auto()
    cross_gain = enum.auto()
    cross_send = enum.auto()
    cross_sums = enum.auto()
    dckv = enum.auto()
    dcq = enum.auto()
    dcqkv = enum.auto()
    device = enum.auto()
    dh = enum.auto()
    dist = enum.auto()
    dm = enum.auto()
    dmid = enum.auto()
    dn = enum.auto()
    dqkv = enum.auto()
    dqkvb = enum.auto()
    du = enum.auto()
    dx = enum.auto()
    dxb = enum.auto()
    fc1 = enum.auto()
    fc1_send = enum.auto()
    fc1_sums = enum.auto()
    fc2 = enum.auto()
    fc2_send = enum.auto()
    fc2_sums = enum.auto()
    forward = enum.auto()
    g = enum.auto()
    gaf = enum.auto()
    gains = enum.auto()
    gbr = enum.auto()
    gin = enum.auto()
    gl = enum.auto()
    gm = enum.auto()
    gnat = enum.auto()
    gnat_tall = enum.auto()
    go = enum.auto()
    gout = enum.auto()
    gout_tall = enum.auto()
    gp = enum.auto()
    gr = enum.auto()
    grads_attn = enum.auto()
    grads_cross = enum.auto()
    grads_fc1 = enum.auto()
    grads_fc2 = enum.auto()
    grads_more = enum.auto()
    gsums = enum.auto()
    h = enum.auto()
    h2 = enum.auto()
    heard = enum.auto()
    input_grads = enum.auto()
    layer_out = enum.auto()
    ln = enum.auto()
    m = enum.auto()
    merged = enum.auto()
    mlp_bias = enum.auto()
    n = enum.auto()
    n2 = enum.auto()
    o = enum.auto()
    p = enum.auto()
    positions = enum.auto()
    qkv = enum.auto()
    radar = enum.auto()
    radar_back = enum.auto()
    radar_counts = enum.auto()
    radar_positions = enum.auto()
    rb = enum.auto()
    rdr = enum.auto()
    received = enum.auto()
    returned = enum.auto()
    rkv = enum.auto()
    section = enum.auto()
    send = enum.auto()
    shifts = enum.auto()
    slopes = enum.auto()
    small = enum.auto()
    streams = enum.auto()
    u = enum.auto()
    wcout = enum.auto()
    wcqkv = enum.auto()
    wfc1 = enum.auto()
    wfc2 = enum.auto()
    wout = enum.auto()
    wqkv = enum.auto()
    x = enum.auto()
    xb = enum.auto()
    y = enum.auto()
    yout = enum.auto()
    ysend = enum.auto()


SENT = {K.cross: K.cross_send, K.fc2: K.fc2_send, K.fc1: K.fc1_send, K.attn: K.attn_send}
SUMS = {K.cross: K.cross_sums, K.fc2: K.fc2_sums, K.fc1: K.fc1_sums, K.attn: K.attn_sums}
FIRST = [(K.ln, 0, at) for at in range(64)]
SECOND = [(K.ln, 1, at) for at in range(64)]
IN_VMEM = FIRST + SECOND + list(SUMS.values())
GRAD_JOBS = (K.grads_cross, K.grads_fc2, K.grads_fc1, K.grads_attn, K.grads_more)
BACK_JOBS = (K.backward, K.backward_mlp, K.backward_self)


class Job(typing.NamedTuple):
    reads: tuple
    writes: tuple
    weights: tuple
    scratch: tuple


def dot_nn(left, right):
    return jnp.dot(left, right, preferred_element_type=F32)


def dot_tn(left, right):
    return lax.dot_general(left, right, (((0,), (0,)), ((), ())), preferred_element_type=F32)


def dot_nt(left, right):
    return lax.dot_general(left, right, (((1,), (1,)), ((), ())), preferred_element_type=F32)


class Copies:
    def __init__(self, sems):
        self.sems = sems
        self.used = 0

    def start(self, source, target):
        copy = pltpu.make_async_copy(source, target, self.sems.at[self.used])
        self.used += 1
        copy.start()
        return copy

    def reserve(self, count):
        first = self.used
        self.used += count
        return lambda at: self.sems.at[first + at]


def spans(rows):
    return [slice(at, at + CHUNK) for at in range(0, rows, CHUNK)]


def norm_parts(values):
    average = jnp.mean(values, axis=-1, keepdims=True)
    centred = values - average
    spread = jnp.mean(centred * centred, axis=-1, keepdims=True)
    scale = lax.rsqrt(spread + NORM_EPS)
    return centred * scale, scale


def norm_forward(source, gain, shift, target):
    for span in spans(source.shape[0]):
        unit, _ = norm_parts(source[span, :])
        target[span, :] = (unit * gain + shift).astype(BF)


def norm_backward(source, gain, upstream, residual, target):
    gain_sum = jnp.zeros((8, source.shape[1]), F32)
    shift_sum = jnp.zeros((8, source.shape[1]), F32)
    for span in spans(source.shape[0]):
        unit, scale = norm_parts(source[span, :])
        grad = upstream[span, :]
        product = grad * unit
        gain_sum = gain_sum + product[:8] + product[8:]
        shift_sum = shift_sum + grad[:8] + grad[8:]
        inner = grad * gain
        mean_one = jnp.mean(inner, axis=-1, keepdims=True)
        mean_two = jnp.mean(inner * unit, axis=-1, keepdims=True)
        target[span, :] = residual[span, :] + scale * (inner - mean_one - unit * mean_two)
    return (
        jnp.sum(gain_sum, axis=0, keepdims=True),
        jnp.sum(shift_sum, axis=0, keepdims=True),
    )


def gelu_both(values):
    cdf = 0.5 + 0.5 * lax.erf(values * 0.7071067811865476)
    density = 0.3989422804014327 * jnp.exp(-0.5 * values * values)
    return values * cdf, cdf + values * density


def place(positions):
    values = positions
    row = jnp.floor((values + 0.5) * (1.0 / GRID))
    return row, values - GRID * row


def distances(key_col, query_row, live_keys):
    row_q, col_q = place(query_row)
    row_k, col_k = place(key_col)
    gap_row = row_q - row_k
    gap_col = col_q - col_k
    distance = jnp.sqrt(gap_row * gap_row + gap_col * gap_col)
    slot = lax.broadcasted_iota(jnp.int32, distance.shape, 0)
    return jnp.where(slot < live_keys, distance, FAR)


def both_heads(pair):
    first = lax.broadcasted_iota(jnp.int32, pair.shape, 1) < HD
    zero = jnp.zeros_like(pair)
    return jnp.concatenate([jnp.where(first, pair, zero), jnp.where(first, zero, pair)], axis=0)


def one_pair(stacked):
    half = stacked.shape[0] // 2
    first = lax.broadcasted_iota(jnp.int32, (half, LANES), 1) < HD
    return jnp.where(first, stacked[:half], stacked[half:])


def by_size(plan, most_live, work):
    def step(image, carry):
        if plan.slots <= LANES:
            work(image, plan.slots)
        else:
            live = most_live(image)

            @pl.when(live <= LANES)
            def _():
                work(image, LANES)

            @pl.when(live > LANES)
            def _():
                work(image, plan.slots)

        return carry

    lax.fori_loop(0, plan.per, step, 0)


def rows_of(plan, image, first, size):
    return pl.ds(pl.multiple_of(image * plan.slots + first, 8), size)


def pair_lanes(base, pair):
    if isinstance(pair, int):
        return pl.ds(base + pair * LANES, LANES)
    return pl.ds(pl.multiple_of(base + pair * LANES, LANES), LANES)


def over_pairs(plan, work, size):
    unroll = PAIRS if size <= LANES else plan.unroll

    def step(at, carry):
        for part in range(unroll):
            work(at * unroll + part)
        return carry

    if unroll == PAIRS:
        step(0, 0)
    else:
        lax.fori_loop(0, PAIRS // unroll, step, 0)


def attend(plan, most_live, query, keys, values, spread, slopes, heard, weights):
    def work(image, size):
        rows = rows_of(plan, image, 0, size)
        if size < plan.slots:
            rest = rows_of(plan, image, size, plan.slots - size)
            heard[rest, :] = jnp.zeros((plan.slots - size, plan.width), F32)
        spread(image, size)
        gap_ref = spread.target

        def one(pair):
            q = both_heads(query[0][rows, pair_lanes(query[1], pair)]).astype(BF)
            k = keys[0][rows, pair_lanes(keys[1], pair)].astype(BF)
            v = values[0][rows, pair_lanes(values[1], pair)].astype(BF)
            first = lax.broadcasted_iota(jnp.int32, (1, 2 * size), 1) < size
            slope = jnp.where(first, slopes[2 * pair], slopes[2 * pair + 1])
            scores = dot_nt(k, q) - slope * gap_ref[image, :size, : 2 * size]
            scores = jnp.exp(scores - jnp.max(scores, axis=0, keepdims=True))
            totals = jnp.sum(scores, axis=0, keepdims=True)
            p = (scores * (1.0 / totals)).astype(BF)
            weights[image * PAIRS + pair, :size, : 2 * size] = p
            heard[rows, pair_lanes(0, pair)] = one_pair(dot_tn(p, v))

        over_pairs(plan, one, size)

    by_size(plan, most_live, work)


def attend_back(plan, most_live, query, keys, values, grad_heard, weights, grads):
    grad_q, grad_k, grad_v = grads

    def work(image, size):
        rows = rows_of(plan, image, 0, size)
        if size < plan.slots:
            rest = rows_of(plan, image, size, plan.slots - size)
            for ref, offset in grads:
                ref[rest, offset : offset + plan.width] = jnp.zeros((plan.slots - size, plan.width), F32)

        def one(pair):
            q = both_heads(query[0][rows, pair_lanes(query[1], pair)]).astype(BF)
            k = keys[0][rows, pair_lanes(keys[1], pair)].astype(BF)
            v = values[0][rows, pair_lanes(values[1], pair)].astype(BF)
            g = both_heads(grad_heard[rows, pair_lanes(0, pair)]).astype(BF)
            p = weights[image * PAIRS + pair, :size, : 2 * size]
            wide = p.astype(F32)
            product = dot_nt(v, g) * wide
            grad_s = (product - wide * jnp.sum(product, axis=0, keepdims=True)).astype(BF)
            grad_v[0][rows, pair_lanes(grad_v[1], pair)] = dot_nn(p, g)
            grad_k[0][rows, pair_lanes(grad_k[1], pair)] = dot_nn(grad_s, q)
            grad_q[0][rows, pair_lanes(grad_q[1], pair)] = one_pair(dot_tn(grad_s, k)) * SCORE_SCALE

        over_pairs(plan, one, size)

    by_size(plan, most_live, work)


def columns_of(positions):
    images = positions.shape[0]
    low = positions.astype(F32).astype(BF)
    row = lax.broadcasted_iota(jnp.int32, (images, LANES), 0)
    lane = lax.broadcasted_iota(jnp.int32, (images, LANES), 1)
    return dot_tn(low, (row == lane).astype(F32).astype(BF))


def twice(positions, size):
    slots = positions.shape[1]
    low = positions.astype(F32).astype(BF)
    row = lax.broadcasted_iota(jnp.int32, (slots, 2 * size), 0)
    lane = lax.broadcasted_iota(jnp.int32, (slots, 2 * size), 1)
    from_slot = jnp.where(lane < size, lane, lane - size)
    return dot_nn(low, (row == from_slot).astype(F32).astype(BF))


class Spread:
    def __init__(self, plan, r, target, k, key_positions, key_count):
        self.plan, self.r, self.target, self.k = plan, r, target, k
        self.key_positions, self.key_count = key_positions, key_count

    def __call__(self, image, size):
        at = self.k * self.plan.per + image
        query = twice(self.r[K.positions][pl.ds(at, 1), :], size)
        keys = columns_of(self.r[self.key_positions][pl.ds(at, 1), :])
        self.target[image, :size, : 2 * size] = distances(
            keys[:size, :1], query, self.r[self.key_count][at]
        )


def most_live(plan, r, k, names):
    def live(image):
        found = r[names[0]][k * plan.per + image]
        for name in names[1:]:
            found = jnp.maximum(found, r[name][k * plan.per + image])
        return found

    return live


def fill_rows(target, images, slots, counts, first_image, source):
    for image in range(images):
        live = counts[first_image + image]
        for at in range(0, slots, 8):
            span = slice(image * slots + at, image * slots + at + 8)
            row = at + lax.broadcasted_iota(jnp.int32, (8, source.shape[1]), 0)
            target[span, :] = jnp.where(row < live, source[span, :], 0.0)


class Plan:
    def __init__(self, batches, slots, width, hidden, halving, unroll=1):
        self.batches, self.slots, self.width, self.hidden = batches, slots, width, hidden
        self.halving = halving
        self.unroll = unroll
        self.per = 2 if batches % 2 == 0 else 1
        self.steps = batches // self.per
        self.rows = self.per * slots
        self.total = batches * slots

    def unrolled(self, unroll):
        return Plan(self.batches, self.slots, self.width, self.hidden, self.halving, unroll)


def small_shape(plan):
    rows = 13 + plan.hidden // plan.width
    return (-(-rows // 8) * 8, plan.width)


WEIGHT_NAMES = (K.wqkv, K.wout, K.wfc1, K.wfc2, K.wcqkv, K.wcout)


def scratch_shapes(plan):
    r, d, f = plan.rows, plan.width, plan.hidden
    w = {
        K.wqkv: ((d, 3 * d), BF),
        K.wout: ((d, d), BF),
        K.wfc1: ((d, f), BF),
        K.wfc2: ((f, d), BF),
        K.wcqkv: ((d, 3 * d), BF),
        K.wcout: ((d, d), BF),
        K.xb: ((r, d), BF),
        K.x: ((r, d), F32),
        K.n: ((r, d), BF),
        K.qkv: ((r, 3 * d), F32),
        K.p: ((plan.per * PAIRS, plan.slots, 2 * plan.slots), BF),
        K.dist: ((plan.per, plan.slots, 2 * plan.slots), F32),
        K.heard: ((r, d), F32),
        K.o: ((r, d), BF),
        K.h: ((r, d), F32),
        K.n2: ((r, d), BF),
        K.u: ((r, f), F32),
        K.a: ((r, f), BF),
        K.gp: ((r, f), BF),
        K.y: ((r, d), F32),
        K.yout: ((r, d), F32),
        K.ysend: ((r, d), BF),
        K.gin: ((r, d), BF),
        K.g: ((r, d), F32),
        K.gbr: ((r, d), BF),
        K.du: ((r, f), BF),
        K.dn: ((r, d), F32),
        K.dh: ((r, d), F32),
        K.gm: ((r, d), BF),
        K.go: ((r, d), F32),
        K.dqkv: ((r, 3 * d), F32),
        K.dqkvb: ((r, 3 * d), BF),
        K.dx: ((r, d), F32),
        K.dxb: ((r, d), BF),
        K.ln: ((8, d), F32),
        K.cdist: ((plan.per, plan.slots, 2 * plan.slots), F32),
        K.m: ((r, d), BF),
        K.cq: ((r, d), F32),
        K.ckvb: ((r, 2 * d), BF),
        K.ckv: ((r, 2 * d), F32),
        K.cp: ((plan.per * PAIRS, plan.slots, 2 * plan.slots), BF),
        K.cheard: ((r, d), F32),
        K.co: ((r, d), BF),
        K.h2: ((r, d), F32),
        K.gaf: ((r, d), BF),
        K.cgo: ((r, d), F32),
        K.dcqkv: ((r, 3 * d), F32),
        K.dcq: ((r, d), BF),
        K.dckv: ((r, 2 * d), BF),
        K.dm: ((r, d), F32),
        K.dmid: ((r, d), F32),
        K.gl: ((plan.total, f), BF),
        K.gr: ((plan.total, f), BF),
        K.gsums: ((8, f), F32),
        K.small: (small_shape(plan), F32),
        K.gnat: ((2, 16, d // 16, d) if plan.halving else (2, d, d), BF),
        K.gnat_tall: ((2, 4, d // 4, d), BF),
        K.gout: ((2, 2, 8, d // 16, d), BF),
        K.gout_tall: ((2, 2, 2, d // 4, d), BF),
        K.rdr: ((plan.total, d), F32),
        K.rb: ((plan.total, d), BF),
        K.rkv: ((plan.total, 2 * d), BF),
    }
    return w


def chunk_shape(plan, height, breadth):
    if not plan.halving:
        return (height, breadth), BF
    if height == plan.width:
        return (8, height // 16, breadth), BF
    return (2, 2, 2, height // 16, breadth), BF


def chunk_state(name, height, breadth):
    def size(plan, amount):
        return plan.hidden if amount is None else amount * plan.width

    def main(plan):
        return chunk_shape(plan, size(plan, height), size(plan, breadth))

    def sums(plan):
        return (8, size(plan, breadth)), F32

    return {name: main, SENT[name]: main, SUMS[name]: sums}


STATE = {
    K.n: lambda p: ((p.total, p.width), BF),
    K.o: lambda p: ((p.total, p.width), BF),
    K.n2: lambda p: ((p.total, p.width), BF),
    K.a: lambda p: ((p.total, p.hidden), BF),
    K.layer_out: lambda p: ((p.total, p.width), F32),
    K.qkv: lambda p: ((p.total, 3 * p.width), F32),
    K.p: lambda p: ((p.batches * PAIRS, p.slots, 2 * p.slots), BF),
    K.h: lambda p: ((p.total, p.width), F32),
    K.gp: lambda p: ((p.total, p.hidden), BF),
    K.ckv: lambda p: ((p.total, 2 * p.width), BF),
    K.gbr: lambda p: ((p.total, p.width), BF),
    K.du: lambda p: ((p.total, p.hidden), BF),
    K.gm: lambda p: ((p.total, p.width), BF),
    K.dqkv: lambda p: ((p.total, 3 * p.width), BF),
    K.input_grads: lambda p: ((p.total, p.width), F32),
    K.m: lambda p: ((p.total, p.width), BF),
    K.co: lambda p: ((p.total, p.width), BF),
    K.gaf: lambda p: ((p.total, p.width), BF),
    K.dcq: lambda p: ((p.total, p.width), BF),
    K.dckv: lambda p: ((p.total, 2 * p.width), BF),
    K.between: lambda p: ((p.rows, p.width), F32),
    K.send: lambda p: ((p.rows, p.width), BF),
    K.ln: lambda p: ((8, p.width), F32),
    K.small: lambda p: (small_shape(p), F32),
    **chunk_state(K.cross, 1, 4),
    **chunk_state(K.fc2, None, 1),
    **chunk_state(K.fc1, 1, None),
    **chunk_state(K.attn, 1, 4),
}

FORWARD_0 = Job(
    reads=(K.streams,),
    writes=(K.n, K.o, K.n2, K.a, K.layer_out, K.qkv, K.p, K.h, K.gp, K.send),
    weights=(K.wqkv, K.wout, K.wfc1, K.wfc2),
    scratch=(K.xb, K.x, K.n, K.qkv, K.p, K.dist, K.heard, K.o, K.h, K.n2, K.u, K.a, K.gp, K.y, K.yout, K.ysend),
)
RADAR = Job(reads=(K.streams,), writes=(K.ckv,), weights=(K.wcqkv,), scratch=[K.rb, K.rkv])
MERGED = Job(
    reads=(K.received, K.cotangent, K.ckv),
    writes=(K.n, K.o, K.n2, K.a, K.layer_out, K.gbr, K.du, K.gm, K.dqkv, K.m, K.co, K.gaf, K.dcq, K.dckv, K.send, K.ln),
    weights=WEIGHT_NAMES,
    scratch=(K.xb, K.x, K.n, K.qkv, K.p, K.dist, K.heard, K.o, K.h, K.n2, K.u, K.a, K.gp, K.y, K.yout, K.gin, K.g, K.gbr, K.du, K.dn, K.dh, K.gm, K.go, K.dqkv, K.dqkvb, K.dxb, K.ln, K.cdist, K.m, K.cq, K.ckvb, K.ckv, K.cp, K.cheard, K.co, K.h2, K.gaf, K.cgo, K.dcqkv, K.dcq, K.dckv, K.dm, K.dmid,),
)
BACKWARD_0 = Job(
    reads=(K.streams, K.returned, K.qkv, K.p, K.h, K.gp),
    writes=(K.gbr, K.du, K.gm, K.dqkv, K.input_grads, K.ln),
    weights=(K.wfc2, K.wfc1, K.wout, K.wqkv),
    scratch=(K.xb, K.x, K.qkv, K.p, K.h, K.gp, K.gin, K.g, K.gbr, K.du, K.dn, K.dh, K.gm, K.go, K.dqkv, K.dqkvb, K.dx, K.ln),
)
BACKWARD_MLP = Job(
    reads=(K.returned, K.gp, K.h),
    writes=(K.du, K.between, K.ln),
    weights=(K.wfc2, K.wfc1),
    scratch=(K.h, K.gp, K.gin, K.g, K.gbr, K.du, K.dn, K.dh, K.ln),
)
BACKWARD_SELF = Job(
    reads=(K.between, K.streams, K.qkv, K.p),
    writes=(K.gm, K.dqkv, K.input_grads, K.ln),
    weights=(K.wout, K.wqkv),
    scratch=(K.xb, K.x, K.qkv, K.p, K.dn, K.dh, K.gm, K.go, K.dqkv, K.dqkvb, K.dx, K.ln),
)
RADAR_BACK = Job(
    reads=(K.dckv,), writes=(K.input_grads,), weights=(K.wcqkv,), scratch=(K.rkv, K.rdr)
)
GRAD_SCRATCH = (K.gl, K.gr, K.gnat, K.gout, K.gsums)
GRADS_CROSS = Job(
    reads=(K.m, K.streams, K.co, K.dcq, K.dckv, K.gaf),
    writes=(K.cross, K.cross_send, K.cross_sums),
    weights=(),
    scratch=GRAD_SCRATCH,
)
GRADS_FC2 = Job(
    reads=(K.a, K.gbr, K.returned),
    writes=(K.fc2, K.fc2_send, K.fc2_sums),
    weights=(),
    scratch=(K.gl, K.gr, K.gnat, K.gnat_tall, K.gout_tall, K.gsums, K.gin, K.dn, K.g),
)
GRADS_FC1 = Job(
    reads=(K.n2, K.du), writes=(K.fc1, K.fc1_send, K.fc1_sums), weights=(), scratch=GRAD_SCRATCH
)
GRADS_ATTN = Job(
    reads=(K.n, K.o, K.dqkv, K.gm, K.fc1_sums, K.fc2_sums, K.cross_sums),
    writes=(K.attn, K.attn_send, K.attn_sums, K.small),
    weights=(),
    scratch=GRAD_SCRATCH + (K.small,),
)
GRADS_MORE = Job(*(tuple(dict.fromkeys(one + two)) for one, two in zip(GRADS_FC2, GRADS_FC1)))
JOBS = {
    K.forward: FORWARD_0,
    K.radar: RADAR,
    K.merged: MERGED,
    K.backward: BACKWARD_0,
    K.backward_mlp: BACKWARD_MLP,
    K.backward_self: BACKWARD_SELF,
    K.radar_back: RADAR_BACK,
    K.grads_cross: GRADS_CROSS,
    K.grads_fc2: GRADS_FC2,
    K.grads_fc1: GRADS_FC1,
    K.grads_attn: GRADS_ATTN,
    K.grads_more: GRADS_MORE,
}
TILE = 768


def tiles(extent, tile=TILE):
    return [slice(at, min(at + tile, extent)) for at in range(0, extent, tile)]


def self_forward(plan, r, s, c, k, waits, save):
    d = plan.width
    rows = pl.ds(k * plan.rows, plan.rows)
    out = []
    gain, shift, bias = r[K.gains], r[K.shifts], r[K.attn_bias]
    norm_forward(s[K.x], gain[:, :d], shift[:, :d], s[K.n])
    out.append(c.start(s[K.n], r[K.n].at[rows]))
    waits[K.wqkv].wait()
    normed = s[K.n][...]
    s[K.qkv][:, :d] = (dot_nn(normed, s[K.wqkv][:, :d]) + bias[:, :d]).astype(BF).astype(F32) * SCORE_SCALE
    s[K.qkv][:, d : 2 * d] = dot_nn(normed, s[K.wqkv][:, d : 2 * d])
    s[K.qkv][:, 2 * d :] = dot_nn(normed, s[K.wqkv][:, 2 * d :]) + bias[:, d : 2 * d]
    if save:
        out.append(c.start(s[K.qkv], r[K.qkv].at[rows]))
    attend(
        plan,
        most_live(plan, r, k, (K.counts,)),
        (s[K.qkv], 0),
        (s[K.qkv], d),
        (s[K.qkv], 2 * d),
        Spread(plan, r, s[K.dist], k, K.positions, K.counts),
        r[K.slopes],
        s[K.heard],
        s[K.p],
    )
    if save:
        out.append(c.start(s[K.p], r[K.p].at[pl.ds(k * plan.per * PAIRS, plan.per * PAIRS)]))
    s[K.o][...] = s[K.heard][...].astype(BF)
    out.append(c.start(s[K.o], r[K.o].at[rows]))
    waits[K.wout].wait()
    s[K.h][...] = s[K.x][...] + dot_nn(s[K.o][...], s[K.wout][...]) + bias[:, 2 * d :]
    if save:
        out.append(c.start(s[K.h], r[K.h].at[rows]))
    return out


def mlp_forward(plan, r, s, c, k, waits, after, save):
    d, f = plan.width, plan.hidden
    rows = pl.ds(k * plan.rows, plan.rows)
    out = []
    norm_forward(after, r[K.gains][:, d:], r[K.shifts][:, d:], s[K.n2])
    out.append(c.start(s[K.n2], r[K.n2].at[rows]))
    waits[K.wfc1].wait()
    bias = r[K.mlp_bias]
    for tile in tiles(f):
        s[K.u][:, tile] = dot_nn(s[K.n2][...], s[K.wfc1][:, tile]) + bias[:, tile]
        for span in spans(plan.rows):
            active, slope = gelu_both(s[K.u][span, tile])
            s[K.a][span, tile] = active.astype(BF)
            s[K.gp][span, tile] = slope.astype(BF)
    out.append(c.start(s[K.a], r[K.a].at[rows]))
    if save:
        out.append(c.start(s[K.gp], r[K.gp].at[rows]))
    waits[K.wfc2].wait()
    s[K.y][...] = after[...] + dot_nn(s[K.a][...], s[K.wfc2][...]) + bias[:, f:]
    fill_rows(s[K.yout], plan.per, plan.slots, r[K.counts], k * plan.per, s[K.y])
    out.append(c.start(s[K.yout], r[K.layer_out].at[rows]))
    return out


def mlp_backward(plan, r, s, c, k, waits, after, target):
    d, f = plan.width, plan.hidden
    rows = pl.ds(k * plan.rows, plan.rows)
    out = []
    s[K.dn][...] = s[K.gin][...].astype(F32)
    fill_rows(s[K.g], plan.per, plan.slots, r[K.counts], k * plan.per, s[K.dn])
    s[K.gbr][...] = s[K.g][...].astype(BF)
    if K.gbr in r:
        out.append(c.start(s[K.gbr], r[K.gbr].at[rows]))
    if K.wfc2 in waits:
        waits[K.wfc2].wait()
    for tile in tiles(f):
        grad = dot_nt(s[K.gbr][...], s[K.wfc2][tile, :])
        s[K.du][:, tile] = (grad * s[K.gp][:, tile].astype(F32)).astype(BF)
    out.append(c.start(s[K.du], r[K.du].at[rows]))
    if K.wfc1 in waits:
        waits[K.wfc1].wait()
    s[K.dn][...] = dot_nt(s[K.du][...], s[K.wfc1][...])
    sums = norm_backward(after, r[K.gains][:, d:], s[K.dn], s[K.g], target)
    return out, sums


def self_backward(plan, r, s, c, k, waits, grad, target):
    d = plan.width
    rows = pl.ds(k * plan.rows, plan.rows)
    out = []
    s[K.gm][...] = grad[...].astype(BF)
    out.append(c.start(s[K.gm], r[K.gm].at[rows]))
    if K.wout in waits:
        waits[K.wout].wait()
    s[K.go][...] = dot_nt(s[K.gm][...], s[K.wout][...])
    attend_back(
        plan,
        most_live(plan, r, k, (K.counts,)),
        (s[K.qkv], 0),
        (s[K.qkv], d),
        (s[K.qkv], 2 * d),
        s[K.go],
        s[K.p],
        [(s[K.dqkv], part * d) for part in range(3)],
    )
    s[K.dqkvb][...] = s[K.dqkv][...].astype(BF)
    out.append(c.start(s[K.dqkvb], r[K.dqkv].at[rows]))
    if K.wqkv in waits:
        waits[K.wqkv].wait()
    s[K.dn][...] = dot_nt(s[K.dqkvb][...], s[K.wqkv][...])
    sums = norm_backward(s[K.x], r[K.gains][:, :d], s[K.dn], grad, target)
    return out, sums


def write_sums(s, c, r, parts):
    s[K.ln][...] = jnp.zeros_like(s[K.ln])
    for at, part in enumerate(parts):
        s[K.ln][at : at + 1, :] = part
    return c.start(s[K.ln], r[K.ln])


def start_weights(r, s, c, names):
    return {name: c.start(r[name], s[name]) for name in names}


def run_forward(plan, r, s, c, k):
    rows = pl.ds(k * plan.rows, plan.rows)
    arrive = c.start(r[K.streams].at[rows], s[K.xb])
    waits = start_weights(r, s, c, FORWARD_0.weights)
    arrive.wait()
    s[K.x][...] = s[K.xb][...].astype(F32)
    out = self_forward(plan, r, s, c, k, waits, True)
    out += mlp_forward(plan, r, s, c, k, waits, s[K.h], True)
    s[K.ysend][...] = s[K.yout][...].astype(BF)
    out.append(c.start(s[K.ysend], r[K.send]))
    for copy in out:
        copy.wait()


def run_radar(plan, r, s, c, k):
    d = plan.width
    arrive = c.start(r[K.streams], s[K.rb])
    weight = c.start(r[K.wcqkv], s[K.wcqkv])
    arrive.wait()
    weight.wait()
    s[K.rkv][:, :d] = dot_nn(s[K.rb][...], s[K.wcqkv][:, d : 2 * d]).astype(BF)
    s[K.rkv][:, d:] = (
        dot_nn(s[K.rb][...], s[K.wcqkv][:, 2 * d :]) + r[K.cross_bias][:, d : 2 * d]
    ).astype(BF)
    c.start(s[K.rkv], r[K.ckv]).wait()


def run_merged(plan, r, s, c, k):
    plan = plan.unrolled(3)
    d = plan.width
    rows = pl.ds(k * plan.rows, plan.rows)
    arrive = c.start(r[K.received], s[K.xb])
    waits = start_weights(r, s, c, (K.wqkv, K.wout, K.wcqkv, K.wcout, K.wfc1, K.wfc2))
    arrive_kv = c.start(r[K.ckv].at[rows], s[K.ckvb])
    arrive_grad = c.start(r[K.cotangent].at[rows], s[K.gin])
    arrive.wait()
    s[K.x][...] = s[K.xb][...].astype(F32)
    out = self_forward(plan, r, s, c, k, waits, False)
    bias = r[K.cross_bias]
    norm_forward(s[K.h], r[K.cross_gain][...], bias[:, 3 * d :], s[K.m])
    out.append(c.start(s[K.m], r[K.m].at[rows]))
    waits[K.wcqkv].wait()
    s[K.cq][...] = (dot_nn(s[K.m][...], s[K.wcqkv][:, :d]) + bias[:, :d]).astype(BF).astype(F32) * SCORE_SCALE
    arrive_kv.wait()
    s[K.ckv][...] = s[K.ckvb][...].astype(F32)
    live = most_live(plan, r, k, (K.counts, K.radar_counts))
    attend(
        plan,
        live,
        (s[K.cq], 0),
        (s[K.ckv], 0),
        (s[K.ckv], d),
        Spread(plan, r, s[K.cdist], k, K.radar_positions, K.radar_counts),
        r[K.slopes],
        s[K.cheard],
        s[K.cp],
    )
    s[K.co][...] = s[K.cheard][...].astype(BF)
    out.append(c.start(s[K.co], r[K.co].at[rows]))
    waits[K.wcout].wait()
    s[K.h2][...] = s[K.h][...] + dot_nn(s[K.co][...], s[K.wcout][...]) + bias[:, 2 * d : 3 * d]
    out += mlp_forward(plan, r, s, c, k, waits, s[K.h2], False)
    arrive_grad.wait()
    more, sums_two = mlp_backward(plan, r, s, c, k, {}, s[K.h2], s[K.dh])
    out += more
    s[K.gaf][...] = s[K.dh][...].astype(BF)
    out.append(c.start(s[K.gaf], r[K.gaf].at[rows]))
    s[K.cgo][...] = dot_nt(s[K.gaf][...], s[K.wcout][...])
    attend_back(
        plan,
        live,
        (s[K.cq], 0),
        (s[K.ckv], 0),
        (s[K.ckv], d),
        s[K.cgo],
        s[K.cp],
        [(s[K.dcqkv], part * d) for part in range(3)],
    )
    s[K.dcq][...] = s[K.dcqkv][:, :d].astype(BF)
    s[K.dckv][...] = s[K.dcqkv][:, d:].astype(BF)
    out.append(c.start(s[K.dcq], r[K.dcq].at[rows]))
    out.append(c.start(s[K.dckv], r[K.dckv].at[rows]))
    s[K.dm][...] = dot_nt(s[K.dcq][...], s[K.wcqkv][:, :d])
    sums_cross = norm_backward(s[K.h], r[K.cross_gain][...], s[K.dm], s[K.dh], s[K.dmid])
    more, sums_one = self_backward(plan, r, s, c, k, {}, s[K.dmid], s[K.dh])
    out += more
    s[K.dxb][...] = s[K.dh][...].astype(BF)
    out.append(c.start(s[K.dxb], r[K.send]))
    out.append(write_sums(s, c, r, sums_one + sums_two + sums_cross))
    for copy in out:
        copy.wait()


def load_mlp_back(plan, r, s, c, k):
    rows = pl.ds(k * plan.rows, plan.rows)
    arrive = [c.start(r[K.returned], s[K.gin])]
    waits = start_weights(r, s, c, (K.wfc2,))
    arrive.append(c.start(r[K.gp].at[rows], s[K.gp]))
    waits.update(start_weights(r, s, c, (K.wfc1,)))
    arrive.append(c.start(r[K.h].at[rows], s[K.h]))
    return arrive, waits


def load_self_back(plan, r, s, c, k):
    rows = pl.ds(k * plan.rows, plan.rows)
    waits = start_weights(r, s, c, (K.wout,))
    arrive = [
        c.start(r[K.qkv].at[rows], s[K.qkv]),
        c.start(r[K.p].at[pl.ds(k * plan.per * PAIRS, plan.per * PAIRS)], s[K.p]),
    ]
    waits.update(start_weights(r, s, c, (K.wqkv,)))
    arrive.append(c.start(r[K.streams].at[rows], s[K.xb]))
    return arrive, waits


def wait_all(copies):
    for copy in copies:
        copy.wait()


def run_backward(plan, r, s, c, k):
    rows = pl.ds(k * plan.rows, plan.rows)
    arrive, waits = load_mlp_back(plan, r, s, c, k)
    arrive_self, waits_self = load_self_back(plan, r, s, c, k)
    waits.update(waits_self)
    wait_all(arrive)
    out, sums_two = mlp_backward(plan, r, s, c, k, waits, s[K.h], s[K.dh])
    wait_all(arrive_self)
    s[K.x][...] = s[K.xb][...].astype(F32)
    more, sums_one = self_backward(plan, r, s, c, k, waits, s[K.dh], s[K.dx])
    out += more
    out.append(c.start(s[K.dx], r[K.input_grads].at[rows]))
    out.append(write_sums(s, c, r, sums_one + sums_two))
    wait_all(out)


def run_backward_mlp(plan, r, s, c, k):
    arrive, waits = load_mlp_back(plan, r, s, c, k)
    wait_all(arrive)
    out, sums_two = mlp_backward(plan, r, s, c, k, waits, s[K.h], s[K.dh])
    out.append(c.start(s[K.dh], r[K.between]))
    nothing = jnp.zeros_like(sums_two[0])
    out.append(write_sums(s, c, r, (nothing, nothing) + sums_two))
    wait_all(out)


def run_backward_self(plan, r, s, c, k):
    rows = pl.ds(k * plan.rows, plan.rows)
    arrive = [c.start(r[K.between], s[K.dh])]
    more, waits = load_self_back(plan, r, s, c, k)
    wait_all(arrive + more)
    s[K.x][...] = s[K.xb][...].astype(F32)
    out, sums_one = self_backward(plan, r, s, c, k, waits, s[K.dh], s[K.dx])
    out.append(c.start(s[K.dx], r[K.input_grads].at[rows]))
    out.append(write_sums(s, c, r, sums_one))
    wait_all(out)


def run_radar_back(plan, r, s, c, k):
    d = plan.width
    arrive = c.start(r[K.dckv], s[K.rkv])
    weight = c.start(r[K.wcqkv], s[K.wcqkv])
    arrive.wait()
    weight.wait()
    s[K.rdr][...] = dot_nt(s[K.rkv][...], s[K.wcqkv][:, d:])
    c.start(s[K.rdr], r[K.input_grads]).wait()


def slot_of(relative):
    return ((relative >> 1) & 1) * 4 + ((relative >> 2) & 1) * 2 + ((relative >> 3) & 1)


def weight_grads(plan, r, s, c, lefts, rights, left_of, tall, name, fix=None):
    d, total = plan.width, plan.total

    def blocks(buffer, names):
        found = []
        for array in names:
            for tile in tiles(r[array].shape[1], d):
                at = len(found) * d
                found.append((r[array].at[:, tile], buffer.at[:, at : at + d]))
        return found

    left_blocks, right_blocks = blocks(s[K.gl], lefts), blocks(s[K.gr], rights)
    count = max(len(left_blocks), len(right_blocks))
    loads, seen = [], set()
    for t in range(count):
        wanted = [(0, 0 if tall else t), (1, left_of(t))]
        fresh = [key for key in wanted if key not in seen]
        seen.update(fresh)
        loads.append([c.start(*(right_blocks, left_blocks)[side][at]) for side, at in fresh])
    if fix is not None:
        wait_all(loads[0])
        loads[0] = []
        fix()
    mine = r[K.device][0]
    block = d // 4 if tall else d // 16
    natural = s[K.gnat_tall if tall and plan.halving else K.gnat]
    gout = s[K.gout_tall if tall else K.gout] if plan.halving else None
    sems = c.reserve(4)

    def columns(at):
        return pl.ds(pl.multiple_of(at * d, LANES), d)

    def copies_out(t):
        slot = lax.rem(t, 2)
        found = []
        for sent in range(2 if plan.halving else 1):
            ref = r[SENT[name] if sent else name]
            if not plan.halving:
                target = ref.at[columns(t), :] if tall else ref.at[:, columns(t)]
                source = natural.at[slot]
            elif tall:
                away = t ^ (mine >> 2)
                target, source = ref.at[:, away & 1, away >> 1], gout.at[slot, sent]
            else:
                target, source = ref.at[:, :, columns(t)], gout.at[slot, sent]
            found.append(pltpu.make_async_copy(source, target, sems(slot * 2 + sent)))
        return found

    def wait_out(t):
        wait_all(copies_out(t))

    def hand_on(t):
        for one in copies_out(t):
            one.start()

    def arrange(slot):
        if tall:
            for relative in range(4):
                gout[slot, relative & 1, relative >> 1] = natural[slot, (mine & 3) ^ relative]
        else:
            for relative in range(16):
                gout[slot, relative & 1, slot_of(relative)] = natural[slot, mine ^ relative]

    behind = 1 if plan.halving else 0

    def step(t, carry):
        for at, found in enumerate(loads):
            if found:
                pl.when(t == at)(lambda found=found: wait_all(found))
        pl.when(t >= 2 + behind)(lambda: wait_out(t - 2 - behind))
        slot = lax.rem(t, 2)
        grad = s[K.gr][:, columns(0 if tall else t)]
        low = dot_tn(s[K.gl][:, columns(left_of(t))], grad).astype(BF)
        if plan.halving:
            for part in range(d // block):
                natural[slot, part] = low[part * block : (part + 1) * block]
            arrange(1 - slot)
        else:
            natural[slot] = low
        sums = jnp.sum(grad.astype(F32).reshape(total // 8, 8, d), axis=0)
        s[K.gsums][:, columns(0 if tall else t)] = sums
        pl.when(t >= behind)(lambda: hand_on(t - behind))
        return carry

    lax.fori_loop(0, count, step, 0)
    if plan.halving:
        wait_out(count - 3)
        arrange((count - 1) % 2)
        hand_on(count - 1)
    breadth = len(right_blocks) * d
    last = c.start(s[K.gsums].at[:, :breadth], r[SUMS[name]])
    wait_out(count - 2)
    wait_out(count - 1)
    last.wait()


def run_grads_cross(plan, r, s, c, k):
    weight_grads(
        plan, r, s, c, (K.m, K.streams, K.co), (K.dcq, K.dckv, K.gaf),
        lambda t: (t + 1) // 2, False, K.cross,
    )


def run_grads_fc2(plan, r, s, c, k):
    last = plan.steps - 1
    arrive = c.start(r[K.returned], s[K.gin])

    def fix():
        arrive.wait()

        @pl.when(r[K.section][0] == 0)
        def _():
            s[K.dn][...] = s[K.gin][...].astype(F32)
            fill_rows(s[K.g], plan.per, plan.slots, r[K.counts], last * plan.per, s[K.dn])
            s[K.gr][last * plan.rows :, : plan.width] = s[K.g][...].astype(BF)

    weight_grads(plan, r, s, c, (K.a,), (K.gbr,), lambda t: t, True, K.fc2, fix)


def run_grads_fc1(plan, r, s, c, k):
    weight_grads(plan, r, s, c, (K.n2,), (K.du,), lambda t: 0 * t, False, K.fc1)


def run_grads_more(plan, r, s, c, k):
    run_grads_fc2(plan, r, s, c, k)
    run_grads_fc1(plan, r, s, c, k)


def run_grads_attn(plan, r, s, c, k):
    weight_grads(plan, r, s, c, (K.n, K.o), (K.dqkv, K.gm), lambda t: t // 3, False, K.attn)
    d = plan.width
    first = sum(r[name][...] for name in r if name in FIRST)
    second = sum(r[name][...] for name in r if name in SECOND)
    norms = jnp.where(r[K.section][0] == 0, first, second)
    ratio = plan.hidden // d

    def column(ref, at):
        return jnp.sum(ref[:, at * d : (at + 1) * d], axis=0, keepdims=True)

    rows = [column(s[K.gsums], 0), column(s[K.gsums], 2), column(s[K.gsums], 3)]
    rows += [column(r[K.fc1_sums], at) for at in range(ratio)] + [column(r[K.fc2_sums], 0)]
    rows += [norms[0:1], norms[2:3], norms[1:2], norms[3:4], norms[4:5]]
    rows += [column(r[K.cross_sums], at) for at in (0, 2, 3)] + [norms[5:6]]
    s[K.small][...] = jnp.zeros_like(s[K.small])
    for at, row in enumerate(rows):
        s[K.small][at : at + 1, :] = row
    c.start(s[K.small], r[K.small]).wait()


RUN = {
    K.forward: run_forward,
    K.radar: run_radar,
    K.merged: run_merged,
    K.backward: run_backward,
    K.backward_mlp: run_backward_mlp,
    K.backward_self: run_backward_self,
    K.radar_back: run_radar_back,
    K.grads_cross: run_grads_cross,
    K.grads_fc2: run_grads_fc2,
    K.grads_fc1: run_grads_fc1,
    K.grads_attn: run_grads_attn,
    K.grads_more: run_grads_more,
}


def phase(plan, fixed, state, weights, first, second, after=()):
    jobs = [job for job in (first, second) if job is not None]
    shared = len(jobs) == 2 and jobs[0][0] == jobs[1][0]
    kinds = [JOBS[job[0]] for job in jobs]
    taken = {}
    for job in jobs:
        taken.update(job[2])
    writes = []
    for kind in kinds:
        writes += [name for name in kind.writes if name not in writes]
    reads = []
    for kind in kinds:
        for name in kind.reads:
            if name in state and name not in reads and name not in writes:
                reads.append(name)
            elif name in (K.streams, K.cotangent):
                taken[name] = fixed[name]
    used = [name for name in WEIGHT_NAMES if any(name in kind.weights for kind in kinds)]
    fresh = [name for name in writes if name not in state or name in (K.send, K.ln)]
    kept = [name for name in writes if name not in fresh]
    small = [name for name in fixed if name not in (K.streams, K.cotangent)]
    if all(job[0] in GRAD_JOBS for job in jobs):
        small = [K.section, K.device, K.counts]
    elif not any(job[0] in (K.radar, K.merged) for job in jobs):
        small = [name for name in small if name not in (K.cross_gain, K.cross_bias)]
    every = scratch_shapes(plan)
    need = list(used)
    for kind in kinds:
        need += [name for name in kind.scratch if name not in need]

    operands, specs, names = [], [], []
    for name in small:
        operands.append(fixed[name])
        specs.append(SM if name in (K.section, K.device, K.counts, K.radar_counts, K.slopes) else VM)
        names.append(name)
    for name in used:
        operands.append(weights[name])
        specs.append(ANY)
        names.append(name)
    for name, array in list(taken.items()) + [(name, state[name]) for name in reads]:
        operands.append(array)
        specs.append(VM if name in IN_VMEM else ANY)
        names.append(name)
    operands += after
    specs += [ANY] * len(after)
    names += [None] * len(after)
    alias = {}
    for at, name in enumerate(kept):
        alias[len(operands)] = at
        operands.append(state[name])
        specs.append(ANY)
        names.append(None)
    outs = kept + fresh
    shapes = [jax.ShapeDtypeStruct(*STATE[name](plan)) for name in outs]

    def kernel(*refs):
        r, s = {}, {}
        for name, ref in zip(names, refs):
            if name is not None:
                r[name] = ref
        refs = refs[len(names) :]
        for name, ref in zip(outs, refs):
            r[name] = ref
        refs = refs[len(outs) :]
        for name, ref in zip(need, refs):
            s[name] = ref
        sems = refs[len(need)]
        if shared:
            RUN[first[0]](plan, r, s, Copies(sems), first[1])
            return
        for which, job in ((0, first), (1, second)):
            if job is not None:

                @pl.when(r[K.section][0] == which)
                def _():
                    RUN[job[0]](plan, r, s, Copies(sems), job[1])

    results = pl.pallas_call(
        kernel,
        out_shape=shapes,
        in_specs=specs,
        out_specs=[ANY] * len(outs),
        scratch_shapes=[pltpu.VMEM(*every[name]) for name in need] + [pltpu.SemaphoreType.DMA((32,))],
        input_output_aliases=alias,
        compiler_params=pltpu.CompilerParams(vmem_limit_bytes=VMEM_LIMIT),
        cost_estimate=CHEAP,
        name="_".join(job[0].name + str(job[1]) for job in jobs),
    )(*operands)
    new = dict(zip(outs, results))
    for name in outs:
        if name not in (K.send, K.ln):
            state[name] = new[name]
    return new.get(K.send), new.get(K.ln)


def body(
    streams,
    cotangent,
    counts,
    positions,
    radar_counts,
    radar_positions,
    qkv_weight,
    out_weight,
    fc1_weight,
    fc2_weight,
    attn_bias,
    mlp_bias,
    norm_gains,
    norm_shifts,
    cross_qkv_weight,
    cross_out_weight,
    cross_gain,
    cross_bias,
):
    devices = lax.axis_size(BATCH)
    section_id = lax.axis_index(SECTION)
    me = lax.axis_index(BATCH)
    width = cotangent.shape[1]
    hidden = fc1_weight.shape[2]
    halving = devices == 16
    plan = Plan(counts.shape[0], positions.shape[1], width, hidden, halving)
    device = me.astype(jnp.int32).reshape(1)
    section = section_id.astype(jnp.int32).reshape(1)
    head_slopes = [2.0 ** (-8.0 * (head + 1.0) / H) for head in range(H)]
    fixed = {
        K.section: section,
        K.device: device,
        K.counts: counts,
        K.radar_counts: radar_counts,
        K.slopes: jnp.array(head_slopes, F32),
        K.positions: positions,
        K.radar_positions: radar_positions,
        K.attn_bias: attn_bias,
        K.mlp_bias: mlp_bias,
        K.gains: norm_gains,
        K.shifts: norm_shifts,
        K.cross_gain: cross_gain.reshape(1, width),
        K.cross_bias: cross_bias.reshape(1, 4 * width),
        K.streams: streams[0],
        K.cotangent: cotangent,
    }
    weights = dict(
        zip(
            WEIGHT_NAMES,
            (
                qkv_weight[0],
                out_weight[0],
                fc1_weight[0],
                fc2_weight[0],
                cross_qkv_weight,
                cross_out_weight,
            ),
        )
    )
    state = {}
    steps = plan.steps
    arrived = []
    for k in range(steps):
        second = (K.radar, 0, {}) if k == min(1, steps - 1) else None
        send, _ = phase(plan, fixed, state, weights, (K.forward, k, {}), second)
        arrived.append(lax.ppermute(send, SECTION, [(0, 1)]))
    returned, first_sums, second_sums = [], [], []
    for k in range(steps):
        send, sums = phase(
            plan, fixed, state, weights, None, (K.merged, k, {K.received: arrived[k]})
        )
        second_sums.append(sums)
        returned.append(lax.ppermute(send, SECTION, [(1, 0)]))
        if 0 < k < steps - 1:
            _, sums = phase(
                plan, fixed, state, weights, (K.backward, k - 1, {K.returned: returned[k - 1]}), None
            )
            first_sums.append(sums)

    route = {bit: [(at, at ^ bit) for at in range(devices)] for bit in (1, 2, 4, 8, 12)} if halving else {}

    def trade(block, bit):
        return lax.ppermute(block, BATCH, route[bit])

    def trade_second(block, bit):
        pairs = [(devices + left, devices + right) for left, right in route[bit]]
        return lax.ppermute(block, (SECTION, BATCH), pairs)

    def scatter(part):
        return lax.psum_scatter(part, BATCH, scatter_dimension=0, tiled=True).astype(F32)

    def run(first, second, after=()):
        _, sums = phase(plan, fixed, state, weights, first, second, after=list(after))
        if first is not None and first[0] in BACK_JOBS:
            first_sums.append(sums)

    def both(job, taken, after=()):
        run((job, 0, taken), (job, 0, taken), after)

    def add_up(parts, low, high):
        return sum(part[low:high].astype(F32) for part in parts)

    def begin(name, exchange, pieces=1):
        kept, sent = state[name], state[SENT[name]]
        kept, sent = (x.reshape(8, -1, x.shape[-1]) for x in (kept, sent))
        come = [exchange(piece, 1) for piece in jnp.split(sent, pieces)]
        return [kept, jnp.concatenate(come) if pieces > 1 else come[0]]

    def step(parts, exchange, bit):
        half = parts[-1].shape[0] // 2
        return parts + [exchange(add_up(parts, half, 2 * half).astype(BF), bit)]

    def spread(parts, exchange):
        found = [exchange(add_up(parts, at, at + 1).astype(BF), bit) for at, bit in ((1, 8), (2, 4), (3, 12))]
        return [part[:1] for part in parts] + found

    def total(parts):
        return add_up(parts, 0, 1)[0]

    def taken_sums():
        return dict(zip(FIRST, first_sums)) | dict(zip(SECOND, second_sums))

    def once(*arrays):
        return lax.optimization_barrier(arrays)

    last = steps - 1
    queue = [(K.backward, k, {K.returned: returned[k]}) for k in range(max(last - 1, 0), last)] or [None]
    for job in queue[:-1]:
        run(job, None)
    run(queue[-1], (K.grads_cross, 0, {}))
    if halving:
        state[K.cross_send], returned[last] = once(state[K.cross_send], returned[last])
        cross = step(begin(K.cross, trade_second), trade_second, 2)
        taken = {K.returned: returned[last]}
        run((K.grads_fc2, 0, taken), (K.grads_more, 0, taken), [cross[1]])
        state[K.fc2], state[K.fc2_send], cross[-1] = once(
            state[K.fc2], state[K.fc2_send], cross[-1]
        )
        fc2 = begin(K.fc2, trade)
        ahead = add_up(fc2, 4, 8).astype(BF)
        cross[-1], ahead = once(cross[-1], ahead)
        fc2.append(trade(ahead, 2))
        cross = spread(cross, trade_second)
        run((K.backward_mlp, last, taken), None, [fc2[1]])
        run((K.grads_fc1, 0, {}), None)
        state[K.fc1], state[K.fc1_send], fc2[-1], *cross[-3:] = once(
            state[K.fc1], state[K.fc1_send], fc2[-1], *cross[-3:]
        )
        fc1 = begin(K.fc1, trade)
        fc2 = spread(fc2, trade)
        run((K.backward_self, last, {}), None, [fc1[-1]])
        fc1 = step(fc1, trade, 2)
        both(K.grads_attn, taken_sums())
        state[K.attn], state[K.attn_send], fc1[-1], *fc2[-3:] = once(
            state[K.attn], state[K.attn_send], fc1[-1], *fc2[-3:]
        )
        attn = begin(K.attn, trade)
        ahead = add_up(attn, 4, 8).astype(BF)
        ahead, fc1[-1], small = once(ahead, fc1[-1], state[K.small])
        attn.append(trade(ahead, 2))
        fc1 = spread(fc1, trade)
        small = small + trade(small, 1)
        next_small = trade(small, 2)
        run(None, (K.radar_back, 0, {}), [small])
        attn[-1], next_small, state[K.input_grads], *fc1[-3:] = once(
            attn[-1], next_small, state[K.input_grads], *fc1[-3:]
        )
        small = small + next_small
        small = small + sum(trade(small, bit) for bit in (4, 8, 12))
        attn = spread(attn, trade)
        cross_share, grad_fc2, grad_fc1, grad_attn = (total(x) for x in (cross, fc2, fc1, attn))
    else:
        both(K.grads_fc2, {K.returned: returned[last]})
        run((K.backward_mlp, last, {K.returned: returned[last]}), None)
        both(K.grads_fc1, {})
        run((K.backward_self, last, {}), None)
        both(K.grads_attn, taken_sums())
        small = lax.psum(state[K.small], BATCH)
        run(None, (K.radar_back, 0, {}))
        cross_share, grad_fc2, grad_fc1, grad_attn = (
            scatter(state[name]) for name in (K.cross, K.fc2, K.fc1, K.attn)
        )
    split = qkv_weight.shape[2]

    is_first = section_id == 0

    def to_both(block):
        return jnp.where(is_first, lax.ppermute(block, SECTION, [(1, 0)]), block).astype(F32)

    cross_all = to_both(cross_share.astype(BF))
    ratio = hidden // width
    edges = [0, 3, 4 + ratio, 6 + ratio, 8 + ratio, 9 + ratio, 13 + ratio]
    cross_small = to_both(small[edges[4] : edges[6]])
    parts = []
    for low, high in zip(edges, edges[1:]):
        rows = small[low:high] if high <= edges[4] else cross_small[low - edges[4] : high - edges[4]]
        size = (high - low) * width // devices
        parts.append(lax.dynamic_slice(rows.reshape(-1), (me * size,), (size,)))
    return (
        state[K.layer_out][None],
        state[K.input_grads][None],
        grad_attn[None, :, :split],
        grad_attn[None, :, split:],
        grad_fc1[None],
        grad_fc2[None],
        parts[0][None],
        parts[1][None],
        parts[2][None],
        parts[3][None],
        cross_all[:, :split],
        cross_all[:, split:],
        parts[4],
        parts[5],
    )


def solution(mesh):
    in_specs = (
        P(SECTION, BATCH, None),
        P(BATCH, None),
        P(BATCH),
        P(BATCH, None),
        P(BATCH),
        P(BATCH, None),
        P(SECTION, None, None),
        P(SECTION, None, None),
        P(SECTION, None, None),
        P(SECTION, None, None),
        P(SECTION, None),
        P(SECTION, None),
        P(SECTION, None),
        P(SECTION, None),
        P(),
        P(),
        P(),
        P(),
    )
    out_specs = (
        P(SECTION, BATCH, None),
        P(SECTION, BATCH, None),
        P(SECTION, BATCH, None),
        P(SECTION, BATCH, None),
        P(SECTION, BATCH, None),
        P(SECTION, BATCH, None),
        P(SECTION, BATCH),
        P(SECTION, BATCH),
        P(SECTION, BATCH),
        P(SECTION, BATCH),
        P(BATCH, None),
        P(BATCH, None),
        P(BATCH),
        P(BATCH),
    )
    return jax.shard_map(body, mesh=mesh, in_specs=in_specs, out_specs=out_specs, check_vma=False)
```

time: 363 us -> 346 us (0.953)
  the two profiles are of different devices: /device:TPU:6 before, /device:TPU:12 now
where the time goes in v2:
time: 346 us; the launch traced here: 340 us
  Pallas kernels  154 us (45%)
  waiting for transfers between devices  87.7 us (25%)
  starting transfers between devices  54 us (16%)
  other arithmetic  31.1 us (9%)
  local copies, waits for them, and re-layouts  12.2 us (4%)
    pallas_call x14, Pallas kernels, phase(): pl.pallas_call(kernel, out_shape=shapes, in_specs=specs, out_specs=[ANY]...  154 us
    ppermute x20, waiting for transfers between devices, trade(): return lax.ppermute(block, BATCH, route[bit])  49.1 us
    ppermute x5, waiting for transfers between devices, trade_second(): return lax.ppermute(block, (SECTION, BATCH), pairs)  27.7 us
    ppermute x5, starting transfers between devices, trade_second(): return lax.ppermute(block, (SECTION, BATCH), pairs)  22.9 us
    ppermute x20, starting transfers between devices, trade(): return lax.ppermute(block, BATCH, route[bit])  19.7 us
    convert_element_type x4, other arithmetic, spread(): add_up(parts, at, at + 1).astype(BF)  10.7 us
    ppermute x3, waiting for transfers between devices, body(): arrived.append(lax.ppermute(send, SECTION, [(0, 1)]))  10.6 us
    convert_element_type x2, other arithmetic, step(): return parts + [exchange(add_up(parts, half, 2 * half).astype(BF), bit)]  7.15 us
  transfers between devices with their start and end apart: 33, of which 16 were waited for; matrix products, arithmetic and copies ran while one was open for 8% of the time, Pallas kernels for 45%

profile of v2, /device:TPU:12, one launch (start us, length us, event | category | flops | bytes accessed | tf_op | source)
XLA Modules:
  0.0 340.2 jit_solution(11968715772082640512)
XLA Ops:
  3.7 7.6 %forward1_radar0.1 = (bf16[816,768]{1,0:T(8,128)(2,1)}, bf16[816,768]{1,0:T(8,128)(2,1)}, bf16[816,768]{1,0:T(8,128)(2,1)}, bf16[816,3072]{1,0:T(8,128)(2,1)}, f...) custom-call(s32[1]{0:T(128)} %bitcast.refs_0_, ...), custom_call_target="tpu_custom_call", output_to_operand_aliasing={{0}: (19, {}), {1}: (20, {}), {2}: (21, {}), {3}: (22, {}),... | custom-call | flops 1 | bytes 1 | tf_op jit(solution)/shard_map/forward1_radar0/pallas_call | solution.py:1161
  13.9 10.6 %collective-permute-done.2.refs_19_ = bf16[272,768]{1,0:T(8,128)(2,1)S(1)} collective-permute-done((bf16[272,768]{1,0:T(8,128)(2,1)}, bf16[272,768]{1,0:T(8,128)(2,1)S(1)}, u32[]{:S(2)}, u32[]{:S(2)}) %collective-permute-start.2) | collective-permute-done | bytes 417824 | tf_op jit(solution)/shard_map/ppermute | solution.py:1245
  25.3 29.6 %merged0.1 = (bf16[816,768]{1,0:T(8,128)(2,1)}, bf16[816,768]{1,0:T(8,128)(2,1)}, bf16[816,768]{1,0:T(8,128)(2,1)}, bf16[816,3072]{1,0:T(8,128)(2,1)}, f32[816,7...) custom-call(s32[1]{0:T(128)} %bitcast.refs_0_, ...), custom_call_target="tpu_custom_call", output_to_operand_aliasing={{0}: (22, {}), {1}: (23, {}), {2}: (24, {}), {3}: (25, {}),... | custom-call | flops 1 | bytes 1 | tf_op jit(solution)/shard_map/merged0/pallas_call | solution.py:1161
  59.4 29.6 %merged1.1 = (bf16[816,768]{1,0:T(8,128)(2,1)}, bf16[816,768]{1,0:T(8,128)(2,1)}, bf16[816,768]{1,0:T(8,128)(2,1)}, bf16[816,3072]{1,0:T(8,128)(2,1)}, f32[816,7...) custom-call(s32[1]{0:T(128)} %bitcast.refs_0_, ...), custom_call_target="tpu_custom_call", output_to_operand_aliasing={{0}: (22, {}), {1}: (23, {}), {2}: (24, {}), {3}: (25, {}),... | custom-call | flops 1 | bytes 1 | tf_op jit(solution)/shard_map/merged1/pallas_call | solution.py:1161
  92.9 29.4 %merged2.1 = (bf16[816,768]{1,0:T(8,128)(2,1)}, bf16[816,768]{1,0:T(8,128)(2,1)}, bf16[816,768]{1,0:T(8,128)(2,1)}, bf16[816,3072]{1,0:T(8,128)(2,1)}, f32[816,7...) custom-call(s32[1]{0:T(128)} %bitcast.refs_0_, ...), custom_call_target="tpu_custom_call", output_to_operand_aliasing={{0}: (22, {}), {1}: (23, {}), {2}: (24, {}), {3}: (25, {}),... | custom-call | flops 1 | bytes 1 | tf_op jit(solution)/shard_map/merged2/pallas_call | solution.py:1161
  124.4 10.6 %backward1_grads_cross0.1 = (bf16[816,768]{1,0:T(8,128)(2,1)}, bf16[816,3072]{1,0:T(8,128)(2,1)}, bf16[816,768]{1,0:T(8,128)(2,1)}, bf16[816,2304]{1,0:T(8,128)(...) custom-call(s32[1]{0:T(128)} %bitcast.refs_0_, ...), custom_call_target="tpu_custom_call", output_to_operand_aliasing={{0}: (26, {}), {1}: (27, {}), {2}: (28, {}), {3}: (29, {}),... | custom-call | flops 1 | bytes 1 | tf_op jit(solution)/shard_map/backward1_grads_cross0/pallas_call | solution.py:1161
  135.0 4.4 %collective-permute-start.6 = (bf16[8,48,3072]{2,1,0:T(8,128)(2,1)}, bf16[8,48,3072]{2,1,0:T(8,128)(2,1)S(1)}, u32[]{:S(2)}, u32[]{:S(2)}) collective-permute-start(bf16[8,48,3072]{2,1,0:T(8,128)(2,1)} %get-tuple-element.240), channel_id=1, source_target_pairs={{16,17},{17,16},{18,19},{19,18},{20,21},{21,20},{22,23},{23,22},{2... | collective-permute-start | bytes 7077896 | tf_op jit(solution)/shard_map/ppermute | solution.py:1266
  139.5 4.3 %collective-permute-done.6.refs_8_ = bf16[8,48,3072]{2,1,0:T(8,128)(2,1)S(1)} collective-permute-done((bf16[8,48,3072]{2,1,0:T(8,128)(2,1)}, bf16[8,48,3072]{2,1,0:T(8,128)(2,1)S(1)}, u32[]{:S(2)}, u32[]{:S(2)}) %collective-permute-start.6) | collective-permute-done | bytes 2359328 | tf_op jit(solution)/shard_map/ppermute | solution.py:1266
  143.8 3.6 %add_convert_fusion.2 = bf16[4,48,3072]{2,1,0:T(8,128)(2,1)} fusion(bf16[8,48,3072]{2,1,0:T(8,128)(2,1)S(1)} %collective-permute-done.6.refs_8_, bf16[8,48,3072]{2,1,0:T(8,128)(2,1)} %get-tuple-element.243), kind=kLoop, calls=%fused_computation.4 | loop fusion | flops 2359296 | bytes 3538944 | tf_op jit(solution)/shard_map/convert_element_type | solution.py:1290
  147.4 9.3 %collective-permute-start.7 = (bf16[4,48,3072]{2,1,0:T(8,128)(2,1)}, bf16[4,48,3072]{2,1,0:T(8,128)(2,1)S(1)}, u32[]{:S(2)}, u32[]{:S(2)}) collective-permute-start(bf16[4,48,3072]{2,1,0:T(8,128)(2,1)} %add_convert_fusion.2), channel_id=1, source_target_pairs={{16,18},{17,19},{18,16},{19,17},{20,22},{21,23},{22,20},{23,21},{2... | collective-permute-start | bytes 3538952 | tf_op jit(solution)/shard_map/ppermute | solution.py:1266
  156.7 20.7 %grads_fc20_grads_more0.1 = (bf16[2,2,2,192,768]{4,3,2,1,0:T(8,128)(2,1)}, bf16[2,2,2,192,768]{4,3,2,1,0:T(8,128)(2,1)}, f32[8,768]{1,0:T(8,128)}, bf16[8,48,307...) custom-call(s32[1]{0:T(128)} %bitcast.refs_0_, s32[1]{0:T(128)} %bitcast.1.refs_1_, s32[6]{0:T(128)} %refs_2_.27, ...), custom_call_target="tpu_custom_call" | custom-call | flops 1 | bytes 1 | tf_op jit(solution)/shard_map/grads_fc20_grads_more0/pallas_call | solution.py:1161
  177.4 5.9 %collective-permute-done.7 = bf16[4,48,3072]{2,1,0:T(8,128)(2,1)S(1)} collective-permute-done((bf16[4,48,3072]{2,1,0:T(8,128)(2,1)}, bf16[4,48,3072]{2,1,0:T(8,128)(2,1)S(1)}, u32[]{:S(2)}, u32[]{:S(2)}) %collective-permute-start.7) | collective-permute-done | bytes 1179680 | tf_op jit(solution)/shard_map/ppermute | solution.py:1266
  196.4 3.9 %collective-permute-start.11 = (bf16[1,48,3072]{2,1,0:T(8,128)(2,1)}, bf16[1,48,3072]{2,1,0:T(8,128)(2,1)}, u32[]{:S(2)}, u32[]{:S(2)}) collective-permute-start(bf16[1,48,3072]{2,1,0:T(8,128)(2,1)} %get-tuple-element.306), channel_id=1, source_target_pairs={{16,20},{17,21},{18,22},{19,23},{20,16},{21,17},{22,18},{23,19},{2... | collective-permute-start | bytes 884744 | tf_op jit(solution)/shard_map/ppermute | solution.py:1266
  205.8 4.8 %collective-permute-done.10 = bf16[1,48,3072]{2,1,0:T(8,128)(2,1)} collective-permute-done((bf16[1,48,3072]{2,1,0:T(8,128)(2,1)}, bf16[1,48,3072]{2,1,0:T(8,128)(2,1)}, u32[]{:S(2)}, u32[]{:S(2)}) %collective-permute-start.10) | collective-permute-done | bytes 294944 | tf_op jit(solution)/shard_map/ppermute | solution.py:1266
  212.8 10.4 %collective-permute-done.12 = bf16[1,48,3072]{2,1,0:T(8,128)(2,1)} collective-permute-done((bf16[1,48,3072]{2,1,0:T(8,128)(2,1)S(1)}, bf16[1,48,3072]{2,1,0:T(8,128)(2,1)}, u32[]{:S(2)}, u32[]{:S(2)}) %collective-permute-start.12) | collective-permute-done | bytes 294944 | tf_op jit(solution)/shard_map/ppermute | solution.py:1266
  223.3 4.7 %collective-permute-done.13.refs_17_ = bf16[8,48,3072]{2,1,0:T(8,128)(2,1)S(1)} collective-permute-done((bf16[8,48,3072]{2,1,0:T(8,128)(2,1)}, bf16[8,48,3072]{2,1,0:T(8,128)(2,1)S(1)}, u32[]{:S(2)}, u32[]{:S(2)}) %collective-permute-start.13) | collective-permute-done | bytes 2359328 | tf_op jit(solution)/shard_map/ppermute | solution.py:1262
  228.0 3.6 %add_convert_fusion.1 = bf16[4,48,3072]{2,1,0:T(8,128)(2,1)} fusion(bf16[8,48,3072]{2,1,0:T(8,128)(2,1)S(1)} %collective-permute-done.13.refs_17_, bf16[8,48,3072]{2,1,0:T(8,128)(2,1)} %get-tuple-element.274), kind=kLoop, calls=%fused_computation.3 | loop fusion | flops 2359296 | bytes 3538944 | tf_op jit(solution)/shard_map/convert_element_type | solution.py:1290
  240.4 11.7 %grads_attn0_grads_attn0.1 = (bf16[8,48,3072]{2,1,0:T(8,128)(2,1)}, bf16[8,48,3072]{2,1,0:T(8,128)(2,1)}, f32[8,3072]{1,0:T(8,128)}, f32[24,768]{1,0:T(8,128)}) custom-call(s32[1]{0:T(128)} %bitcast.refs_0_, s32[1]{0:T(128)} %bitcast.1.refs_1_, s32[6]{0:T(128)} %refs_2_.27, f32[8,768]{1,0:T(8,128)} %get-tuple-element.220.refs_3_, ...), custom_call_target="tpu_custom_call" | custom-call | flops 1 | bytes 1 | tf_op jit(solution)/shard_map/grads_attn0_grads_attn0/pallas_call | solution.py:1161
  252.2 9.8 %collective-permute-done.17 = bf16[1,192,768]{2,1,0:T(8,128)(2,1)} collective-permute-done((bf16[1,192,768]{2,1,0:T(8,128)(2,1)S(1)}, bf16[1,192,768]{2,1,0:T(8,128)(2,1)}, u32[]{:S(2)}, u32[]{:S(2)}) %collective-permute-start.17) | collective-permute-done | bytes 294944 | tf_op jit(solution)/shard_map/ppermute | solution.py:1262
  282.2 7.6 %radar_back0.1 = f32[816,768]{1,0:T(8,128)} custom-call(s32[1]{0:T(128)} %bitcast.refs_0_, s32[1]{0:T(128)} %bitcast.1.refs_1_, s32[6]{0:T(128)} %refs_2_.27, s32[6]{0:T(128)} %refs_3_.21, f32[12]{0:T(128)} %constant.34.clone.refs_4_, s32[6,136]{1,0:T(8,128)} %refs_5_.21, s32[6,136]{1,0:T(8,128)} %refs_6_.21, ...), custom_call_target="tpu_custom_call", output_to_operand_aliasing={{}: (14, {})} | custom-call | flops 1 | bytes 1 | tf_op jit(solution)/shard_map/radar_back0/pallas_call | solution.py:1161
  289.8 10.0 %collective-permute-done.21 = f32[24,768]{1,0:T(8,128)S(1)} collective-permute-done((f32[24,768]{1,0:T(8,128)S(1)}, f32[24,768]{1,0:T(8,128)S(1)}, u32[]{:S(2)}, u32[]{:S(2)}) %collective-permute-start.21) | collective-permute-done | bytes 73760 | tf_op jit(solution)/shard_map/ppermute | solution.py:1262
  314.3 4.6 %collective-permute-done.30 = f32[24,768]{1,0:T(8,128)S(1)} collective-permute-done((f32[24,768]{1,0:T(8,128)S(1)}, f32[24,768]{1,0:T(8,128)S(1)}, u32[]{:S(2)}, u32[]{:S(2)}) %collective-permute-start.30) | collective-permute-done | bytes 73760 | tf_op jit(solution)/shard_map/ppermute | solution.py:1262
  323.8 6.7 %collective-permute-done.25 = bf16[1,48,3072]{2,1,0:T(8,128)(2,1)S(1)} collective-permute-done((bf16[1,48,3072]{2,1,0:T(8,128)(2,1)}, bf16[1,48,3072]{2,1,0:T(8,128)(2,1)S(1)}, u32[]{:S(2)}, u32[]{:S(2)}) %collective-permute-start.25) | collective-permute-done | bytes 294944 | tf_op jit(solution)/shard_map/ppermute | solution.py:1262
  330.5 6.7 %collective-permute-done.27 = bf16[1,48,3072]{2,1,0:T(8,128)(2,1)} collective-permute-done((bf16[1,48,3072]{2,1,0:T(8,128)(2,1)S(1)}, bf16[1,48,3072]{2,1,0:T(8,128)(2,1)}, u32[]{:S(2)}, u32[]{:S(2)}) %collective-permute-start.27) | collective-permute-done | bytes 294944 | tf_op jit(solution)/shard_map/ppermute | solution.py:1262
  (126 shorter events, 88.7 us)
Async XLA Ops:
  1.8 22.8 %collective-permute-start.2 = (bf16[272,768]{1,0:T(8,128)(2,1)}, bf16[272,768]{1,0:T(8,128)(2,1)S(1)}, u32[]{:S(2)}, u32[]{:S(2)}) collective-permute-start(bf16[272,768]{1,0:T(8,128)(2,1)} %get-tuple-element.176), channel_id=1, source_target_pairs={{0,16},{1,17},{2,18},{3,19},{4,20},{5,21},{6,22},{7,23},{8,24},{9,... | collective-permute-start | bytes 1253384 | tf_op jit(solution)/shard_map/ppermute | solution.py:1245
  11.3 47.3 %collective-permute-start.1 = (bf16[272,768]{1,0:T(8,128)(2,1)}, bf16[272,768]{1,0:T(8,128)(2,1)S(1)}, u32[]{:S(2)}, u32[]{:S(2)}) collective-permute-start(bf16[272,768]{1,0:T(8,128)(2,1)} %get-tuple-element.175), channel_id=1, source_target_pairs={{0,16},{1,17},{2,18},{3,19},{4,20},{5,21},{6,22},{7,23},{8,24},{9,... | collective-permute-start | bytes 1253384 | tf_op jit(solution)/shard_map/ppermute | solution.py:1245
  55.0 35.3 %collective-permute-start.3 = (bf16[272,768]{1,0:T(8,128)(2,1)}, bf16[272,768]{1,0:T(8,128)(2,1)S(1)}, u32[]{:S(2)}, u32[]{:S(2)}) collective-permute-start(bf16[272,768]{1,0:T(8,128)(2,1)} %get-tuple-element.201), channel_id=1, source_target_pairs={{16,0},{17,1},{18,2},{19,3},{20,4},{21,5},{22,6},{23,7},{24,8},{25... | collective-permute-start | bytes 1253384 | tf_op jit(solution)/shard_map/ppermute | solution.py:1252
  57.3 34.9 %collective-permute-start = (bf16[272,768]{1,0:T(8,128)(2,1)S(1)}, bf16[272,768]{1,0:T(8,128)(2,1)S(1)}, u32[]{:S(2)}, u32[]{:S(2)}) collective-permute-start(bf16[272,768]{1,0:T(8,128)(2,1)S(1)} %copy-done.15), channel_id=1, source_target_pairs={{0,16},{1,17},{2,18},{3,19},{4,20},{5,21},{6,22},{7,23},{8,24},{9,... | collective-permute-start | bytes 1253384 | tf_op jit(solution)/shard_map/ppermute | solution.py:1245
  88.9 34.7 %collective-permute-start.4 = (bf16[272,768]{1,0:T(8,128)(2,1)}, bf16[272,768]{1,0:T(8,128)(2,1)S(1)}, u32[]{:S(2)}, u32[]{:S(2)}) collective-permute-start(bf16[272,768]{1,0:T(8,128)(2,1)} %get-tuple-element.221), channel_id=1, source_target_pairs={{16,0},{17,1},{18,2},{19,3},{20,4},{21,5},{22,6},{23,7},{24,8},{25... | collective-permute-start | bytes 1253384 | tf_op jit(solution)/shard_map/ppermute | solution.py:1252
  147.4 36.0 %collective-permute-start.7 = (bf16[4,48,3072]{2,1,0:T(8,128)(2,1)}, bf16[4,48,3072]{2,1,0:T(8,128)(2,1)S(1)}, u32[]{:S(2)}, u32[]{:S(2)}) collective-permute-start(bf16[4,48,3072]{2,1,0:T(8,128)(2,1)} %add_convert_fusion.2), channel_id=1, source_target_pairs={{16,18},{17,19},{18,16},{19,17},{20,22},{21,23},{22,20},{23,21},{2... | collective-permute-start | bytes 3538952 | tf_op jit(solution)/shard_map/ppermute | solution.py:1266
  189.8 33.4 %collective-permute-start.9 = (bf16[4,192,768]{2,1,0:T(8,128)(2,1)}, bf16[4,192,768]{2,1,0:T(8,128)(2,1)S(1)}, u32[]{:S(2)}, u32[]{:S(2)}) collective-permute-start(bf16[4,192,768]{2,1,0:T(8,128)(2,1)} %fusion), channel_id=1, source_target_pairs={{0,2},{1,3},{2,0},{3,1},{4,6},{5,7},{6,4},{7,5},{8,10},{9,11},{10,... | collective-permute-start | bytes 3538952 | tf_op jit(solution)/shard_map/ppermute | solution.py:1262
  194.5 16.2 %collective-permute-start.10 = (bf16[1,48,3072]{2,1,0:T(8,128)(2,1)}, bf16[1,48,3072]{2,1,0:T(8,128)(2,1)}, u32[]{:S(2)}, u32[]{:S(2)}) collective-permute-start(bf16[1,48,3072]{2,1,0:T(8,128)(2,1)} %get-tuple-element.307), channel_id=1, source_target_pairs={{16,24},{17,25},{18,26},{19,27},{20,28},{21,29},{22,30},{23,31},{2... | collective-permute-start | bytes 884744 | tf_op jit(solution)/shard_map/ppermute | solution.py:1266
  196.4 16.5 %collective-permute-start.11 = (bf16[1,48,3072]{2,1,0:T(8,128)(2,1)}, bf16[1,48,3072]{2,1,0:T(8,128)(2,1)}, u32[]{:S(2)}, u32[]{:S(2)}) collective-permute-start(bf16[1,48,3072]{2,1,0:T(8,128)(2,1)} %get-tuple-element.306), channel_id=1, source_target_pairs={{16,20},{17,21},{18,22},{19,23},{20,16},{21,17},{22,18},{23,19},{2... | collective-permute-start | bytes 884744 | tf_op jit(solution)/shard_map/ppermute | solution.py:1266
  200.3 23.0 %collective-permute-start.12 = (bf16[1,48,3072]{2,1,0:T(8,128)(2,1)S(1)}, bf16[1,48,3072]{2,1,0:T(8,128)(2,1)}, u32[]{:S(2)}, u32[]{:S(2)}) collective-permute-start(bf16[1,48,3072]{2,1,0:T(8,128)(2,1)S(1)} %get-tuple-element.305), channel_id=1, source_target_pairs={{16,28},{17,29},{18,30},{19,31},{20,24},{21,25},{22,26},{23,27},{2... | collective-permute-start | bytes 884744 | tf_op jit(solution)/shard_map/ppermute | solution.py:1266
  231.6 30.3 %collective-permute-start.14 = (bf16[4,48,3072]{2,1,0:T(8,128)(2,1)}, bf16[4,48,3072]{2,1,0:T(8,128)(2,1)}, u32[]{:S(2)}, u32[]{:S(2)}) collective-permute-start(bf16[4,48,3072]{2,1,0:T(8,128)(2,1)} %add_convert_fusion.1), channel_id=1, source_target_pairs={{0,2},{1,3},{2,0},{3,1},{4,6},{5,7},{6,4},{7,5},{8,10},{9,11},{10,... | collective-permute-start | bytes 3538952 | tf_op jit(solution)/shard_map/ppermute | solution.py:1262
  235.6 16.6 %collective-permute-start.15 = (bf16[1,192,768]{2,1,0:T(8,128)(2,1)}, bf16[1,192,768]{2,1,0:T(8,128)(2,1)}, u32[]{:S(2)}, u32[]{:S(2)}) collective-permute-start(bf16[1,192,768]{2,1,0:T(8,128)(2,1)} %get-tuple-element.304), channel_id=1, source_target_pairs={{0,8},{1,9},{2,10},{3,11},{4,12},{5,13},{6,14},{7,15},{8,0},{9,1},... | collective-permute-start | bytes 884744 | tf_op jit(solution)/shard_map/ppermute | solution.py:1262
  235.6 16.6 %collective-permute-start.16 = (bf16[1,192,768]{2,1,0:T(8,128)(2,1)}, bf16[1,192,768]{2,1,0:T(8,128)(2,1)}, u32[]{:S(2)}, u32[]{:S(2)}) collective-permute-start(bf16[1,192,768]{2,1,0:T(8,128)(2,1)} %get-tuple-element.303), channel_id=1, source_target_pairs={{0,4},{1,5},{2,6},{3,7},{4,0},{5,1},{6,2},{7,3},{8,12},{9,13},{10,... | collective-permute-start | bytes 884744 | tf_op jit(solution)/shard_map/ppermute | solution.py:1262
  237.1 24.8 %collective-permute-start.17 = (bf16[1,192,768]{2,1,0:T(8,128)(2,1)S(1)}, bf16[1,192,768]{2,1,0:T(8,128)(2,1)}, u32[]{:S(2)}, u32[]{:S(2)}) collective-permute-start(bf16[1,192,768]{2,1,0:T(8,128)(2,1)S(1)} %get-tuple-element.302), channel_id=1, source_target_pairs={{0,12},{1,13},{2,14},{3,15},{4,8},{5,9},{6,10},{7,11},{8,4},{9,5},... | collective-permute-start | bytes 884744 | tf_op jit(solution)/shard_map/ppermute | solution.py:1262
  263.6 14.4 %collective-permute-start.31 = (bf16[48,3072]{1,0:T(8,128)(2,1)S(1)}, bf16[48,3072]{1,0:T(8,128)(2,1)S(1)}, u32[]{:S(2)}, u32[]{:S(2)}) collective-permute-start(bf16[48,3072]{1,0:T(8,128)(2,1)S(1)} %fusion.1), channel_id=1, source_target_pairs={{16,0},{17,1},{18,2},{19,3},{20,4},{21,5},{22,6},{23,7},{24,8},{25... | collective-permute-start | bytes 884744 | tf_op jit(solution)/shard_map/ppermute | solution.py:1367
  269.9 31.5 %collective-permute-start.19 = (bf16[4,48,3072]{2,1,0:T(8,128)(2,1)}, bf16[4,48,3072]{2,1,0:T(8,128)(2,1)}, u32[]{:S(2)}, u32[]{:S(2)}) collective-permute-start(bf16[4,48,3072]{2,1,0:T(8,128)(2,1)} %add_convert_fusion), channel_id=1, source_target_pairs={{0,2},{1,3},{2,0},{3,1},{4,6},{5,7},{6,4},{7,5},{8,10},{9,11},{10,... | collective-permute-start | bytes 3538952 | tf_op jit(solution)/shard_map/ppermute | solution.py:1262
  274.5 25.2 %collective-permute-start.22 = (bf16[1,48,3072]{2,1,0:T(8,128)(2,1)}, bf16[1,48,3072]{2,1,0:T(8,128)(2,1)S(1)}, u32[]{:S(2)}, u32[]{:S(2)}) collective-permute-start(bf16[1,48,3072]{2,1,0:T(8,128)(2,1)} %get-tuple-element.301), channel_id=1, source_target_pairs={{0,8},{1,9},{2,10},{3,11},{4,12},{5,13},{6,14},{7,15},{8,0},{9,1},... | collective-permute-start | bytes 884744 | tf_op jit(solution)/shard_map/ppermute | solution.py:1262
  274.5 25.2 %collective-permute-start.23 = (bf16[1,48,3072]{2,1,0:T(8,128)(2,1)}, bf16[1,48,3072]{2,1,0:T(8,128)(2,1)}, u32[]{:S(2)}, u32[]{:S(2)}) collective-permute-start(bf16[1,48,3072]{2,1,0:T(8,128)(2,1)} %get-tuple-element.300), channel_id=1, source_target_pairs={{0,4},{1,5},{2,6},{3,7},{4,0},{5,1},{6,2},{7,3},{8,12},{9,13},{10,... | collective-permute-start | bytes 884744 | tf_op jit(solution)/shard_map/ppermute | solution.py:1262
  276.4 24.9 %collective-permute-start.24 = (bf16[1,48,3072]{2,1,0:T(8,128)(2,1)}, bf16[1,48,3072]{2,1,0:T(8,128)(2,1)}, u32[]{:S(2)}, u32[]{:S(2)}) collective-permute-start(bf16[1,48,3072]{2,1,0:T(8,128)(2,1)} %get-tuple-element.299), channel_id=1, source_target_pairs={{0,12},{1,13},{2,14},{3,15},{4,8},{5,9},{6,10},{7,11},{8,4},{9,5},... | collective-permute-start | bytes 884744 | tf_op jit(solution)/shard_map/ppermute | solution.py:1262
  279.5 20.2 %collective-permute-start.21 = (f32[24,768]{1,0:T(8,128)S(1)}, f32[24,768]{1,0:T(8,128)S(1)}, u32[]{:S(2)}, u32[]{:S(2)}) collective-permute-start(f32[24,768]{1,0:T(8,128)S(1)} %add.191.refs_13_), channel_id=1, source_target_pairs={{0,2},{1,3},{2,0},{3,1},{4,6},{5,7},{6,4},{7,5},{8,10},{9,11},{10,... | collective-permute-start | bytes 221192 | tf_op jit(solution)/shard_map/ppermute | solution.py:1262
  305.3 13.7 %collective-permute-start.30 = (f32[24,768]{1,0:T(8,128)S(1)}, f32[24,768]{1,0:T(8,128)S(1)}, u32[]{:S(2)}, u32[]{:S(2)}) collective-permute-start(f32[24,768]{1,0:T(8,128)S(1)} %add.219), channel_id=1, source_target_pairs={{0,12},{1,13},{2,14},{3,15},{4,8},{5,9},{6,10},{7,11},{8,4},{9,5},... | collective-permute-start | bytes 221192 | tf_op jit(solution)/shard_map/ppermute | solution.py:1262
  308.5 22.0 %collective-permute-start.25 = (bf16[1,48,3072]{2,1,0:T(8,128)(2,1)}, bf16[1,48,3072]{2,1,0:T(8,128)(2,1)S(1)}, u32[]{:S(2)}, u32[]{:S(2)}) collective-permute-start(bf16[1,48,3072]{2,1,0:T(8,128)(2,1)} %get-tuple-element.296), channel_id=1, source_target_pairs={{0,8},{1,9},{2,10},{3,11},{4,12},{5,13},{6,14},{7,15},{8,0},{9,1},... | collective-permute-start | bytes 884744 | tf_op jit(solution)/shard_map/ppermute | solution.py:1262
  310.4 20.1 %collective-permute-start.26 = (bf16[1,48,3072]{2,1,0:T(8,128)(2,1)}, bf16[1,48,3072]{2,1,0:T(8,128)(2,1)S(1)}, u32[]{:S(2)}, u32[]{:S(2)}) collective-permute-start(bf16[1,48,3072]{2,1,0:T(8,128)(2,1)} %get-tuple-element.298), channel_id=1, source_target_pairs={{0,4},{1,5},{2,6},{3,7},{4,0},{5,1},{6,2},{7,3},{8,12},{9,13},{10,... | collective-permute-start | bytes 884744 | tf_op jit(solution)/shard_map/ppermute | solution.py:1262
  313.8 23.4 %collective-permute-start.27 = (bf16[1,48,3072]{2,1,0:T(8,128)(2,1)S(1)}, bf16[1,48,3072]{2,1,0:T(8,128)(2,1)}, u32[]{:S(2)}, u32[]{:S(2)}) collective-permute-start(bf16[1,48,3072]{2,1,0:T(8,128)(2,1)S(1)} %get-tuple-element.297), channel_id=1, source_target_pairs={{0,12},{1,13},{2,14},{3,15},{4,8},{5,9},{6,10},{7,11},{8,4},{9,5},... | collective-permute-start | bytes 884744 | tf_op jit(solution)/shard_map/ppermute | solution.py:1262
  (25 other events, 217.0 us)
